TPU v7x, 32 devices: a whole 2x2x4 slice. The times are simulated.
32 devices in a mesh: groups: 2 (over x), dp: 2 (over core), ctx: 8 (over z, y).
Axes of the slice: x: 2, y: 2, z: 4, core: 2. Of those that a mesh axis runs over, the one named last changes fastest.
Arguments:
- queries: bfloat16 [4, 1024, 4096], P(('groups', 'dp'), 'ctx'), parts along dimension 0, may hold values from -16 to 16
- key_matrix: bfloat16 [4, 1024, 512], P(('groups', 'dp'), 'ctx'), parts along dimension 0, may hold values from -16 to 16
- value_matrix: bfloat16 [4, 1024, 512], P(('groups', 'dp'), 'ctx'), parts along dimension 0, may hold values from -6 to 6
- cotangent: bfloat16 [4, 1024, 4096], P(('groups', 'dp'), 'ctx'), parts along dimension 0, may hold values from -6 to 6
- segment: int32 [4, 1024], P(('groups', 'dp'), 'ctx'), parts along dimension 0, may hold values from 0 to 3, never falling along the last dimension, each value on 1 to 512 neighbouring positions
Outputs:
- attended: bfloat16 [4, 1024, 4096], P(('groups', 'dp'), 'ctx'), parts along dimension 0
- grad_query: float32 [4, 1024, 4096], P(('groups', 'dp'), 'ctx'), parts along dimension 0
- key_gradient_rows: float32 [4, 1024, 512], P(('groups', 'dp'), 'ctx'), parts along dimension 0
- value_gradient_rows: float32 [4, 1024, 512], P(('groups', 'dp'), 'ctx'), parts along dimension 0
There are 2 independent parts, one for each index of `groups`. A program takes and returns all parts, laid end to end along the dimension named above; each array names one. Nothing has to cross between parts.
All inputs are finite; a program needn't handle non-finite values.
Results may differ from a plain program's by a relative error of at most 0.04.
Values may be sent and summed in bfloat16 or wider, within the bound.
No kernel may reach another device: no remote copies, remote signals or barrier semaphores. Data moves between devices by JAX's collectives and lax.ppermute only.
A program may use at most 128 MiB of HBM per device.

v0:
```python
import math

import jax
import jax.numpy as jnp
from jax import lax
from jax.sharding import PartitionSpec as P

QUERY_HEADS = 32
KEY_VALUE_HEADS = 4
HEAD_WIDTH = 128


def per_device(queries, key_matrix, value_matrix, cotangent, segment):
    ctx_size = lax.axis_size("ctx")
    row_count = queries.shape[1]
    query_group = QUERY_HEADS // KEY_VALUE_HEADS
    scale = 1.0 / math.sqrt(HEAD_WIDTH)
    here = lax.axis_index("ctx")
    complete_keys, complete_values, whole_segment = (
        lax.all_gather(key_matrix, "ctx", axis=1, tiled=True),
        lax.all_gather(value_matrix, "ctx", axis=1, tiled=True),
        lax.all_gather(segment, "ctx", axis=1, tiled=True),
    )
    complete_keys = complete_keys[0]
    complete_values = complete_values[0]
    whole_segment = whole_segment[0]
    stream_index = complete_keys.shape[0]
    query_head_rows = queries[0].reshape(row_count, KEY_VALUE_HEADS, query_group, HEAD_WIDTH)
    gradient_heads = cotangent[0].reshape(row_count, KEY_VALUE_HEADS, query_group, HEAD_WIDTH)
    q_places = here * row_count + jnp.arange(row_count, dtype=jnp.int32)
    q_segment = segment[0]
    per_block = max(1, min(ctx_size, 512 // row_count))
    block_index = per_block * row_count
    blocks = ctx_size // per_block

    def fetch(index):
        block_start = index * block_index
        key_block = lax.dynamic_slice_in_dim(complete_keys, block_start, block_index, 0).reshape(
            block_index, KEY_VALUE_HEADS, HEAD_WIDTH
        )
        value_block = lax.dynamic_slice_in_dim(
            complete_values, block_start, block_index, 0
        ).reshape(block_index, KEY_VALUE_HEADS, HEAD_WIDTH)
        s_block = lax.dynamic_slice_in_dim(whole_segment, block_start, block_index, 0)
        k_places = block_start + jnp.arange(block_index, dtype=jnp.int32)
        allowed = (k_places[None, :] <= q_places[:, None]) & (
            (s_block[None, :] == q_segment[:, None]) | (s_block[None, :] == 0)
        )
        return (key_block, value_block, allowed)

    def logits_of(key_block, allowed):
        raw = (
            jnp.einsum(
                "tkgd,skd->kgts", query_head_rows, key_block, preferred_element_type=jnp.float32
            )
            * scale
        )
        return jnp.where(allowed[None, None], raw, jnp.float32(-1e30))

    def forward_step(index, carry):
        key_block, value_block, allowed = fetch(index)

        def update(state):
            run_max, run_sum, accum = state
            logits = logits_of(key_block, allowed)
            new_max = jnp.maximum(run_max, jnp.max(logits, axis=-1))
            factor = jnp.exp(run_max - new_max)
            weights = jnp.where(
                allowed[None, None], jnp.exp(logits - new_max[..., None]), jnp.float32(0.0)
            )
            run_sum = run_sum * factor + jnp.sum(weights, axis=-1)
            weights_b = weights.astype(jnp.bfloat16)
            accum = accum * factor[..., None] + jnp.einsum(
                "kgts,skd->kgtd", weights_b, value_block, preferred_element_type=jnp.float32
            )
            return (new_max, run_sum, accum)

        def unchanged(state):
            return state

        return lax.cond(jnp.any(allowed), update, unchanged, carry)

    start_state = (
        jnp.full((KEY_VALUE_HEADS, query_group, row_count), -1e30, jnp.float32),
        jnp.zeros((KEY_VALUE_HEADS, query_group, row_count), jnp.float32),
        jnp.zeros((KEY_VALUE_HEADS, query_group, row_count, HEAD_WIDTH), jnp.float32),
    )
    run_max, run_sum, accum = lax.fori_loop(0, blocks, forward_step, start_state)
    out_heads = (accum / run_sum[..., None]).astype(jnp.bfloat16).transpose(2, 0, 1, 3)
    attended = out_heads.reshape(1, row_count, QUERY_HEADS * HEAD_WIDTH)
    log_sum = run_max + jnp.log(run_sum)
    delta = jnp.sum(
        gradient_heads.astype(jnp.float32) * out_heads.astype(jnp.float32), axis=-1
    ).transpose(1, 2, 0)

    def backward_step(grad_acc, index):
        key_block, value_block, allowed = fetch(index)

        def work(grad_acc):
            logits = logits_of(key_block, allowed)
            probs = jnp.where(
                allowed[None, None], jnp.exp(logits - log_sum[..., None]), jnp.float32(0.0)
            )
            probs_b = probs.astype(jnp.bfloat16)
            value_piece = jnp.einsum(
                "kgts,tkgd->skd", probs_b, gradient_heads, preferred_element_type=jnp.float32
            )
            along = jnp.einsum(
                "tkgd,skd->kgts", gradient_heads, value_block, preferred_element_type=jnp.float32
            )
            slopes = (probs * (along - delta[..., None])).astype(jnp.bfloat16)
            grad_acc = grad_acc + jnp.einsum(
                "kgts,skd->kgtd", slopes, key_block, preferred_element_type=jnp.float32
            )
            key_piece = (
                jnp.einsum(
                    "kgts,tkgd->skd", slopes, query_head_rows, preferred_element_type=jnp.float32
                )
                * scale
            )
            return (
                grad_acc,
                (
                    key_piece.reshape(block_index, KEY_VALUE_HEADS * HEAD_WIDTH),
                    value_piece.reshape(block_index, KEY_VALUE_HEADS * HEAD_WIDTH),
                ),
            )

        def skipped(grad_acc):
            blank_state = jnp.zeros((block_index, KEY_VALUE_HEADS * HEAD_WIDTH), jnp.float32)
            return (grad_acc, (blank_state, blank_state))

        return lax.cond(jnp.any(allowed), work, skipped, grad_acc)

    grad_acc, (key_pieces, value_pieces) = lax.scan(
        backward_step,
        jnp.zeros((KEY_VALUE_HEADS, query_group, row_count, HEAD_WIDTH), jnp.float32),
        jnp.arange(blocks, dtype=jnp.int32),
    )
    key_pieces = key_pieces.reshape(stream_index, KEY_VALUE_HEADS * HEAD_WIDTH)
    value_pieces = value_pieces.reshape(stream_index, KEY_VALUE_HEADS * HEAD_WIDTH)
    grad_query = (
        (scale * grad_acc).transpose(2, 0, 1, 3).reshape(1, row_count, QUERY_HEADS * HEAD_WIDTH)
    )
    key_gradient_rows, value_gradient_rows = (
        lax.psum_scatter(
            key_pieces.astype(jnp.bfloat16), "ctx", scatter_dimension=0, tiled=True
        ).astype(jnp.float32),
        lax.psum_scatter(
            value_pieces.astype(jnp.bfloat16), "ctx", scatter_dimension=0, tiled=True
        ).astype(jnp.float32),
    )
    return (
        attended,
        grad_query,
        key_gradient_rows.reshape(1, row_count, KEY_VALUE_HEADS * HEAD_WIDTH),
        value_gradient_rows.reshape(1, row_count, KEY_VALUE_HEADS * HEAD_WIDTH),
    )


def solution(mesh):
    in_specs = (
        P(("groups", "dp"), "ctx", None),
        P(("groups", "dp"), "ctx", None),
        P(("groups", "dp"), "ctx", None),
        P(("groups", "dp"), "ctx", None),
        P(("groups", "dp"), "ctx"),
    )
    out_specs = (
        P(("groups", "dp"), "ctx", None),
        P(("groups", "dp"), "ctx", None),
        P(("groups", "dp"), "ctx", None),
        P(("groups", "dp"), "ctx", None),
    )
    return jax.shard_map(
        per_device, mesh=mesh, in_specs=in_specs, out_specs=out_specs, check_vma=False
    )
```

profile of v0, /device:TPU:0, one launch (start us, length us, event | category | flops | bytes accessed | tf_op | source)
XLA Modules:
  0.0 295.9 jit_solution(9166675928046072248)
XLA Ops:
  7.2 1.7 copy.34
  9.0 1.7 copy.36
  10.7 1.6 copy.35
  12.3 0.7 copy.37
  13.0 2.3 copy.40
  15.3 22.4 %all_gather.9 = s32[1,1024]{1,0:T(1,128)S(1)} all-gather(s32[1,128]{1,0:T(1,128)} %param.17), channel_id=1, replica_groups=mesh['groups'=2,'dp'=2,'ctx'=8] {'ctx'}, dimensions={1}, use_global_device_ids=true | all-gather | bytes 4608 | tf_op jit(solution)/shard_map/all_gather | solution.py:22
  37.7 15.2 %all-gather.3.cloned.1.call-done = bf16[1,1024,512]{1,2,0:T(8,128)(2,1)} async-done(((bf16[1,128,512]{1,2,0:T(8,128)(2,1)}), bf16[1,1024,512]{1,2,0:T(8,128)(2,1)}) %all-gather.3.cloned.1.call-update) | async-done | bytes 1048592 | tf_op jit(solution)/shard_map/all_gather | solution.py:20
  52.9 41.1 %all-gather.5.cloned.1.call-done = bf16[1,1024,512]{1,2,0:T(8,128)(2,1)} async-done(((bf16[1,128,512]{1,2,0:T(8,128)(2,1)}), bf16[1,1024,512]{1,2,0:T(8,128)(2,1)}) %all-gather.5.cloned.1.call-update) | async-done | bytes 1048592 | tf_op jit(solution)/shard_map/all_gather | solution.py:21
  94.0 1.6 broadcast.65.clone
  95.5 13.6 %while.36 = (s32[]{:T(128)}, f32[4,8,128]{2,1,0:T(8,128)S(1)}, f32[4,8,128]{2,1,0:T(8,128)S(1)}, f32[4,8,128,128]{3,2,1,0:T(8,128)}, s32[1024]{0:T(1024)S(1)}, /...) while((s32[]{:T(128)}, f32[4,8,128]{2,1,0:T(8,128)S(1)}, ...), condition=%wide.region_6.7_spmd.clone, body=%wide.region_0.6_spmd.clone.sunk | while | flops 1102390400 | bytes 34091840 | solution.py:88
  95.6 0.1 broadcast_compare_fusion.4
  95.6 0.9 fusion.45
  97.2 10.2 %conditional.6 = ((f32[4,8,128]{2,1,0:T(8,128)S(1)}, f32[4,8,128]{2,1,0:T(8,128)S(1)}, f32[4,8,128,128]{3,2,1,0:T(8,128)})) conditional(s32[]{:T(128)} %convert_element_type.70, (f32[4,8,128]{2,1,0:T(8,128)S(1)}, f32[4,8,128]{2,1,0:T(8,128)S(1)}, f32[4,8,128,128]{3,2,1,0:T(8,128)}) %tuple.102, (pred[128,512]{0,1:T(8,128)(4,1)S(1)}, ...), branch_computations={%region_2.0_spmd, %region_3.5_spmd} | conditional | flops 1102061568 | bytes 34013220 | solution.py:81
  97.2 1.3 constant_dynamic-slice_fusion
  98.5 1.5 fusion.4
  100.0 2.2 fusion.6
  102.2 5.3 %multiply_add_fusion = f32[4,8,128,128]{3,2,1,0:T(8,128)} fusion(f32[4,8,128,128]{3,2,1,0:T(8,128)} %get-tuple-element.358, bf16[512,4,128,1]{0,2,3,1:T(8,128)(2,1)S(1)} %bitcast.119, f32[4,512,128,8]{2,1,3,0:T(8,128)S(1)} %get-tuple-element.560, f32[4,8,128]{2,1,0:T(8,128)S(1)} %max.4, pred[128,512]{0,1:T(8,128)(4,1)S(1)} %get-tuple-element.353, ...), kind=kOutput, calls=%fused_computation.9 | convolution fusion | flops 548405248 | bytes 13205504 | tf_op jit(solution)/shard_map/while/body/eval_jaxpr/cond/branch_1_fun/kgts,skd->kgtd/dot_general | solution.py:73
  107.4 0.1 broadcast_compare_fusion.4
  107.5 0.9 fusion.45
  109.1 1.9 copy.38
  111.1 2.7 multiply_reduce_fusion
  113.8 0.2 broadcast.65
  114.0 20.6 %while.37 = (s32[]{:T(128)}, f32[4,8,128,128]{3,2,1,0:T(8,128)S(1)}, bf16[2,512,512]{1,2,0:T(8,128)(2,1)}, bf16[2,512,512]{1,2,0:T(8,128)(2,1)}, s32[2]{0:T(128)...) while((s32[]{:T(128)}, ...), condition=%wide.region_12.13_spmd.clone, body=%wide.region_8.12_spmd.clone.sunk | while | flops 2710897920 | bytes 57406332 | solution.py:135
  114.2 0.6 dynamic_slice.68
  115.5 0.1 broadcast_compare_fusion.5
  115.6 0.9 fusion.46
  117.1 12.3 %conditional.7 = (f32[4,8,128,128]{3,2,1,0:T(8,128)S(1)}, bf16[1,512,512]{1,2,0:T(8,128)(2,1)S(1)}, bf16[1,512,512]{1,2,0:T(8,128)(2,1)S(1)}) conditional(s32[]{:T(128)} %convert_element_type.71, f32[4,8,128,128]{3,2,1,0:T(8,128)S(1)} %get-tuple-element.816, (pred[128,512]{0,1:T(8,128)(4,1)S(1)}, bf16[1024,512]{0,1:T(8,128)(2,1)}, s32[]{:T(128)}, ...), branch_computations={%region_10.10_spmd, %region_11.11_spmd} | conditional | flops 2710568960 | bytes 55230520 | solution.py:133
  117.1 1.8 constant_dynamic-slice_fusion.2
  119.0 1.3 fusion.30
  120.3 2.2 fusion.21
  122.5 3.1 %fusion.16 = bf16[4,8,128,512]{2,3,1,0:T(8,128)(2,1)S(1)} fusion(f32[4,512,128,8]{2,1,3,0:T(8,128)S(1)} %fusion.30, f32[4,8,128]{2,1,0:T(8,128)S(1)} %get-tuple-element.382, f32[4,8,128]{2,1,0:T(8,128)S(1)} %get-tuple-element.379, pred[128,512]{0,1:T(8,128)(4,1)S(1)} %get-tuple-element.375, bf16[512,4,128,1]{0,2,3,1:T(8,128)(2,1)S(1)} %bitcast.120, ...), kind=kOutput, calls=%fused_computation.19 | convolution fusion | flops 551550976 | bytes 14254080 | tf_op jit(solution)/shard_map/while/body/eval_jaxpr/cond/branch_1_fun/tkgd,skd->kgts/dot_general | solution.py:108
  125.6 1.5 fusion.24
  127.1 2.4 convolution_add_fusion
  129.5 1.1 constant_dynamic-update-slice_fusion.3
  130.5 0.6 dynamic_slice.68
  131.9 0.9 fusion.46
  133.4 0.1 conditional.7
  133.6 1.0 constant_dynamic-update-slice_fusion.3
  134.6 2.3 copy.43
  136.9 2.3 copy.42
  139.2 2.3 copy.67
  141.5 0.2 multiply_bitcast_fusion
  141.7 1.2 copy.41
  142.9 1.5 reshape.98
  144.5 77.1 %reduce-scatter.5.cloned.1.call-done = bf16[128,512]{1,0:T(8,128)(2,1)} async-done(((bf16[1024,512]{1,0:T(8,128)(2,1)}), bf16[128,512]{1,0:T(8,128)(2,1)}) %reduce-scatter.5.cloned.1.call-update) | async-done | bytes 131088 | tf_op jit(solution)/shard_map/reduce_scatter | solution.py:149
  221.6 1.6 bitcast_convert_fusion
  223.2 64.6 %reduce-scatter.3.cloned.1.call-done = bf16[128,512]{1,0:T(8,128)(2,1)} async-done(((bf16[1024,512]{1,0:T(8,128)(2,1)}), bf16[128,512]{1,0:T(8,128)(2,1)}) %reduce-scatter.3.cloned.1.call-update) | async-done | bytes 131088 | tf_op jit(solution)/shard_map/reduce_scatter | solution.py:146
  287.8 1.6 bitcast_convert_fusion.1
  (33 shorter events, 0.5 us)
Async XLA Ops:
  7.2 88.4 %copy-start.1 = (s32[1,128]{1,0:T(1,128)S(1)}, s32[1,128]{1,0:T(1,128)}, u32[]{:S(2)}) copy-start(s32[1,128]{1,0:T(1,128)} %param.17) | copy-start | bytes 1540
  7.2 45.7 %all-gather.3.cloned.1.call-start = ((), (), s32[]{:S(2)}) async-start(), calls=%async_computation.2 | async-start | bytes 1179648 | tf_op jit(solution)/shard_map/all_gather | solution.py:20
  8.9 85.1 %all-gather.5.cloned.1.call-start = ((), (), s32[]{:S(2)}) async-start(), calls=%async_computation.3 | async-start | bytes 1179648 | tf_op jit(solution)/shard_map/all_gather | solution.py:21
  10.7 210.9 %reduce-scatter.5.cloned.1.call-start = ((), (), s32[]{:S(2)}) async-start(), calls=%async_computation.5 | async-start | bytes 1179648 | tf_op jit(solution)/shard_map/reduce_scatter | solution.py:149
  117.1 3.2 %copy-start = (bf16[128,4,8,128]{0,3,2,1:T(8,128)(2,1)S(1)}, bf16[128,4,8,128]{0,3,2,1:T(8,128)(2,1)}, u32[]{:S(2)}) copy-start(bf16[128,4,8,128]{0,3,2,1:T(8,128)(2,1)} %get-tuple-element.381) | copy-start | bytes 3145732 | tf_op jit(solution)/shard_map/while/body/eval_jaxpr/cond
  136.9 150.9 %reduce-scatter.3.cloned.1.call-start = ((), (), s32[]{:S(2)}) async-start(), calls=%async_computation.4 | async-start | bytes 1179648 | tf_op jit(solution)/shard_map/reduce_scatter | solution.py:146
Sparse Core Ops, SparseCore 0:
  10.6 42.2 all-gather.2
  55.5 38.4 all-gather.4
  137.0 84.5 reduce-scatter.4
  225.2 62.5 reduce-scatter.2
where the time goes:
time: 296 us
  waiting for transfers between devices  198 us (67%)
  local copies, waits for them, and re-layouts  27.6 us (9%)
  blocking collectives  22.4 us (8%)
  matrix products  17.1 us (6%)
  between operations  13.9 us (5%)
  other arithmetic  12.4 us (4%)
  loops' own time  4.36 us (1%)
    reduce_scatter x1, waiting for transfers between devices, per_device(): lax.psum_scatter(value_pieces.astype(jnp.bfloat16), 'ctx', scatter_dimens...  77.1 us
    reduce_scatter x1, waiting for transfers between devices, per_device(): lax.psum_scatter(key_pieces.astype(jnp.bfloat16), 'ctx', scatter_dimensio...  64.6 us
    all_gather x1, waiting for transfers between devices, per_device(): lax.all_gather(value_matrix, 'ctx', axis=1, tiled=True)  41.1 us
    all_gather x1, blocking collectives, per_device(): lax.all_gather(segment, 'ctx', axis=1, tiled=True)  22.4 us
    all_gather x1, waiting for transfers between devices, per_device(): lax.all_gather(key_matrix, 'ctx', axis=1, tiled=True)  15.2 us
    unnamed x7, local copies, waits for them, and re-layouts  7.88 us
  transfers between devices with their start and end apart: 4, of which 4 were waited for; matrix products, arithmetic and copies ran while one was open for 5% of the time, Pallas kernels for 0%

commit v1 on v0

v1 whole, which is shorter than its diff:
```python
import functools
import math

import jax
import jax.numpy as jnp
from jax import lax
from jax.experimental import pallas as pl
from jax.experimental.pallas import tpu as pltpu
from jax.sharding import PartitionSpec as P

KV = 4
D = 128
CHUNKS = 1
NEG = -1e30
NN = (((1,), (0,)), ((), ()))
NT = (((1,), (1,)), ((), ()))
TN = (((0,), (0,)), ((), ()))


def dot(a, b, dims):
    return lax.dot_general(a, b, dims, preferred_element_type=jnp.float32)


def pack_kernel(k_ref, v_ref, s_ref, *outs):
    rows = k_ref.shape[1]
    per = KV // len(outs)
    seg = jnp.broadcast_to(s_ref[...].astype(jnp.float32), (16, rows)).astype(jnp.bfloat16)
    for c, out in enumerate(outs):
        for g in range(per):
            cols = slice((c * per + g) * D, (c * per + g + 1) * D)
            out[2 * g * rows : (2 * g + 1) * rows, :] = k_ref[0, :, cols]
            out[(2 * g + 1) * rows : (2 * g + 2) * rows, :] = v_ref[0, :, cols]
        out[2 * per * rows :, :] = seg


def attend_kernel(pairs, per, has_prev, here_ref, *refs):
    own = refs[:pairs]
    peer = refs[pairs : 2 * pairs]
    q_ref, c_ref, sq_ref = refs[2 * pairs : 2 * pairs + 3]
    refs = refs[2 * pairs + 3 + (2 if has_prev else 0) :]
    out_ref, gq_ref, mine_ref, theirs_ref = refs[:4]
    kv, mask, e_scr, cnt, order = refs[4:]
    rows = q_ref.shape[1]
    heads = q_ref.shape[2] // D
    wide = heads * rows
    scale = 1.0 / math.sqrt(D)
    power = scale * math.log2(math.e)
    g = pl.program_id(0)
    here = here_ref[0]

    @pl.when(g == 0)
    def _():
        seg_q = sq_ref[...].astype(jnp.float32)
        q_pos = here * rows + lax.broadcasted_iota(jnp.int32, (rows, rows), 1)
        local = lax.broadcasted_iota(jnp.int32, (rows, rows), 0)
        cnt[0] = 0
        for k in range(pairs):
            live = jnp.float32(0.0)
            for lane, src in enumerate((own[k], peer[k])):
                block = (here ^ lane) - 2 * k
                seg_row = src[2 * per * rows : 2 * per * rows + 16, :].astype(jnp.float32)
                seg_k = jnp.transpose(jnp.broadcast_to(seg_row[:1], (rows, rows)))
                ok = (block * rows + local <= q_pos) & ((seg_k == seg_q) | (seg_k == 0.0)) & (block >= 0)
                add = jnp.where(ok, 0.0, NEG)
                mask[k, lane * rows : (lane + 1) * rows, :] = add
                live = jnp.maximum(live, jnp.max(jnp.where(ok, 1.0, 0.0)))
                for h in range(per):
                    for part in range(2):
                        kv[k, h, part, lane * rows : (lane + 1) * rows, :] = src[
                            (2 * h + part) * rows : (2 * h + part + 1) * rows, :
                        ]

            @pl.when(live > 0.0)
            def _():
                order[cnt[0]] = k
                cnt[0] = cnt[0] + 1

    zero = jnp.zeros((2 * rows, D), jnp.float32)
    at = pl.multiple_of(g * 2 * rows, 2 * rows)
    for k in range(pairs):
        mine_ref[k, pl.ds(at, 2 * rows), :] = zero
        theirs_ref[k, pl.ds(at, 2 * rows), :] = zero.astype(jnp.bfloat16)

    def stack(ref):
        return jnp.concatenate([ref[0, :, h * D : (h + 1) * D] for h in range(heads)], axis=0)

    q_all = stack(q_ref)
    c_all = stack(c_ref)
    live_pairs = cnt[0]

    def scores(t, top):
        k = order[t]
        s = dot(kv[k, g, 0], q_all, NT)
        s = s + jnp.concatenate([mask[k]] * heads, axis=1)
        e_scr[k] = s
        return jnp.maximum(top, jnp.max(s, axis=0, keepdims=True))

    top = lax.fori_loop(0, live_pairs, scores, jnp.full((1, wide), NEG, jnp.float32))

    def forward(t, carry):
        total, acc = carry
        k = order[t]
        e = jnp.exp2((e_scr[k] - top) * power)
        e_scr[k] = e
        total = total + jnp.sum(e, axis=0, keepdims=True)
        return total, acc + dot(kv[k, g, 1], e.astype(jnp.bfloat16), TN)

    total, acc = lax.fori_loop(
        0, live_pairs, forward, (jnp.zeros((1, wide), jnp.float32), jnp.zeros((D, wide), jnp.float32))
    )
    inverse = 1.0 / total
    acc = acc * inverse
    deltas = []
    for h in range(heads):
        o = acc[:, h * rows : (h + 1) * rows]
        out_ref[0, :, h * D : (h + 1) * D] = jnp.transpose(o).astype(jnp.bfloat16)
        c_t = jnp.transpose(c_ref[0, :, h * D : (h + 1) * D].astype(jnp.float32))
        deltas.append(jnp.sum(c_t * o.astype(jnp.bfloat16).astype(jnp.float32), axis=0, keepdims=True))
    delta = jnp.concatenate(deltas, axis=1)

    def backward(t, acc):
        k = order[t]
        probs = e_scr[k] * inverse
        along = dot(kv[k, g, 1], c_all, NT)
        slopes = (probs * (along - delta)).astype(jnp.bfloat16)
        grad_v = dot(probs.astype(jnp.bfloat16), c_all, NN)
        grad_k = dot(slopes, q_all, NN) * scale
        mine_ref[k, pl.ds(at, rows), :] = grad_k[:rows]
        mine_ref[k, pl.ds(at + rows, rows), :] = grad_v[:rows]
        theirs_ref[k, pl.ds(at, rows), :] = grad_k[rows:].astype(jnp.bfloat16)
        theirs_ref[k, pl.ds(at + rows, rows), :] = grad_v[rows:].astype(jnp.bfloat16)
        return acc + dot(kv[k, g, 0], slopes, TN)

    grad = lax.fori_loop(0, live_pairs, backward, jnp.zeros((D, wide), jnp.float32)) * scale
    for h in range(heads):
        gq_ref[0, :, h * D : (h + 1) * D] = jnp.transpose(grad[:, h * rows : (h + 1) * rows])


def attend(chunk, here, own, peer, queries, cotangent, segment, prev):
    pairs = len(own)
    per = KV // CHUNKS
    _, rows, width = queries.shape
    block = width // KV
    wide = block // D * rows
    tall = own[0].shape
    whole = pl.BlockSpec(tall, lambda g: (0, 0))
    columns = pl.BlockSpec((1, rows, block), lambda g: (0, 0, chunk * per + g))
    parts = pl.BlockSpec((pairs, per * 2 * rows, D), lambda g: (0, 0, 0))
    args = [here, *own, *peer, queries, cotangent, segment]
    in_specs = [pl.BlockSpec(memory_space=pltpu.SMEM)] + [whole] * (2 * pairs)
    in_specs += [columns, columns, pl.BlockSpec(segment.shape, lambda g: (0, 0))]
    aliases = {}
    if prev is not None:
        aliases = {len(args): 0, len(args) + 1: 1}
        args += list(prev)
        in_specs += [pl.BlockSpec(memory_space=pl.ANY)] * 2
    macs = per * wide * 2 * rows * D * 6 * pairs
    return pl.pallas_call(
        functools.partial(attend_kernel, pairs, per, prev is not None),
        grid=(per,),
        in_specs=in_specs,
        out_specs=[columns, columns, parts, parts],
        out_shape=[
            jax.ShapeDtypeStruct(queries.shape, jnp.bfloat16),
            jax.ShapeDtypeStruct(queries.shape, jnp.float32),
            jax.ShapeDtypeStruct((pairs, per * 2 * rows, D), jnp.float32),
            jax.ShapeDtypeStruct((pairs, per * 2 * rows, D), jnp.bfloat16),
        ],
        scratch_shapes=[
            pltpu.VMEM((pairs, per, 2, 2 * rows, D), jnp.bfloat16),
            pltpu.VMEM((pairs, 2 * rows, rows), jnp.float32),
            pltpu.VMEM((pairs, 2 * rows, wide), jnp.float32),
            pltpu.SMEM((1,), jnp.int32),
            pltpu.SMEM((pairs,), jnp.int32),
        ],
        input_output_aliases=aliases,
        compiler_params=pltpu.CompilerParams(vmem_limit_bytes=56 << 20),
        cost_estimate=pl.CostEstimate(flops=4 * macs, bytes_accessed=8 << 20, transcendentals=0),
    )(*args)


def add_kernel(mine_ref, got_ref, keep_ref, *sends):
    keep_ref[...] = mine_ref[0] + got_ref[0].astype(jnp.float32)
    for k, send in enumerate(sends):
        send[...] = (mine_ref[k + 1] + got_ref[k + 1].astype(jnp.float32)).astype(jnp.bfloat16)


def add_lanes(mine, got):
    pairs, tall, _ = mine.shape
    return pl.pallas_call(
        add_kernel,
        out_shape=[jax.ShapeDtypeStruct((tall, D), jnp.float32)]
        + [jax.ShapeDtypeStruct((tall, D), jnp.bfloat16)] * (pairs - 1),
        cost_estimate=pl.CostEstimate(flops=mine.size, bytes_accessed=8 * mine.size, transcendentals=0),
        compiler_params=pltpu.CompilerParams(vmem_limit_bytes=48 << 20),
    )(mine, got)


def finish_kernel(pairs, *refs):
    ins, (gk_ref, gv_ref) = refs[:-2], refs[-2:]
    rows = gk_ref.shape[1]
    per = ins[0].shape[0] // (2 * rows)
    for c in range(len(ins) // pairs):
        chunk = ins[c * pairs : (c + 1) * pairs]
        for g in range(per):
            cols = slice((c * per + g) * D, (c * per + g + 1) * D)
            for part, out in enumerate((gk_ref, gv_ref)):
                span = slice((2 * g + part) * rows, (2 * g + part + 1) * rows)
                total = chunk[0][span, :]
                for ref in chunk[1:]:
                    total = total + ref[span, :].astype(jnp.float32)
                out[0, :, cols] = total


def per_device(size, queries, key_matrix, value_matrix, cotangent, segment):
    rows = queries.shape[1]
    pairs = size // 2
    per = KV // CHUNKS
    here = lax.axis_index("ctx").astype(jnp.int32).reshape(1)
    swap = [(i, i ^ 1) for i in range(size)]

    def send(x, perm):
        return lax.ppermute(x, "ctx", perm)

    packed = pl.pallas_call(
        pack_kernel,
        out_shape=[jax.ShapeDtypeStruct((per * 2 * rows + 16, D), jnp.bfloat16)] * CHUNKS,
    )(key_matrix, value_matrix, segment)

    prev = None
    finals = []
    for c in range(CHUNKS):
        own = [packed[c]] + [
            send(packed[c], [(i, i + 2 * k) for i in range(size - 2 * k)]) for k in range(1, pairs)
        ]
        peer = [send(x, swap) for x in own]
        attended, grad_query, mine, theirs = attend(
            c, here, own, peer, queries, cotangent, segment, prev
        )
        prev = (attended, grad_query)
        keep, *down = add_lanes(mine, send(theirs, swap))
        finals.append(keep)
        finals += [
            send(x, [(i + 2 * k, i) for i in range(size - 2 * k)]) for k, x in enumerate(down, 1)
        ]
    grads = pl.pallas_call(
        functools.partial(finish_kernel, pairs),
        out_shape=[jax.ShapeDtypeStruct(key_matrix.shape, jnp.float32)] * 2,
    )(*finals)
    return (attended, grad_query, grads[0], grads[1])


def solution(mesh):
    wide = P(("groups", "dp"), "ctx", None)
    return jax.shard_map(
        functools.partial(per_device, mesh.shape["ctx"]),
        mesh=mesh,
        in_specs=(wide, wide, wide, wide, P(("groups", "dp"), "ctx")),
        out_specs=(wide, wide, wide, wide),
        check_vma=False,
    )
```

time: 296 us -> 123 us (0.42)
  the two profiles are of different devices: /device:TPU:0 before, /device:TPU:6 now
where the time goes in v1:
time: 123 us
  waiting for transfers between devices  85.4 us (69%)
  Pallas kernels  16.9 us (14%)
  starting transfers between devices  15.8 us (13%)
  local copies, waits for them, and re-layouts  3.9 us (3%)
    ppermute x11, waiting for transfers between devices, send(): return lax.ppermute(x, 'ctx', perm)  85.4 us
    ppermute x11, starting transfers between devices, send(): return lax.ppermute(x, 'ctx', perm)  15.8 us
    pallas_call x1, Pallas kernels, attend(): pl.pallas_call(functools.partial(attend_kernel, pairs, per, prev is not N...  12.9 us
    unnamed x24, local copies, waits for them, and re-layouts  3.9 us
  transfers between devices with their start and end apart: 11, of which 9 were waited for; matrix products, arithmetic and copies ran while one was open for 0% of the time, Pallas kernels for 0%

profile of v1, /device:TPU:6, one launch (start us, length us, event | category | flops | bytes accessed | tf_op | source)
XLA Modules:
  0.0 122.7 jit_solution(13604460533692361341)
XLA Ops:
  0.6 1.7 %shard_map.84.refs_0_ = bf16[1040,128]{1,0:T(8,128)(2,1)} custom-call(bf16[1,128,512]{2,1,0:T(8,128)(2,1)} %k_ref.1, bf16[1,128,512]{2,1,0:T(8,128)(2,1)} %v_ref.1, s32[1,128]{1,0:T(1,128)} %refs_10_.1), custom_call_target="tpu_custom_call" | custom-call | tf_op jit(solution)/shard_map/pallas_call | solution.py:225
  2.3 5.5 %collective-permute-start.2 = (bf16[1040,128]{1,0:T(8,128)(2,1)}, bf16[1040,128]{1,0:T(8,128)(2,1)S(1)}, u32[]{:S(2)}, u32[]{:S(2)}) collective-permute-start(bf16[1040,128]{1,0:T(8,128)(2,1)} %shard_map.84.refs_0_), channel_id=1, source_target_pairs={{0,6},{1,7},{8,14},{9,15},{16,22},{17,23},{24,30},{25,31}} | collective-permute-start | bytes 798728 | tf_op jit(solution)/shard_map/ppermute | solution.py:223
  7.9 1.3 %collective-permute-start.1 = (bf16[1040,128]{1,0:T(8,128)(2,1)}, bf16[1040,128]{1,0:T(8,128)(2,1)S(1)}, u32[]{:S(2)}, u32[]{:S(2)}) collective-permute-start(bf16[1040,128]{1,0:T(8,128)(2,1)} %shard_map.84.refs_0_), channel_id=1, source_target_pairs={{0,4},{1,5},{2,6},{3,7},{8,12},{9,13},{10,14},{11,15},{16,20},{17,... | collective-permute-start | bytes 798728 | tf_op jit(solution)/shard_map/ppermute | solution.py:223
  9.2 2.5 %collective-permute-start = (bf16[1040,128]{1,0:T(8,128)(2,1)}, bf16[1040,128]{1,0:T(8,128)(2,1)S(1)}, u32[]{:S(2)}, u32[]{:S(2)}) collective-permute-start(bf16[1040,128]{1,0:T(8,128)(2,1)} %shard_map.84.refs_0_), channel_id=1, source_target_pairs={{0,2},{1,3},{2,4},{3,5},{4,6},{5,7},{8,10},{9,11},{10,12},{11,13},... | collective-permute-start | bytes 798728 | tf_op jit(solution)/shard_map/ppermute | solution.py:223
  11.7 0.6 collective-permute-start.3
  12.2 2.8 %collective-permute-done.2.refs_3_ = bf16[1040,128]{1,0:T(8,128)(2,1)S(1)} collective-permute-done((bf16[1040,128]{1,0:T(8,128)(2,1)}, bf16[1040,128]{1,0:T(8,128)(2,1)S(1)}, u32[]{:S(2)}, u32[]{:S(2)}) %collective-permute-start.2) | collective-permute-done | bytes 266272 | tf_op jit(solution)/shard_map/ppermute | solution.py:223
  15.0 0.0 copy-start.5
  15.0 0.5 collective-permute-start.6
  15.5 5.2 %collective-permute-done.1.refs_2_ = bf16[1040,128]{1,0:T(8,128)(2,1)S(1)} collective-permute-done((bf16[1040,128]{1,0:T(8,128)(2,1)}, bf16[1040,128]{1,0:T(8,128)(2,1)S(1)}, u32[]{:S(2)}, u32[]{:S(2)}) %collective-permute-start.1) | collective-permute-done | bytes 266272 | tf_op jit(solution)/shard_map/ppermute | solution.py:223
  20.7 0.0 copy-start.6
  20.7 0.5 collective-permute-start.5
  21.2 4.0 %collective-permute-done.refs_1_ = bf16[1040,128]{1,0:T(8,128)(2,1)S(1)} collective-permute-done((bf16[1040,128]{1,0:T(8,128)(2,1)}, bf16[1040,128]{1,0:T(8,128)(2,1)S(1)}, u32[]{:S(2)}, u32[]{:S(2)}) %collective-permute-start) | collective-permute-done | bytes 266272 | tf_op jit(solution)/shard_map/ppermute | solution.py:223
  25.3 0.0 copy-start.7
  25.3 0.5 collective-permute-start.4
  25.8 0.0 collective-permute-done.3.refs_4_
  25.8 0.0 copy-start.8
  25.8 1.2 collective-permute-done.6.refs_7_
  27.0 0.0 copy-start.9
  27.0 5.7 %collective-permute-done.5.refs_6_ = bf16[1040,128]{1,0:T(8,128)(2,1)S(1)} collective-permute-done((bf16[1040,128]{1,0:T(8,128)(2,1)S(1)}, bf16[1040,128]{1,0:T(8,128)(2,1)S(1)}, u32[]{:S(2)}, u32[]{:S(2)}) %collective-permute-start.5) | collective-permute-done | bytes 266272 | tf_op jit(solution)/shard_map/ppermute | solution.py:223
  32.7 0.0 copy-start.10
  32.7 3.9 %collective-permute-done.4.refs_5_ = bf16[1040,128]{1,0:T(8,128)(2,1)S(1)} collective-permute-done((bf16[1040,128]{1,0:T(8,128)(2,1)S(1)}, bf16[1040,128]{1,0:T(8,128)(2,1)S(1)}, u32[]{:S(2)}, u32[]{:S(2)}) %collective-permute-start.4) | collective-permute-done | bytes 266272 | tf_op jit(solution)/shard_map/ppermute | solution.py:223
  36.6 0.0 copy-start.11
  36.6 0.0 copy-done.5
  36.6 0.0 copy-done.6
  36.6 0.0 copy-done.7
  36.6 0.0 copy-done.8
  36.6 0.0 copy-done.9
  36.7 0.0 copy-done.10
  36.7 0.7 copy-done.11
  37.3 12.9 %shard_map.85 = (bf16[1,128,4096]{2,1,0:T(8,128)(2,1)}, f32[1,128,4096]{2,1,0:T(8,128)}, f32[4,1024,128]{2,1,0:T(8,128)}, bf16[4,1024,128]{2,1,0:T(8,128)(2,1)}) custom-call(s32[1]{0:T(128)} %bitcast.here_ref, bf16[1040,128]{1,0:T(8,128)(2,1)} %shard_map.84.refs_0_, bf16[1040,128]{1,0:T(8,128)(2,1)} %copy-done.7, bf16[1040,128]{1,0:T(8,128)(2,1)} %copy-done.6, ...), custom_call_target="tpu_custom_call" | custom-call | flops 12884901888 | bytes 8388608 | tf_op jit(solution)/shard_map/pallas_call | solution.py:158
  50.2 0.5 collective-permute-start.7
  50.8 23.1 %collective-permute-done.7.got_ref = bf16[4,1024,128]{2,1,0:T(8,128)(2,1)S(1)} collective-permute-done((bf16[4,1024,128]{2,1,0:T(8,128)(2,1)}, bf16[4,1024,128]{2,1,0:T(8,128)(2,1)S(1)}, u32[]{:S(2)}, u32[]{:S(2)}) %collective-permute-start.7) | collective-permute-done | bytes 1048608 | tf_op jit(solution)/shard_map/ppermute | solution.py:223
  73.9 0.0 copy-start
  73.9 1.6 %copy-done = f32[4,1024,128]{2,1,0:T(8,128)S(1)} copy-done((f32[4,1024,128]{2,1,0:T(8,128)S(1)}, f32[4,1024,128]{2,1,0:T(8,128)}, u32[]{:S(2)}) %copy-start) | copy-done | bytes 2097176
  75.5 0.2 shard_map.86
  75.6 0.0 copy-start.1
  75.6 0.8 copy-done.1
  76.4 1.3 %collective-permute-start.8 = (bf16[1024,128]{1,0:T(8,128)(2,1)S(1)}, bf16[1024,128]{1,0:T(8,128)(2,1)S(1)}, u32[]{:S(2)}, u32[]{:S(2)}) collective-permute-start(bf16[1024,128]{1,0:T(8,128)(2,1)S(1)} %get-tuple-element.19), channel_id=1, source_target_pairs={{2,0},{3,1},{4,2},{5,3},{6,4},{7,5},{10,8},{11,9},{12,10},{13,11},... | collective-permute-start | bytes 786440 | tf_op jit(solution)/shard_map/ppermute | solution.py:223
  77.7 1.3 %collective-permute-start.9 = (bf16[1024,128]{1,0:T(8,128)(2,1)S(1)}, bf16[1024,128]{1,0:T(8,128)(2,1)S(1)}, u32[]{:S(2)}, u32[]{:S(2)}) collective-permute-start(bf16[1024,128]{1,0:T(8,128)(2,1)S(1)} %get-tuple-element.20), channel_id=1, source_target_pairs={{4,0},{5,1},{6,2},{7,3},{12,8},{13,9},{14,10},{15,11},{20,16},{21,... | collective-permute-start | bytes 786440 | tf_op jit(solution)/shard_map/ppermute | solution.py:223
  79.0 1.3 %collective-permute-start.10 = (bf16[1024,128]{1,0:T(8,128)(2,1)S(1)}, bf16[1024,128]{1,0:T(8,128)(2,1)S(1)}, u32[]{:S(2)}, u32[]{:S(2)}) collective-permute-start(bf16[1024,128]{1,0:T(8,128)(2,1)S(1)} %get-tuple-element.21), channel_id=1, source_target_pairs={{6,0},{7,1},{14,8},{15,9},{22,16},{23,17},{30,24},{31,25}} | collective-permute-start | bytes 786440 | tf_op jit(solution)/shard_map/ppermute | solution.py:223
  80.3 13.4 %collective-permute-done.8.refs_1_ = bf16[1024,128]{1,0:T(8,128)(2,1)S(1)} collective-permute-done((bf16[1024,128]{1,0:T(8,128)(2,1)S(1)}, bf16[1024,128]{1,0:T(8,128)(2,1)S(1)}, u32[]{:S(2)}, u32[]{:S(2)}) %collective-permute-start.8) | collective-permute-done | bytes 262176 | tf_op jit(solution)/shard_map/ppermute | solution.py:223
  93.7 0.0 copy-start.2
  93.8 26.0 %collective-permute-done.9.refs_2_ = bf16[1024,128]{1,0:T(8,128)(2,1)S(1)} collective-permute-done((bf16[1024,128]{1,0:T(8,128)(2,1)S(1)}, bf16[1024,128]{1,0:T(8,128)(2,1)S(1)}, u32[]{:S(2)}, u32[]{:S(2)}) %collective-permute-start.9) | collective-permute-done | bytes 262176 | tf_op jit(solution)/shard_map/ppermute | solution.py:223
  119.8 0.0 collective-permute-done.10.refs_3_
  119.8 0.0 copy-done.2
  119.8 0.7 copy-done.3
  120.5 0.1 copy-done.4
  120.6 2.1 %shard_map.87 = (f32[1,128,512]{2,1,0:T(8,128)}, f32[1,128,512]{2,1,0:T(8,128)}) custom-call(f32[1024,128]{1,0:T(8,128)} %copy-done.1, bf16[1024,128]{1,0:T(8,128)(2,1)} %copy-done.2, bf16[1024,128]{1,0:T(8,128)(2,1)} %copy-done.3, bf16[1024,128]{1,0:T(8,128)(2,1)} %copy-done.4), custom_call_target="tpu_custom_call" | custom-call | tf_op jit(solution)/shard_map/pallas_call | solution.py:246
  (2 shorter events, 0.0 us)
Async XLA Ops:
  2.3 12.7 %collective-permute-start.2 = (bf16[1040,128]{1,0:T(8,128)(2,1)}, bf16[1040,128]{1,0:T(8,128)(2,1)S(1)}, u32[]{:S(2)}, u32[]{:S(2)}) collective-permute-start(bf16[1040,128]{1,0:T(8,128)(2,1)} %shard_map.84.refs_0_), channel_id=1, source_target_pairs={{0,6},{1,7},{8,14},{9,15},{16,22},{17,23},{24,30},{25,31}} | collective-permute-start | bytes 798728 | tf_op jit(solution)/shard_map/ppermute | solution.py:223
  7.9 12.9 %collective-permute-start.1 = (bf16[1040,128]{1,0:T(8,128)(2,1)}, bf16[1040,128]{1,0:T(8,128)(2,1)S(1)}, u32[]{:S(2)}, u32[]{:S(2)}) collective-permute-start(bf16[1040,128]{1,0:T(8,128)(2,1)} %shard_map.84.refs_0_), channel_id=1, source_target_pairs={{0,4},{1,5},{2,6},{3,7},{8,12},{9,13},{10,14},{11,15},{16,20},{17,... | collective-permute-start | bytes 798728 | tf_op jit(solution)/shard_map/ppermute | solution.py:223
  9.2 16.1 %collective-permute-start = (bf16[1040,128]{1,0:T(8,128)(2,1)}, bf16[1040,128]{1,0:T(8,128)(2,1)S(1)}, u32[]{:S(2)}, u32[]{:S(2)}) collective-permute-start(bf16[1040,128]{1,0:T(8,128)(2,1)} %shard_map.84.refs_0_), channel_id=1, source_target_pairs={{0,2},{1,3},{2,4},{3,5},{4,6},{5,7},{8,10},{9,11},{10,12},{11,13},... | collective-permute-start | bytes 798728 | tf_op jit(solution)/shard_map/ppermute | solution.py:223
  11.7 14.2 %collective-permute-start.3 = (bf16[1040,128]{1,0:T(8,128)(2,1)}, bf16[1040,128]{1,0:T(8,128)(2,1)S(1)}, u32[]{:S(2)}, u32[]{:S(2)}) collective-permute-start(bf16[1040,128]{1,0:T(8,128)(2,1)} %shard_map.84.refs_0_), channel_id=1, source_target_pairs={{0,1},{1,0},{2,3},{3,2},{4,5},{5,4},{6,7},{7,6},{8,9},{9,8},{10,11... | collective-permute-start | bytes 798728 | tf_op jit(solution)/shard_map/ppermute | solution.py:223
  15.0 21.6 %copy-start.5 = (bf16[1040,128]{1,0:T(8,128)(2,1)}, bf16[1040,128]{1,0:T(8,128)(2,1)S(1)}, u32[]{:S(2)}) copy-start(bf16[1040,128]{1,0:T(8,128)(2,1)S(1)} %collective-permute-done.2.refs_3_) | copy-start | bytes 798724
  15.0 11.9 %collective-permute-start.6 = (bf16[1040,128]{1,0:T(8,128)(2,1)S(1)}, bf16[1040,128]{1,0:T(8,128)(2,1)S(1)}, u32[]{:S(2)}, u32[]{:S(2)}) collective-permute-start(bf16[1040,128]{1,0:T(8,128)(2,1)S(1)} %collective-permute-done.2.refs_3_), channel_id=1, source_target_pairs={{0,1},{1,0},{2,3},{3,2},{4,5},{5,4},{6,7},{7,6},{8,9},{9,8},{10,11... | collective-permute-start | bytes 798728 | tf_op jit(solution)/shard_map/ppermute | solution.py:223
  20.7 15.9 %copy-start.6 = (bf16[1040,128]{1,0:T(8,128)(2,1)}, bf16[1040,128]{1,0:T(8,128)(2,1)S(1)}, u32[]{:S(2)}) copy-start(bf16[1040,128]{1,0:T(8,128)(2,1)S(1)} %collective-permute-done.1.refs_2_) | copy-start | bytes 798724
  20.7 11.9 %collective-permute-start.5 = (bf16[1040,128]{1,0:T(8,128)(2,1)S(1)}, bf16[1040,128]{1,0:T(8,128)(2,1)S(1)}, u32[]{:S(2)}, u32[]{:S(2)}) collective-permute-start(bf16[1040,128]{1,0:T(8,128)(2,1)S(1)} %collective-permute-done.1.refs_2_), channel_id=1, source_target_pairs={{0,1},{1,0},{2,3},{3,2},{4,5},{5,4},{6,7},{7,6},{8,9},{9,8},{10,11... | collective-permute-start | bytes 798728 | tf_op jit(solution)/shard_map/ppermute | solution.py:223
  25.3 11.3 %copy-start.7 = (bf16[1040,128]{1,0:T(8,128)(2,1)}, bf16[1040,128]{1,0:T(8,128)(2,1)S(1)}, u32[]{:S(2)}) copy-start(bf16[1040,128]{1,0:T(8,128)(2,1)S(1)} %collective-permute-done.refs_1_) | copy-start | bytes 798724
  25.3 11.3 %collective-permute-start.4 = (bf16[1040,128]{1,0:T(8,128)(2,1)S(1)}, bf16[1040,128]{1,0:T(8,128)(2,1)S(1)}, u32[]{:S(2)}, u32[]{:S(2)}) collective-permute-start(bf16[1040,128]{1,0:T(8,128)(2,1)S(1)} %collective-permute-done.refs_1_), channel_id=1, source_target_pairs={{0,1},{1,0},{2,3},{3,2},{4,5},{5,4},{6,7},{7,6},{8,9},{9,8},{10,11... | collective-permute-start | bytes 798728 | tf_op jit(solution)/shard_map/ppermute | solution.py:223
  25.8 10.8 %copy-start.8 = (bf16[1040,128]{1,0:T(8,128)(2,1)}, bf16[1040,128]{1,0:T(8,128)(2,1)S(1)}, u32[]{:S(2)}) copy-start(bf16[1040,128]{1,0:T(8,128)(2,1)S(1)} %collective-permute-done.3.refs_4_) | copy-start | bytes 798724
  27.0 9.7 %copy-start.9 = (bf16[1040,128]{1,0:T(8,128)(2,1)}, bf16[1040,128]{1,0:T(8,128)(2,1)S(1)}, u32[]{:S(2)}) copy-start(bf16[1040,128]{1,0:T(8,128)(2,1)S(1)} %collective-permute-done.6.refs_7_) | copy-start | bytes 798724
  32.7 4.0 %copy-start.10 = (bf16[1040,128]{1,0:T(8,128)(2,1)}, bf16[1040,128]{1,0:T(8,128)(2,1)S(1)}, u32[]{:S(2)}) copy-start(bf16[1040,128]{1,0:T(8,128)(2,1)S(1)} %collective-permute-done.5.refs_6_) | copy-start | bytes 798724
  36.6 0.7 copy-start.11
  50.2 23.6 %collective-permute-start.7 = (bf16[4,1024,128]{2,1,0:T(8,128)(2,1)}, bf16[4,1024,128]{2,1,0:T(8,128)(2,1)S(1)}, u32[]{:S(2)}, u32[]{:S(2)}) collective-permute-start(bf16[4,1024,128]{2,1,0:T(8,128)(2,1)} %get-tuple-element.17), channel_id=1, source_target_pairs={{0,1},{1,0},{2,3},{3,2},{4,5},{5,4},{6,7},{7,6},{8,9},{9,8},{10,11... | collective-permute-start | bytes 3145736 | tf_op jit(solution)/shard_map/ppermute | solution.py:223
  73.9 1.6 %copy-start = (f32[4,1024,128]{2,1,0:T(8,128)S(1)}, f32[4,1024,128]{2,1,0:T(8,128)}, u32[]{:S(2)}) copy-start(f32[4,1024,128]{2,1,0:T(8,128)} %get-tuple-element.16.mine_ref) | copy-start | bytes 6291460
  75.6 0.8 copy-start.1
  76.4 17.3 %collective-permute-start.8 = (bf16[1024,128]{1,0:T(8,128)(2,1)S(1)}, bf16[1024,128]{1,0:T(8,128)(2,1)S(1)}, u32[]{:S(2)}, u32[]{:S(2)}) collective-permute-start(bf16[1024,128]{1,0:T(8,128)(2,1)S(1)} %get-tuple-element.19), channel_id=1, source_target_pairs={{2,0},{3,1},{4,2},{5,3},{6,4},{7,5},{10,8},{11,9},{12,10},{13,11},... | collective-permute-start | bytes 786440 | tf_op jit(solution)/shard_map/ppermute | solution.py:223
  77.7 42.0 %collective-permute-start.9 = (bf16[1024,128]{1,0:T(8,128)(2,1)S(1)}, bf16[1024,128]{1,0:T(8,128)(2,1)S(1)}, u32[]{:S(2)}, u32[]{:S(2)}) collective-permute-start(bf16[1024,128]{1,0:T(8,128)(2,1)S(1)} %get-tuple-element.20), channel_id=1, source_target_pairs={{4,0},{5,1},{6,2},{7,3},{12,8},{13,9},{14,10},{15,11},{20,16},{21,... | collective-permute-start | bytes 786440 | tf_op jit(solution)/shard_map/ppermute | solution.py:223
  79.0 40.8 %collective-permute-start.10 = (bf16[1024,128]{1,0:T(8,128)(2,1)S(1)}, bf16[1024,128]{1,0:T(8,128)(2,1)S(1)}, u32[]{:S(2)}, u32[]{:S(2)}) collective-permute-start(bf16[1024,128]{1,0:T(8,128)(2,1)S(1)} %get-tuple-element.21), channel_id=1, source_target_pairs={{6,0},{7,1},{14,8},{15,9},{22,16},{23,17},{30,24},{31,25}} | collective-permute-start | bytes 786440 | tf_op jit(solution)/shard_map/ppermute | solution.py:223
  93.7 26.0 %copy-start.2 = (bf16[1024,128]{1,0:T(8,128)(2,1)}, bf16[1024,128]{1,0:T(8,128)(2,1)S(1)}, u32[]{:S(2)}) copy-start(bf16[1024,128]{1,0:T(8,128)(2,1)S(1)} %collective-permute-done.8.refs_1_) | copy-start | bytes 786436
  119.8 0.7 copy-start.3
  119.8 0.8 copy-start.4

commit v2 on v1

v2 whole, which is shorter than its diff:
```python
import functools
import math

import jax
import jax.numpy as jnp
from jax import lax
from jax.experimental import pallas as pl
from jax.experimental.pallas import tpu as pltpu
from jax.sharding import PartitionSpec as P

KV = 4
D = 128
CHUNKS = 2
BUNDLE = 4
LANES = 256
STEPS = 4
NEG = -1e30
NN = (((1,), (0,)), ((), ()))
NT = (((1,), (1,)), ((), ()))
TN = (((0,), (0,)), ((), ()))


def dot(a, b, dims):
    return lax.dot_general(a, b, dims, preferred_element_type=jnp.float32)


def pack_kernel(k_ref, v_ref, s_ref, *outs):
    rows = k_ref.shape[1]
    per = KV // len(outs)
    seg = jnp.broadcast_to(s_ref[...].astype(jnp.float32), (16, rows)).astype(jnp.bfloat16)
    for c, out in enumerate(outs):
        for g in range(per):
            cols = slice((c * per + g) * D, (c * per + g + 1) * D)
            out[2 * g * rows : (2 * g + 1) * rows, :] = k_ref[0, :, cols]
            out[(2 * g + 1) * rows : (2 * g + 2) * rows, :] = v_ref[0, :, cols]
        out[2 * per * rows :, :] = seg


def loop(count, body, start, pairs):
    if pairs <= BUNDLE:
        return body(0, start)
    return lax.fori_loop(0, count, body, start)


def attend_kernel(pairs, per, chunk, lanes, has_prev, here_ref, *refs):
    own = refs[:pairs]
    peer = refs[pairs : 2 * pairs]
    q_ref, c_ref, sq_ref = refs[2 * pairs : 2 * pairs + 3]
    refs = refs[2 * pairs + 3 + (2 if has_prev else 0) :]
    out_ref, gq_ref = refs[:2]
    parts = refs[2:8]
    kv, mask, s_scr, p_scr, e_scr, probs_scr, slopes_scr, out_scr, gq_scr, cnt, order, sems = refs[8:]
    rows = q_ref.shape[1]
    heads = q_ref.shape[2] // KV // D
    each = heads * D
    static = pairs <= BUNDLE
    wide = heads * rows
    two = 2 * rows
    tall = BUNDLE * two
    scale = 1.0 / math.sqrt(D)
    power = scale * math.log2(math.e)
    here = here_ref[0]

    seg_q = sq_ref[...].astype(jnp.float32)
    q_pos = here * rows + lax.broadcasted_iota(jnp.int32, (rows, rows), 1)
    local = lax.broadcasted_iota(jnp.int32, (rows, rows), 0)
    sources = [src for k in range(pairs) for src in (own[k], peer[k])]
    base = 2 * per * rows
    seg_rows = [src[base : base + 16, :].astype(jnp.float32)[:1] for src in sources]
    seg_rows.append(jnp.zeros((rows - len(sources), rows), jnp.float32))
    seg_cols = jnp.transpose(jnp.concatenate(seg_rows, axis=0))

    def masks(k):
        adds = []
        for lane in range(2):
            block = (here ^ lane) - 2 * k
            seg_k = seg_cols[:, 2 * k + lane : 2 * k + lane + 1]
            ok = (block * rows + local <= q_pos) & ((seg_k == seg_q) | (seg_k == 0.0)) & (block >= 0)
            adds.append(jnp.where(ok, 0.0, NEG))
        return adds

    def store(at, k, adds):
        for lane, src in enumerate((own[k], peer[k])):
            to = pl.ds(pl.multiple_of(at + lane * rows, rows), rows)
            mask[to, :] = adds[lane]
            for h in range(per):
                for part in range(2):
                    kv[h, part, to, :] = src[(2 * h + part) * rows : (2 * h + part + 1) * rows, :]

    if static:
        for k in range(pairs):
            store(k * two, k, masks(k))
    else:
        cnt[0] = 0
        for k in range(pairs):
            adds = masks(k)

            @pl.when(jnp.max(jnp.maximum(adds[0], adds[1])) == 0.0)
            def _():
                store(cnt[0] * two, k, adds)
                order[cnt[0]] = k
                cnt[0] = cnt[0] + 1

        def blank(t, carry):
            at = pl.ds(pl.multiple_of(t * two, two), two)
            mask[at, :] = jnp.full((two, rows), NEG, jnp.float32)
            kv[:, :, at, :] = jnp.zeros((per, 2, two, D), jnp.bfloat16)
            order[t] = -1
            return carry

        lax.fori_loop(cnt[0], pl.cdiv(cnt[0], BUNDLE) * BUNDLE, blank, 0)
        for ref in parts:
            ref[...] = jnp.zeros_like(ref)
    bundles = None if static else pl.cdiv(cnt[0], BUNDLE)
    copies = []

    def send(src, ref, g, which):
        to = ref.at[0, :, pl.ds((chunk * per + g) * each, each)]
        copy = pltpu.make_async_copy(src.at[g], to, sems.at[2 * g + which])
        copy.start()
        copies.append(copy)

    def stack(ref, g):
        first = (chunk * per + g) * heads
        return jnp.concatenate([ref[0, :, (first + h) * D : (first + h + 1) * D] for h in range(heads)], axis=0)

    def tile(t, j):
        step = tall // STEPS
        return pl.ds(pl.multiple_of(t * tall + j * step, step), step)

    def span_of(t):
        return pl.ds(pl.multiple_of(t * tall, tall), tall)

    def one_head(g):
        q_all = stack(q_ref, g)
        c_all = stack(c_ref, g)
        at = g * two
        for w in range(wide // lanes):
            cols = slice(w * lanes, (w + 1) * lanes)
            q_w, c_w = q_all[cols], c_all[cols]

            def scores(t, top, q_w=q_w, c_w=c_w):
                span = span_of(t)
                s = dot(kv[g, 0, span, :], q_w, NT)
                s = s + jnp.concatenate([mask[span, :]] * (lanes // rows), axis=1)
                s_scr[span, :] = s
                p_scr[span, :] = dot(kv[g, 1, span, :], c_w, NT)
                top = jnp.maximum(top, jnp.max(s, axis=0, keepdims=True))
                return top

            top = loop(bundles, scores, jnp.full((1, lanes), NEG, jnp.float32), pairs)

            def forward(t, carry, top=top):
                total, delta, acc = carry
                for j in range(STEPS):
                    at = tile(t, j)
                    e = jnp.exp2((s_scr[at, :] - top) * power)
                    s_scr[at, :] = e
                    e_scr[at, :] = e.astype(jnp.bfloat16)
                    total = total + jnp.sum(e, axis=0, keepdims=True)
                    delta = delta + jnp.sum(e * p_scr[at, :], axis=0, keepdims=True)
                span = span_of(t)
                return total, delta, acc + dot(kv[g, 1, span, :], e_scr[span, :], TN)

            row = jnp.zeros((1, lanes), jnp.float32)
            total, delta, acc = loop(bundles, forward, (row, row, jnp.zeros((D, lanes), jnp.float32)), pairs)
            inverse = 1.0 / total
            delta = delta * inverse
            acc = acc * inverse
            for h in range(lanes // rows):
                to = slice((w * lanes // rows + h) * D, (w * lanes // rows + h + 1) * D)
                out_scr[g, :, to] = jnp.transpose(acc[:, h * rows : (h + 1) * rows]).astype(jnp.bfloat16)

            def backward(t, acc, inverse=inverse, delta=delta, cols=cols):
                for j in range(STEPS):
                    at = tile(t, j)
                    probs = s_scr[at, :] * inverse
                    probs_scr[at, cols] = probs.astype(jnp.bfloat16)
                    slopes_scr[at, cols] = (probs * (p_scr[at, :] - delta)).astype(jnp.bfloat16)
                span = span_of(t)
                return acc + dot(kv[g, 0, span, :], slopes_scr[span, cols], TN)

            grad = loop(bundles, backward, jnp.zeros((D, lanes), jnp.float32), pairs) * scale
            for h in range(lanes // rows):
                to = slice((w * lanes // rows + h) * D, (w * lanes // rows + h + 1) * D)
                gq_scr[g, :, to] = jnp.transpose(grad[:, h * rows : (h + 1) * rows])

        send(out_scr, out_ref, g, 0)
        send(gq_scr, gq_ref, g, 1)

        def key_side(t, carry):
            span = span_of(t)
            all_v = dot(probs_scr[span, :], c_all, NN)
            all_k = dot(slopes_scr[span, :], q_all, NN) * scale
            for j in range(BUNDLE):
                k = None if static else order[t * BUNDLE + j]
                grad_v = all_v[j * two : (j + 1) * two]
                grad_k = all_k[j * two : (j + 1) * two]

                def keep(first, slot):
                    for lane, ref in enumerate(parts[first : first + 2]):
                        part = slice(lane * rows, (lane + 1) * rows)
                        ref[slot, pl.ds(at, rows), :] = grad_k[part].astype(ref.dtype)
                        ref[slot, pl.ds(at + rows, rows), :] = grad_v[part].astype(ref.dtype)

                if static:
                    keep(*((0, 0) if j == 0 else (4, 0) if j == pairs - 1 else (2, j - 1)))
                    continue
                pl.when(k == 0)(lambda: keep(0, 0))
                pl.when((k > 0) & (k < pairs - 1))(lambda: keep(2, k - 1))
                pl.when(k == pairs - 1)(lambda: keep(4, 0))
            return carry

        loop(bundles, key_side, 0, pairs)

    for g in range(per):
        one_head(g)
    for copy in copies:
        copy.wait()


def attend(chunk, here, own, peer, queries, cotangent, segment, prev):
    pairs = len(own)
    per = KV // CHUNKS
    _, rows, width = queries.shape
    each = width // KV
    wide = each // D * rows
    lanes = wide if pairs <= BUNDLE else LANES
    keys = pl.cdiv(pairs, BUNDLE) * BUNDLE * 2 * rows
    vmem = pl.BlockSpec(memory_space=pltpu.VMEM)
    hbm = pl.BlockSpec(memory_space=pl.ANY)
    parts = [
        jax.ShapeDtypeStruct((count, per * 2 * rows, D), dtype)
        for count, dtype in (
            (1, jnp.float32),
            (1, jnp.float32),
            (pairs - 2, jnp.float32),
            (pairs - 2, jnp.bfloat16),
            (1, jnp.bfloat16),
            (1, jnp.bfloat16),
        )
    ]
    args = [here, *own, *peer, queries, cotangent, segment]
    in_specs = [pl.BlockSpec(memory_space=pltpu.SMEM)] + [vmem] * (len(args) - 1)
    aliases = {}
    if prev is not None:
        aliases = {len(args): 0, len(args) + 1: 1}
        args += list(prev)
        in_specs += [hbm] * 2
    macs = per * wide * 2 * rows * D * 6 * pairs
    return pl.pallas_call(
        functools.partial(attend_kernel, pairs, per, chunk, lanes, prev is not None),
        in_specs=in_specs,
        out_specs=[hbm, hbm] + [vmem] * len(parts),
        out_shape=[
            jax.ShapeDtypeStruct(queries.shape, jnp.bfloat16),
            jax.ShapeDtypeStruct(queries.shape, jnp.float32),
            *parts,
        ],
        scratch_shapes=[
            pltpu.VMEM((per, 2, keys, D), jnp.bfloat16),
            pltpu.VMEM((keys, rows), jnp.float32),
            pltpu.VMEM((keys, lanes), jnp.float32),
            pltpu.VMEM((keys, lanes), jnp.float32),
            pltpu.VMEM((keys, lanes), jnp.bfloat16),
            pltpu.VMEM((keys, wide), jnp.bfloat16),
            pltpu.VMEM((keys, wide), jnp.bfloat16),
            pltpu.VMEM((per, rows, each), jnp.bfloat16),
            pltpu.VMEM((per, rows, each), jnp.float32),
            pltpu.SMEM((1,), jnp.int32),
            pltpu.SMEM((pl.cdiv(pairs, BUNDLE) * BUNDLE,), jnp.int32),
            pltpu.SemaphoreType.DMA((2 * per,)),
        ],
        input_output_aliases=aliases,
        compiler_params=pltpu.CompilerParams(vmem_limit_bytes=(32 if pairs <= BUNDLE else 48) << 20),
        cost_estimate=pl.CostEstimate(flops=4 * macs, bytes_accessed=8 << 20, transcendentals=0),
    )(*args)


def add_kernel(mine_ref, got_ref, theirs_ref, last_ref, first_ref, *sends):
    first_ref[...] = (theirs_ref[0] + last_ref[0].astype(jnp.float32)).astype(jnp.bfloat16)
    for k, send in enumerate(sends):
        send[...] = (mine_ref[k] + got_ref[k].astype(jnp.float32)).astype(jnp.bfloat16)


def add_lanes(mine, got, theirs, last):
    count, tall, _ = mine.shape
    return pl.pallas_call(
        add_kernel,
        out_shape=[jax.ShapeDtypeStruct((tall, D), jnp.bfloat16)] * (count + 1),
        cost_estimate=pl.CostEstimate(flops=mine.size, bytes_accessed=8 * mine.size, transcendentals=0),
        compiler_params=pltpu.CompilerParams(vmem_limit_bytes=48 << 20),
    )(mine, got, theirs, last)


def finish_kernel(pairs, *refs):
    ins, (gk_ref, gv_ref) = refs[:-2], refs[-2:]
    rows = gk_ref.shape[1]
    each = pairs + 1
    per = ins[0].shape[1] // (2 * rows)
    for c in range(len(ins) // each):
        mine, last, *others = ins[c * each : (c + 1) * each]
        for g in range(per):
            cols = slice((c * per + g) * D, (c * per + g + 1) * D)
            for part, out in enumerate((gk_ref, gv_ref)):
                span = slice((2 * g + part) * rows, (2 * g + part + 1) * rows)
                total = mine[0, span, :] + last[0, span, :].astype(jnp.float32)
                for ref in others:
                    total = total + ref[span, :].astype(jnp.float32)
                out[0, :, cols] = total


def per_device(size, queries, key_matrix, value_matrix, cotangent, segment):
    rows = queries.shape[1]
    pairs = size // 2
    per = KV // CHUNKS
    here = lax.axis_index("ctx").astype(jnp.int32).reshape(1)

    def up(x, k):
        return lax.ppermute(x, "ctx", [(i, i + 2 * k) for i in range(size - 2 * k)])

    def down(x, k):
        return lax.ppermute(x, "ctx", [(i + 2 * k, i) for i in range(size - 2 * k)])

    def swap(x):
        return lax.ppermute(x, "ctx", [(i, i ^ 1) for i in range(size)])

    packed = pl.pallas_call(
        pack_kernel,
        out_shape=[jax.ShapeDtypeStruct((per * 2 * rows + 16, D), jnp.bfloat16)] * CHUNKS,
    )(key_matrix, value_matrix, segment)

    prev = None
    finals = []
    for c in range(CHUNKS):
        block = packed[c]
        own = [block] + [up(block, k) for k in range(1, pairs)]
        other = swap(block)
        peer = [other] + [swap(x) for x in own[1:-1]] + [up(other, pairs - 1)]
        attended, grad_query, mine_0, theirs_0, mine_mid, theirs_mid, mine_last, theirs_last = attend(
            c, here, own, peer, queries, cotangent, segment, prev
        )
        prev = (attended, grad_query)
        first, *mids = add_lanes(
            mine_mid, swap(theirs_mid), theirs_0, down(theirs_last, pairs - 1)
        )
        finals += [mine_0, down(mine_last, pairs - 1), swap(first)]
        finals += [down(x, k) for k, x in enumerate(mids, 1)]
    grads = pl.pallas_call(
        functools.partial(finish_kernel, pairs),
        out_shape=[jax.ShapeDtypeStruct(key_matrix.shape, jnp.float32)] * 2,
    )(*finals)
    return (attended, grad_query, grads[0], grads[1])


def solution(mesh):
    wide = P(("groups", "dp"), "ctx", None)
    return jax.shard_map(
        functools.partial(per_device, mesh.shape["ctx"]),
        mesh=mesh,
        in_specs=(wide, wide, wide, wide, P(("groups", "dp"), "ctx")),
        out_specs=(wide, wide, wide, wide),
        check_vma=False,
    )
```

time: 123 us -> 98.4 us (0.80)
  the two profiles are of different devices: /device:TPU:6 before, /device:TPU:0 now
where the time goes in v2:
time: 98.4 us; the launch traced here: 97.8 us
  starting transfers between devices  49.2 us (50%)
  Pallas kernels  22.9 us (23%)
  waiting for transfers between devices  18.7 us (19%)
  local copies, waits for them, and re-layouts  6.05 us (6%)
  between operations  1.01 us (1%)
    ppermute x8, starting transfers between devices, up(): return lax.ppermute(x, 'ctx', [(i, i + 2 * k) for i in range(size - 2 * k)])  27.1 us
    pallas_call x2, Pallas kernels, attend(): pl.pallas_call(functools.partial(attend_kernel, pairs, per, chunk, lanes,...  18.7 us
    ppermute x8, waiting for transfers between devices, down(): return lax.ppermute(x, 'ctx', [(i + 2 * k, i) for i in range(size - 2 * k)])  18.6 us
    ppermute x10, starting transfers between devices, swap(): return lax.ppermute(x, 'ctx', [(i, i ^ 1) for i in range(size)])  11.9 us
    ppermute x8, starting transfers between devices, down(): return lax.ppermute(x, 'ctx', [(i + 2 * k, i) for i in range(size - 2 * k)])  10.3 us
    unnamed x34, local copies, waits for them, and re-layouts  6.05 us
    pallas_call x1, Pallas kernels, per_device(): pl.pallas_call(functools.partial(finish_kernel, pairs), out_shape=[jax.Sh...  2.3 us
  transfers between devices with their start and end apart: 26, of which 5 were waited for; matrix products, arithmetic and copies ran while one was open for 0% of the time, Pallas kernels for 19%

profile of v2, /device:TPU:0, one launch (start us, length us, event | category | flops | bytes accessed | tf_op | source)
XLA Modules:
  0.0 97.8 jit_solution(3246721576891485856)
XLA Ops:
  0.6 1.7 %shard_map.84 = (bf16[528,128]{1,0:T(8,128)(2,1)}, bf16[528,128]{1,0:T(8,128)(2,1)}) custom-call(bf16[1,128,512]{2,1,0:T(8,128)(2,1)} %k_ref.1, bf16[1,128,512]{2,1,0:T(8,128)(2,1)} %v_ref.1, s32[1,128]{1,0:T(1,128)} %refs_10_.3), custom_call_target="tpu_custom_call" | custom-call | tf_op jit(solution)/shard_map/pallas_call | solution.py:328
  2.3 3.0 %collective-permute-start.3 = (bf16[528,128]{1,0:T(8,128)(2,1)}, bf16[528,128]{1,0:T(8,128)(2,1)S(1)}, u32[]{:S(2)}, u32[]{:S(2)}) collective-permute-start(bf16[528,128]{1,0:T(8,128)(2,1)} %get-tuple-element.30.refs_0_), channel_id=1, source_target_pairs={{0,1},{1,0},{2,3},{3,2},{4,5},{5,4},{6,7},{7,6},{8,9},{9,8},{10,11... | collective-permute-start | bytes 405512 | tf_op jit(solution)/shard_map/ppermute | solution.py:326
  5.3 4.5 %collective-permute-start.1 = (bf16[528,128]{1,0:T(8,128)(2,1)}, bf16[528,128]{1,0:T(8,128)(2,1)S(1)}, u32[]{:S(2)}, u32[]{:S(2)}) collective-permute-start(bf16[528,128]{1,0:T(8,128)(2,1)} %get-tuple-element.30.refs_0_), channel_id=1, source_target_pairs={{0,4},{1,5},{2,6},{3,7},{8,12},{9,13},{10,14},{11,15},{16,20},{17,... | collective-permute-start | bytes 405512 | tf_op jit(solution)/shard_map/ppermute | solution.py:320
  9.8 0.6 collective-permute-start.10
  10.4 1.3 %collective-permute-start.8 = (bf16[528,128]{1,0:T(8,128)(2,1)}, bf16[528,128]{1,0:T(8,128)(2,1)S(1)}, u32[]{:S(2)}, u32[]{:S(2)}) collective-permute-start(bf16[528,128]{1,0:T(8,128)(2,1)} %get-tuple-element.31.refs_0_), channel_id=1, source_target_pairs={{0,4},{1,5},{2,6},{3,7},{8,12},{9,13},{10,14},{11,15},{16,20},{17,... | collective-permute-start | bytes 405512 | tf_op jit(solution)/shard_map/ppermute | solution.py:320
  11.7 3.5 %collective-permute-start.7 = (bf16[528,128]{1,0:T(8,128)(2,1)}, bf16[528,128]{1,0:T(8,128)(2,1)S(1)}, u32[]{:S(2)}, u32[]{:S(2)}) collective-permute-start(bf16[528,128]{1,0:T(8,128)(2,1)} %get-tuple-element.31.refs_0_), channel_id=1, source_target_pairs={{0,2},{1,3},{2,4},{3,5},{4,6},{5,7},{8,10},{9,11},{10,12},{11,13},... | collective-permute-start | bytes 405512 | tf_op jit(solution)/shard_map/ppermute | solution.py:320
  15.2 0.0 collective-permute-done.3.refs_4_
  15.2 1.9 %collective-permute-start = (bf16[528,128]{1,0:T(8,128)(2,1)}, bf16[528,128]{1,0:T(8,128)(2,1)S(1)}, u32[]{:S(2)}, u32[]{:S(2)}) collective-permute-start(bf16[528,128]{1,0:T(8,128)(2,1)} %get-tuple-element.30.refs_0_), channel_id=1, source_target_pairs={{0,2},{1,3},{2,4},{3,5},{4,6},{5,7},{8,10},{9,11},{10,12},{11,13},... | collective-permute-start | bytes 405512 | tf_op jit(solution)/shard_map/ppermute | solution.py:320
  17.1 0.0 collective-permute-done.1.refs_2_
  17.1 7.6 %collective-permute-start.9 = (bf16[528,128]{1,0:T(8,128)(2,1)}, bf16[528,128]{1,0:T(8,128)(2,1)S(1)}, u32[]{:S(2)}, u32[]{:S(2)}) collective-permute-start(bf16[528,128]{1,0:T(8,128)(2,1)} %get-tuple-element.31.refs_0_), channel_id=1, source_target_pairs={{0,6},{1,7},{8,14},{9,15},{16,22},{17,23},{24,30},{25,31}} | collective-permute-start | bytes 405512 | tf_op jit(solution)/shard_map/ppermute | solution.py:320
  24.7 1.3 %collective-permute-start.13 = (bf16[528,128]{1,0:T(8,128)(2,1)S(1)}, bf16[528,128]{1,0:T(8,128)(2,1)S(1)}, u32[]{:S(2)}, u32[]{:S(2)}) collective-permute-start(bf16[528,128]{1,0:T(8,128)(2,1)S(1)} %collective-permute-done.10.refs_4_), channel_id=1, source_target_pairs={{0,6},{1,7},{8,14},{9,15},{16,22},{17,23},{24,30},{25,31}} | collective-permute-start | bytes 405512 | tf_op jit(solution)/shard_map/ppermute | solution.py:320
  26.1 0.0 collective-permute-done.8.refs_2_
  26.1 0.6 collective-permute-start.12
  26.6 0.0 collective-permute-done.7.refs_1_
  26.6 1.5 %collective-permute-start.11 = (bf16[528,128]{1,0:T(8,128)(2,1)S(1)}, bf16[528,128]{1,0:T(8,128)(2,1)S(1)}, u32[]{:S(2)}, u32[]{:S(2)}) collective-permute-start(bf16[528,128]{1,0:T(8,128)(2,1)S(1)} %collective-permute-done.7.refs_1_), channel_id=1, source_target_pairs={{0,1},{1,0},{2,3},{3,2},{4,5},{5,4},{6,7},{7,6},{8,9},{9,8},{10,11... | collective-permute-start | bytes 405512 | tf_op jit(solution)/shard_map/ppermute | solution.py:326
  28.2 1.5 %collective-permute-start.2 = (bf16[528,128]{1,0:T(8,128)(2,1)}, bf16[528,128]{1,0:T(8,128)(2,1)S(1)}, u32[]{:S(2)}, u32[]{:S(2)}) collective-permute-start(bf16[528,128]{1,0:T(8,128)(2,1)} %get-tuple-element.30.refs_0_), channel_id=1, source_target_pairs={{0,6},{1,7},{8,14},{9,15},{16,22},{17,23},{24,30},{25,31}} | collective-permute-start | bytes 405512 | tf_op jit(solution)/shard_map/ppermute | solution.py:320
  29.7 5.5 %collective-permute-start.6 = (bf16[528,128]{1,0:T(8,128)(2,1)S(1)}, bf16[528,128]{1,0:T(8,128)(2,1)S(1)}, u32[]{:S(2)}, u32[]{:S(2)}) collective-permute-start(bf16[528,128]{1,0:T(8,128)(2,1)S(1)} %collective-permute-done.3.refs_4_), channel_id=1, source_target_pairs={{0,6},{1,7},{8,14},{9,15},{16,22},{17,23},{24,30},{25,31}} | collective-permute-start | bytes 405512 | tf_op jit(solution)/shard_map/ppermute | solution.py:320
  35.2 0.6 collective-permute-start.5
  35.7 1.5 %collective-permute-start.4 = (bf16[528,128]{1,0:T(8,128)(2,1)S(1)}, bf16[528,128]{1,0:T(8,128)(2,1)S(1)}, u32[]{:S(2)}, u32[]{:S(2)}) collective-permute-start(bf16[528,128]{1,0:T(8,128)(2,1)S(1)} %collective-permute-done.refs_1_), channel_id=1, source_target_pairs={{0,1},{1,0},{2,3},{3,2},{4,5},{5,4},{6,7},{7,6},{8,9},{9,8},{10,11... | collective-permute-start | bytes 405512 | tf_op jit(solution)/shard_map/ppermute | solution.py:326
  37.3 0.7 copy-done.2
  37.9 1.2 %copy-done.3 = bf16[1,128,4096]{2,1,0:T(8,128)(2,1)S(1)} copy-done((bf16[1,128,4096]{2,1,0:T(8,128)(2,1)S(1)}, bf16[1,128,4096]{2,1,0:T(8,128)(2,1)}, u32[]{:S(2)}) %copy-start.3) | copy-done | bytes 1048600
  39.1 1.2 %copy-done.5 = bf16[1,128,4096]{2,1,0:T(8,128)(2,1)S(1)} copy-done((bf16[1,128,4096]{2,1,0:T(8,128)(2,1)S(1)}, bf16[1,128,4096]{2,1,0:T(8,128)(2,1)}, u32[]{:S(2)}) %copy-start.5) | copy-done | bytes 1048600
  40.4 0.9 copy-done.8
  41.3 9.3 %shard_map.85 = (bf16[1,128,4096]{2,1,0:T(8,128)(2,1)}, f32[1,128,4096]{2,1,0:T(8,128)}, f32[1,512,128]{2,1,0:T(8,128)S(1)}, f32[1,512,128]{2,1,0:T(8,128)S(1)},...) custom-call(s32[1]{0:T(128)} %bitcast.here_ref, ...), custom_call_target="tpu_custom_call" | custom-call | flops 6442450944 | bytes 8388608 | tf_op jit(solution)/shard_map/pallas_call | solution.py:251
  50.6 0.7 copy-done
  51.3 0.5 collective-permute-start.15
  51.8 9.4 %shard_map.86 = (bf16[1,128,4096]{2,1,0:T(8,128)(2,1)}, f32[1,128,4096]{2,1,0:T(8,128)}, f32[1,512,128]{2,1,0:T(8,128)S(1)}, f32[1,512,128]{2,1,0:T(8,128)S(1)},...) custom-call(s32[1]{0:T(128)} %bitcast.here_ref, ...), custom_call_target="tpu_custom_call", output_to_operand_aliasing={{0}: (12, {}), {1}: (13, {})} | custom-call | flops 6442450944 | bytes 8388608 | tf_op jit(solution)/shard_map/pallas_call | solution.py:251
  61.3 0.7 copy-done.1
  62.0 1.5 %collective-permute-start.21 = (bf16[2,512,128]{2,1,0:T(8,128)(2,1)S(1)}, bf16[2,512,128]{2,1,0:T(8,128)(2,1)S(1)}, u32[]{:S(2)}, u32[]{:S(2)}) collective-permute-start(bf16[2,512,128]{2,1,0:T(8,128)(2,1)S(1)} %get-tuple-element.48), channel_id=1, source_target_pairs={{0,1},{1,0},{2,3},{3,2},{4,5},{5,4},{6,7},{7,6},{8,9},{9,8},{10,11... | collective-permute-start | bytes 786440 | tf_op jit(solution)/shard_map/ppermute | solution.py:326
  63.5 1.3 %collective-permute-start.16 = (bf16[1,512,128]{2,1,0:T(8,128)(2,1)S(1)}, bf16[1,512,128]{2,1,0:T(8,128)(2,1)S(1)}, u32[]{:S(2)}, u32[]{:S(2)}) collective-permute-start(bf16[1,512,128]{2,1,0:T(8,128)(2,1)S(1)} %get-tuple-element.41), channel_id=1, source_target_pairs={{6,0},{7,1},{14,8},{15,9},{22,16},{23,17},{30,24},{31,25}} | collective-permute-start | bytes 393224 | tf_op jit(solution)/shard_map/ppermute | solution.py:323
  64.8 1.3 %collective-permute-start.22 = (bf16[1,512,128]{2,1,0:T(8,128)(2,1)S(1)}, bf16[1,512,128]{2,1,0:T(8,128)(2,1)S(1)}, u32[]{:S(2)}, u32[]{:S(2)}) collective-permute-start(bf16[1,512,128]{2,1,0:T(8,128)(2,1)S(1)} %get-tuple-element.50), channel_id=1, source_target_pairs={{6,0},{7,1},{14,8},{15,9},{22,16},{23,17},{30,24},{31,25}} | collective-permute-start | bytes 393224 | tf_op jit(solution)/shard_map/ppermute | solution.py:323
  66.1 1.3 %collective-permute-start.14 = (bf16[1,512,128]{2,1,0:T(8,128)(2,1)S(1)}, bf16[1,512,128]{2,1,0:T(8,128)(2,1)S(1)}, u32[]{:S(2)}, u32[]{:S(2)}) collective-permute-start(bf16[1,512,128]{2,1,0:T(8,128)(2,1)S(1)} %get-tuple-element.37), channel_id=1, source_target_pairs={{6,0},{7,1},{14,8},{15,9},{22,16},{23,17},{30,24},{31,25}} | collective-permute-start | bytes 393224 | tf_op jit(solution)/shard_map/ppermute | solution.py:323
  67.4 4.8 %collective-permute-done.16.last_ref = bf16[1,512,128]{2,1,0:T(8,128)(2,1)S(1)} collective-permute-done((bf16[1,512,128]{2,1,0:T(8,128)(2,1)S(1)}, bf16[1,512,128]{2,1,0:T(8,128)(2,1)S(1)}, u32[]{:S(2)}, u32[]{:S(2)}) %collective-permute-start.16) | collective-permute-done | bytes 131104 | tf_op jit(solution)/shard_map/ppermute | solution.py:323
  72.1 1.3 %collective-permute-start.20 = (bf16[1,512,128]{2,1,0:T(8,128)(2,1)S(1)}, bf16[1,512,128]{2,1,0:T(8,128)(2,1)S(1)}, u32[]{:S(2)}, u32[]{:S(2)}) collective-permute-start(bf16[1,512,128]{2,1,0:T(8,128)(2,1)S(1)} %get-tuple-element.46), channel_id=1, source_target_pairs={{6,0},{7,1},{14,8},{15,9},{22,16},{23,17},{30,24},{31,25}} | collective-permute-start | bytes 393224 | tf_op jit(solution)/shard_map/ppermute | solution.py:323
  73.4 0.1 shard_map.87
  73.5 0.6 collective-permute-start.17
  74.1 1.3 %collective-permute-start.18 = (bf16[512,128]{1,0:T(8,128)(2,1)S(1)}, bf16[512,128]{1,0:T(8,128)(2,1)S(1)}, u32[]{:S(2)}, u32[]{:S(2)}) collective-permute-start(bf16[512,128]{1,0:T(8,128)(2,1)S(1)} %get-tuple-element.43), channel_id=1, source_target_pairs={{2,0},{3,1},{4,2},{5,3},{6,4},{7,5},{10,8},{11,9},{12,10},{13,11},... | collective-permute-start | bytes 393224 | tf_op jit(solution)/shard_map/ppermute | solution.py:323
  75.4 1.3 %collective-permute-start.19 = (bf16[512,128]{1,0:T(8,128)(2,1)S(1)}, bf16[512,128]{1,0:T(8,128)(2,1)S(1)}, u32[]{:S(2)}, u32[]{:S(2)}) collective-permute-start(bf16[512,128]{1,0:T(8,128)(2,1)S(1)} %get-tuple-element.44), channel_id=1, source_target_pairs={{4,0},{5,1},{6,2},{7,3},{12,8},{13,9},{14,10},{15,11},{20,16},{21,... | collective-permute-start | bytes 393224 | tf_op jit(solution)/shard_map/ppermute | solution.py:323
  76.7 0.1 shard_map.88
  76.8 1.6 %collective-permute-start.23 = (bf16[512,128]{1,0:T(8,128)(2,1)S(1)}, bf16[512,128]{1,0:T(8,128)(2,1)S(1)}, u32[]{:S(2)}, u32[]{:S(2)}) collective-permute-start(bf16[512,128]{1,0:T(8,128)(2,1)S(1)} %get-tuple-element.51), channel_id=1, source_target_pairs={{0,1},{1,0},{2,3},{3,2},{4,5},{5,4},{6,7},{7,6},{8,9},{9,8},{10,11... | collective-permute-start | bytes 393224 | tf_op jit(solution)/shard_map/ppermute | solution.py:326
  78.4 3.7 %collective-permute-done.20.refs_6_ = bf16[1,512,128]{2,1,0:T(8,128)(2,1)S(1)} collective-permute-done((bf16[1,512,128]{2,1,0:T(8,128)(2,1)S(1)}, bf16[1,512,128]{2,1,0:T(8,128)(2,1)S(1)}, u32[]{:S(2)}, u32[]{:S(2)}) %collective-permute-start.20) | collective-permute-done | bytes 131104 | tf_op jit(solution)/shard_map/ppermute | solution.py:323
  82.1 1.3 %collective-permute-start.24 = (bf16[512,128]{1,0:T(8,128)(2,1)S(1)}, bf16[512,128]{1,0:T(8,128)(2,1)S(1)}, u32[]{:S(2)}, u32[]{:S(2)}) collective-permute-start(bf16[512,128]{1,0:T(8,128)(2,1)S(1)} %get-tuple-element.52), channel_id=1, source_target_pairs={{2,0},{3,1},{4,2},{5,3},{6,4},{7,5},{10,8},{11,9},{12,10},{13,11},... | collective-permute-start | bytes 393224 | tf_op jit(solution)/shard_map/ppermute | solution.py:323
  83.4 1.3 %collective-permute-start.25 = (bf16[512,128]{1,0:T(8,128)(2,1)S(1)}, bf16[512,128]{1,0:T(8,128)(2,1)S(1)}, u32[]{:S(2)}, u32[]{:S(2)}) collective-permute-start(bf16[512,128]{1,0:T(8,128)(2,1)S(1)} %get-tuple-element.53), channel_id=1, source_target_pairs={{4,0},{5,1},{6,2},{7,3},{12,8},{13,9},{14,10},{15,11},{20,16},{21,... | collective-permute-start | bytes 393224 | tf_op jit(solution)/shard_map/ppermute | solution.py:323
  84.7 5.1 %collective-permute-done.19.refs_4_ = bf16[512,128]{1,0:T(8,128)(2,1)S(1)} collective-permute-done((bf16[512,128]{1,0:T(8,128)(2,1)S(1)}, bf16[512,128]{1,0:T(8,128)(2,1)S(1)}, u32[]{:S(2)}, u32[]{:S(2)}) %collective-permute-start.19) | collective-permute-done | bytes 131104 | tf_op jit(solution)/shard_map/ppermute | solution.py:323
  89.8 1.1 %collective-permute-done.24.refs_8_ = bf16[512,128]{1,0:T(8,128)(2,1)S(1)} collective-permute-done((bf16[512,128]{1,0:T(8,128)(2,1)S(1)}, bf16[512,128]{1,0:T(8,128)(2,1)S(1)}, u32[]{:S(2)}, u32[]{:S(2)}) %collective-permute-start.24) | collective-permute-done | bytes 131104 | tf_op jit(solution)/shard_map/ppermute | solution.py:323
  90.9 4.0 %collective-permute-done.25.refs_9_ = bf16[512,128]{1,0:T(8,128)(2,1)S(1)} collective-permute-done((bf16[512,128]{1,0:T(8,128)(2,1)S(1)}, bf16[512,128]{1,0:T(8,128)(2,1)S(1)}, u32[]{:S(2)}, u32[]{:S(2)}) %collective-permute-start.25) | collective-permute-done | bytes 131104 | tf_op jit(solution)/shard_map/ppermute | solution.py:323
  94.9 0.6 copy-done.16
  95.5 2.3 %shard_map.89 = (f32[1,128,512]{2,1,0:T(8,128)}, f32[1,128,512]{2,1,0:T(8,128)}) custom-call(f32[1,512,128]{2,1,0:T(8,128)} %copy-done, bf16[1,512,128]{2,1,0:T(8,128)(2,1)} %copy-done.9, bf16[512,128]{1,0:T(8,128)(2,1)} %copy-done.11, bf16[512,128]{1,0:T(8,128)(2,1)} %copy-done.12, bf16[512,128]{1,0:T(8,128)(2,1)} %copy-done.13, f32[1,512,128]{2,1,0:T(8,128)} %copy-done.1, ...), custom_call_target="tpu_custom_call" | custom-call | tf_op jit(solution)/shard_map/pallas_call | solution.py:349
  (44 shorter events, 0.1 us)
Async XLA Ops:
  2.3 12.8 %collective-permute-start.3 = (bf16[528,128]{1,0:T(8,128)(2,1)}, bf16[528,128]{1,0:T(8,128)(2,1)S(1)}, u32[]{:S(2)}, u32[]{:S(2)}) collective-permute-start(bf16[528,128]{1,0:T(8,128)(2,1)} %get-tuple-element.30.refs_0_), channel_id=1, source_target_pairs={{0,1},{1,0},{2,3},{3,2},{4,5},{5,4},{6,7},{7,6},{8,9},{9,8},{10,11... | collective-permute-start | bytes 405512 | tf_op jit(solution)/shard_map/ppermute | solution.py:326
  5.3 11.8 %collective-permute-start.1 = (bf16[528,128]{1,0:T(8,128)(2,1)}, bf16[528,128]{1,0:T(8,128)(2,1)S(1)}, u32[]{:S(2)}, u32[]{:S(2)}) collective-permute-start(bf16[528,128]{1,0:T(8,128)(2,1)} %get-tuple-element.30.refs_0_), channel_id=1, source_target_pairs={{0,4},{1,5},{2,6},{3,7},{8,12},{9,13},{10,14},{11,15},{16,20},{17,... | collective-permute-start | bytes 405512 | tf_op jit(solution)/shard_map/ppermute | solution.py:320
  9.8 14.9 %collective-permute-start.10 = (bf16[528,128]{1,0:T(8,128)(2,1)}, bf16[528,128]{1,0:T(8,128)(2,1)S(1)}, u32[]{:S(2)}, u32[]{:S(2)}) collective-permute-start(bf16[528,128]{1,0:T(8,128)(2,1)} %get-tuple-element.31.refs_0_), channel_id=1, source_target_pairs={{0,1},{1,0},{2,3},{3,2},{4,5},{5,4},{6,7},{7,6},{8,9},{9,8},{10,11... | collective-permute-start | bytes 405512 | tf_op jit(solution)/shard_map/ppermute | solution.py:326
  10.4 15.7 %collective-permute-start.8 = (bf16[528,128]{1,0:T(8,128)(2,1)}, bf16[528,128]{1,0:T(8,128)(2,1)S(1)}, u32[]{:S(2)}, u32[]{:S(2)}) collective-permute-start(bf16[528,128]{1,0:T(8,128)(2,1)} %get-tuple-element.31.refs_0_), channel_id=1, source_target_pairs={{0,4},{1,5},{2,6},{3,7},{8,12},{9,13},{10,14},{11,15},{16,20},{17,... | collective-permute-start | bytes 405512 | tf_op jit(solution)/shard_map/ppermute | solution.py:320
  11.7 15.0 %collective-permute-start.7 = (bf16[528,128]{1,0:T(8,128)(2,1)}, bf16[528,128]{1,0:T(8,128)(2,1)S(1)}, u32[]{:S(2)}, u32[]{:S(2)}) collective-permute-start(bf16[528,128]{1,0:T(8,128)(2,1)} %get-tuple-element.31.refs_0_), channel_id=1, source_target_pairs={{0,2},{1,3},{2,4},{3,5},{4,6},{5,7},{8,10},{9,11},{10,12},{11,13},... | collective-permute-start | bytes 405512 | tf_op jit(solution)/shard_map/ppermute | solution.py:320
  15.2 13.0 %collective-permute-start = (bf16[528,128]{1,0:T(8,128)(2,1)}, bf16[528,128]{1,0:T(8,128)(2,1)S(1)}, u32[]{:S(2)}, u32[]{:S(2)}) collective-permute-start(bf16[528,128]{1,0:T(8,128)(2,1)} %get-tuple-element.30.refs_0_), channel_id=1, source_target_pairs={{0,2},{1,3},{2,4},{3,5},{4,6},{5,7},{8,10},{9,11},{10,12},{11,13},... | collective-permute-start | bytes 405512 | tf_op jit(solution)/shard_map/ppermute | solution.py:320
  17.1 12.6 %collective-permute-start.9 = (bf16[528,128]{1,0:T(8,128)(2,1)}, bf16[528,128]{1,0:T(8,128)(2,1)S(1)}, u32[]{:S(2)}, u32[]{:S(2)}) collective-permute-start(bf16[528,128]{1,0:T(8,128)(2,1)} %get-tuple-element.31.refs_0_), channel_id=1, source_target_pairs={{0,6},{1,7},{8,14},{9,15},{16,22},{17,23},{24,30},{25,31}} | collective-permute-start | bytes 405512 | tf_op jit(solution)/shard_map/ppermute | solution.py:320
  24.7 10.4 %collective-permute-start.13 = (bf16[528,128]{1,0:T(8,128)(2,1)S(1)}, bf16[528,128]{1,0:T(8,128)(2,1)S(1)}, u32[]{:S(2)}, u32[]{:S(2)}) collective-permute-start(bf16[528,128]{1,0:T(8,128)(2,1)S(1)} %collective-permute-done.10.refs_4_), channel_id=1, source_target_pairs={{0,6},{1,7},{8,14},{9,15},{16,22},{17,23},{24,30},{25,31}} | collective-permute-start | bytes 405512 | tf_op jit(solution)/shard_map/ppermute | solution.py:320
  26.1 9.7 %collective-permute-start.12 = (bf16[528,128]{1,0:T(8,128)(2,1)S(1)}, bf16[528,128]{1,0:T(8,128)(2,1)S(1)}, u32[]{:S(2)}, u32[]{:S(2)}) collective-permute-start(bf16[528,128]{1,0:T(8,128)(2,1)S(1)} %collective-permute-done.8.refs_2_), channel_id=1, source_target_pairs={{0,1},{1,0},{2,3},{3,2},{4,5},{5,4},{6,7},{7,6},{8,9},{9,8},{10,11... | collective-permute-start | bytes 405512 | tf_op jit(solution)/shard_map/ppermute | solution.py:326
  26.6 10.6 %collective-permute-start.11 = (bf16[528,128]{1,0:T(8,128)(2,1)S(1)}, bf16[528,128]{1,0:T(8,128)(2,1)S(1)}, u32[]{:S(2)}, u32[]{:S(2)}) collective-permute-start(bf16[528,128]{1,0:T(8,128)(2,1)S(1)} %collective-permute-done.7.refs_1_), channel_id=1, source_target_pairs={{0,1},{1,0},{2,3},{3,2},{4,5},{5,4},{6,7},{7,6},{8,9},{9,8},{10,11... | collective-permute-start | bytes 405512 | tf_op jit(solution)/shard_map/ppermute | solution.py:326
  28.2 23.6 %collective-permute-start.2 = (bf16[528,128]{1,0:T(8,128)(2,1)}, bf16[528,128]{1,0:T(8,128)(2,1)S(1)}, u32[]{:S(2)}, u32[]{:S(2)}) collective-permute-start(bf16[528,128]{1,0:T(8,128)(2,1)} %get-tuple-element.30.refs_0_), channel_id=1, source_target_pairs={{0,6},{1,7},{8,14},{9,15},{16,22},{17,23},{24,30},{25,31}} | collective-permute-start | bytes 405512 | tf_op jit(solution)/shard_map/ppermute | solution.py:320
  29.7 22.1 %collective-permute-start.6 = (bf16[528,128]{1,0:T(8,128)(2,1)S(1)}, bf16[528,128]{1,0:T(8,128)(2,1)S(1)}, u32[]{:S(2)}, u32[]{:S(2)}) collective-permute-start(bf16[528,128]{1,0:T(8,128)(2,1)S(1)} %collective-permute-done.3.refs_4_), channel_id=1, source_target_pairs={{0,6},{1,7},{8,14},{9,15},{16,22},{17,23},{24,30},{25,31}} | collective-permute-start | bytes 405512 | tf_op jit(solution)/shard_map/ppermute | solution.py:320
  35.2 16.6 %collective-permute-start.5 = (bf16[528,128]{1,0:T(8,128)(2,1)S(1)}, bf16[528,128]{1,0:T(8,128)(2,1)S(1)}, u32[]{:S(2)}, u32[]{:S(2)}) collective-permute-start(bf16[528,128]{1,0:T(8,128)(2,1)S(1)} %collective-permute-done.1.refs_2_), channel_id=1, source_target_pairs={{0,1},{1,0},{2,3},{3,2},{4,5},{5,4},{6,7},{7,6},{8,9},{9,8},{10,11... | collective-permute-start | bytes 405512 | tf_op jit(solution)/shard_map/ppermute | solution.py:326
  35.7 16.0 %collective-permute-start.4 = (bf16[528,128]{1,0:T(8,128)(2,1)S(1)}, bf16[528,128]{1,0:T(8,128)(2,1)S(1)}, u32[]{:S(2)}, u32[]{:S(2)}) collective-permute-start(bf16[528,128]{1,0:T(8,128)(2,1)S(1)} %collective-permute-done.refs_1_), channel_id=1, source_target_pairs={{0,1},{1,0},{2,3},{3,2},{4,5},{5,4},{6,7},{7,6},{8,9},{9,8},{10,11... | collective-permute-start | bytes 405512 | tf_op jit(solution)/shard_map/ppermute | solution.py:326
  37.3 0.7 copy-start.2
  37.9 1.2 %copy-start.3 = (bf16[1,128,4096]{2,1,0:T(8,128)(2,1)S(1)}, bf16[1,128,4096]{2,1,0:T(8,128)(2,1)}, u32[]{:S(2)}) copy-start(bf16[1,128,4096]{2,1,0:T(8,128)(2,1)} %refs_8_.3) | copy-start | bytes 3145732
  39.1 1.2 %copy-start.5 = (bf16[1,128,4096]{2,1,0:T(8,128)(2,1)S(1)}, bf16[1,128,4096]{2,1,0:T(8,128)(2,1)}, u32[]{:S(2)}) copy-start(bf16[1,128,4096]{2,1,0:T(8,128)(2,1)} %refs_9_.3) | copy-start | bytes 3145732
  40.4 0.9 copy-start.8
  41.3 10.5 %copy-start.4 = (bf16[1,128,4096]{2,1,0:T(8,128)(2,1)S(1)}, bf16[1,128,4096]{2,1,0:T(8,128)(2,1)}, u32[]{:S(2)}) copy-start(bf16[1,128,4096]{2,1,0:T(8,128)(2,1)} %refs_8_.3) | copy-start | bytes 3145732
  41.3 10.5 %copy-start.6 = (bf16[1,128,4096]{2,1,0:T(8,128)(2,1)S(1)}, bf16[1,128,4096]{2,1,0:T(8,128)(2,1)}, u32[]{:S(2)}) copy-start(bf16[1,128,4096]{2,1,0:T(8,128)(2,1)} %refs_9_.3) | copy-start | bytes 3145732
  41.3 10.5 %copy-start.7 = (bf16[528,128]{1,0:T(8,128)(2,1)S(1)}, bf16[528,128]{1,0:T(8,128)(2,1)}, u32[]{:S(2)}) copy-start(bf16[528,128]{1,0:T(8,128)(2,1)} %get-tuple-element.30.refs_0_) | copy-start | bytes 405508
  50.6 0.7 copy-start
  51.3 22.2 %collective-permute-start.15 = (bf16[2,512,128]{2,1,0:T(8,128)(2,1)S(1)}, bf16[2,512,128]{2,1,0:T(8,128)(2,1)S(1)}, u32[]{:S(2)}, u32[]{:S(2)}) collective-permute-start(bf16[2,512,128]{2,1,0:T(8,128)(2,1)S(1)} %get-tuple-element.39), channel_id=1, source_target_pairs={{0,1},{1,0},{2,3},{3,2},{4,5},{5,4},{6,7},{7,6},{8,9},{9,8},{10,11... | collective-permute-start | bytes 786440 | tf_op jit(solution)/shard_map/ppermute | solution.py:326
  61.2 0.7 copy-start.1
  62.0 13.4 %collective-permute-start.21 = (bf16[2,512,128]{2,1,0:T(8,128)(2,1)S(1)}, bf16[2,512,128]{2,1,0:T(8,128)(2,1)S(1)}, u32[]{:S(2)}, u32[]{:S(2)}) collective-permute-start(bf16[2,512,128]{2,1,0:T(8,128)(2,1)S(1)} %get-tuple-element.48), channel_id=1, source_target_pairs={{0,1},{1,0},{2,3},{3,2},{4,5},{5,4},{6,7},{7,6},{8,9},{9,8},{10,11... | collective-permute-start | bytes 786440 | tf_op jit(solution)/shard_map/ppermute | solution.py:326
  63.5 8.6 %collective-permute-start.16 = (bf16[1,512,128]{2,1,0:T(8,128)(2,1)S(1)}, bf16[1,512,128]{2,1,0:T(8,128)(2,1)S(1)}, u32[]{:S(2)}, u32[]{:S(2)}) collective-permute-start(bf16[1,512,128]{2,1,0:T(8,128)(2,1)S(1)} %get-tuple-element.41), channel_id=1, source_target_pairs={{6,0},{7,1},{14,8},{15,9},{22,16},{23,17},{30,24},{31,25}} | collective-permute-start | bytes 393224 | tf_op jit(solution)/shard_map/ppermute | solution.py:323
  64.8 9.3 %collective-permute-start.22 = (bf16[1,512,128]{2,1,0:T(8,128)(2,1)S(1)}, bf16[1,512,128]{2,1,0:T(8,128)(2,1)S(1)}, u32[]{:S(2)}, u32[]{:S(2)}) collective-permute-start(bf16[1,512,128]{2,1,0:T(8,128)(2,1)S(1)} %get-tuple-element.50), channel_id=1, source_target_pairs={{6,0},{7,1},{14,8},{15,9},{22,16},{23,17},{30,24},{31,25}} | collective-permute-start | bytes 393224 | tf_op jit(solution)/shard_map/ppermute | solution.py:323
  66.1 10.7 %collective-permute-start.14 = (bf16[1,512,128]{2,1,0:T(8,128)(2,1)S(1)}, bf16[1,512,128]{2,1,0:T(8,128)(2,1)S(1)}, u32[]{:S(2)}, u32[]{:S(2)}) collective-permute-start(bf16[1,512,128]{2,1,0:T(8,128)(2,1)S(1)} %get-tuple-element.37), channel_id=1, source_target_pairs={{6,0},{7,1},{14,8},{15,9},{22,16},{23,17},{30,24},{31,25}} | collective-permute-start | bytes 393224 | tf_op jit(solution)/shard_map/ppermute | solution.py:323
  72.1 9.9 %collective-permute-start.20 = (bf16[1,512,128]{2,1,0:T(8,128)(2,1)S(1)}, bf16[1,512,128]{2,1,0:T(8,128)(2,1)S(1)}, u32[]{:S(2)}, u32[]{:S(2)}) collective-permute-start(bf16[1,512,128]{2,1,0:T(8,128)(2,1)S(1)} %get-tuple-element.46), channel_id=1, source_target_pairs={{6,0},{7,1},{14,8},{15,9},{22,16},{23,17},{30,24},{31,25}} | collective-permute-start | bytes 393224 | tf_op jit(solution)/shard_map/ppermute | solution.py:323
  73.5 9.8 %collective-permute-start.17 = (bf16[512,128]{1,0:T(8,128)(2,1)S(1)}, bf16[512,128]{1,0:T(8,128)(2,1)S(1)}, u32[]{:S(2)}, u32[]{:S(2)}) collective-permute-start(bf16[512,128]{1,0:T(8,128)(2,1)S(1)} %get-tuple-element.42), channel_id=1, source_target_pairs={{0,1},{1,0},{2,3},{3,2},{4,5},{5,4},{6,7},{7,6},{8,9},{9,8},{10,11... | collective-permute-start | bytes 393224 | tf_op jit(solution)/shard_map/ppermute | solution.py:326
  74.1 10.6 %collective-permute-start.18 = (bf16[512,128]{1,0:T(8,128)(2,1)S(1)}, bf16[512,128]{1,0:T(8,128)(2,1)S(1)}, u32[]{:S(2)}, u32[]{:S(2)}) collective-permute-start(bf16[512,128]{1,0:T(8,128)(2,1)S(1)} %get-tuple-element.43), channel_id=1, source_target_pairs={{2,0},{3,1},{4,2},{5,3},{6,4},{7,5},{10,8},{11,9},{12,10},{13,11},... | collective-permute-start | bytes 393224 | tf_op jit(solution)/shard_map/ppermute | solution.py:323
  75.4 14.4 %collective-permute-start.19 = (bf16[512,128]{1,0:T(8,128)(2,1)S(1)}, bf16[512,128]{1,0:T(8,128)(2,1)S(1)}, u32[]{:S(2)}, u32[]{:S(2)}) collective-permute-start(bf16[512,128]{1,0:T(8,128)(2,1)S(1)} %get-tuple-element.44), channel_id=1, source_target_pairs={{4,0},{5,1},{6,2},{7,3},{12,8},{13,9},{14,10},{15,11},{20,16},{21,... | collective-permute-start | bytes 393224 | tf_op jit(solution)/shard_map/ppermute | solution.py:323
  76.8 18.1 %copy-start.9 = (bf16[1,512,128]{2,1,0:T(8,128)(2,1)}, bf16[1,512,128]{2,1,0:T(8,128)(2,1)S(1)}, u32[]{:S(2)}) copy-start(bf16[1,512,128]{2,1,0:T(8,128)(2,1)S(1)} %collective-permute-done.14.refs_1_) | copy-start | bytes 393220
  76.8 13.0 %collective-permute-start.23 = (bf16[512,128]{1,0:T(8,128)(2,1)S(1)}, bf16[512,128]{1,0:T(8,128)(2,1)S(1)}, u32[]{:S(2)}, u32[]{:S(2)}) collective-permute-start(bf16[512,128]{1,0:T(8,128)(2,1)S(1)} %get-tuple-element.51), channel_id=1, source_target_pairs={{0,1},{1,0},{2,3},{3,2},{4,5},{5,4},{6,7},{7,6},{8,9},{9,8},{10,11... | collective-permute-start | bytes 393224 | tf_op jit(solution)/shard_map/ppermute | solution.py:326
  82.1 12.8 %copy-start.10 = (bf16[1,512,128]{2,1,0:T(8,128)(2,1)}, bf16[1,512,128]{2,1,0:T(8,128)(2,1)S(1)}, u32[]{:S(2)}) copy-start(bf16[1,512,128]{2,1,0:T(8,128)(2,1)S(1)} %collective-permute-done.20.refs_6_) | copy-start | bytes 393220
  82.1 8.8 %collective-permute-start.24 = (bf16[512,128]{1,0:T(8,128)(2,1)S(1)}, bf16[512,128]{1,0:T(8,128)(2,1)S(1)}, u32[]{:S(2)}, u32[]{:S(2)}) collective-permute-start(bf16[512,128]{1,0:T(8,128)(2,1)S(1)} %get-tuple-element.52), channel_id=1, source_target_pairs={{2,0},{3,1},{4,2},{5,3},{6,4},{7,5},{10,8},{11,9},{12,10},{13,11},... | collective-permute-start | bytes 393224 | tf_op jit(solution)/shard_map/ppermute | solution.py:323
  83.4 11.5 %copy-start.11 = (bf16[512,128]{1,0:T(8,128)(2,1)}, bf16[512,128]{1,0:T(8,128)(2,1)S(1)}, u32[]{:S(2)}) copy-start(bf16[512,128]{1,0:T(8,128)(2,1)S(1)} %collective-permute-done.17.refs_2_) | copy-start | bytes 393220
  83.4 11.5 %collective-permute-start.25 = (bf16[512,128]{1,0:T(8,128)(2,1)S(1)}, bf16[512,128]{1,0:T(8,128)(2,1)S(1)}, u32[]{:S(2)}, u32[]{:S(2)}) collective-permute-start(bf16[512,128]{1,0:T(8,128)(2,1)S(1)} %get-tuple-element.53), channel_id=1, source_target_pairs={{4,0},{5,1},{6,2},{7,3},{12,8},{13,9},{14,10},{15,11},{20,16},{21,... | collective-permute-start | bytes 393224 | tf_op jit(solution)/shard_map/ppermute | solution.py:323
  84.7 10.2 %copy-start.12 = (bf16[512,128]{1,0:T(8,128)(2,1)}, bf16[512,128]{1,0:T(8,128)(2,1)S(1)}, u32[]{:S(2)}) copy-start(bf16[512,128]{1,0:T(8,128)(2,1)S(1)} %collective-permute-done.18.refs_3_) | copy-start | bytes 393220
  89.8 5.1 %copy-start.13 = (bf16[512,128]{1,0:T(8,128)(2,1)}, bf16[512,128]{1,0:T(8,128)(2,1)S(1)}, u32[]{:S(2)}) copy-start(bf16[512,128]{1,0:T(8,128)(2,1)S(1)} %collective-permute-done.19.refs_4_) | copy-start | bytes 393220
  89.8 5.1 %copy-start.14 = (bf16[512,128]{1,0:T(8,128)(2,1)}, bf16[512,128]{1,0:T(8,128)(2,1)S(1)}, u32[]{:S(2)}) copy-start(bf16[512,128]{1,0:T(8,128)(2,1)S(1)} %collective-permute-done.23.refs_7_) | copy-start | bytes 393220
  90.9 4.0 %copy-start.15 = (bf16[512,128]{1,0:T(8,128)(2,1)}, bf16[512,128]{1,0:T(8,128)(2,1)S(1)}, u32[]{:S(2)}) copy-start(bf16[512,128]{1,0:T(8,128)(2,1)S(1)} %collective-permute-done.24.refs_8_) | copy-start | bytes 393220
  94.9 0.7 copy-start.16

commit v3 on v2

--- a/solution.py
+++ b/solution.py
@@ -10,11 +10,20 @@
 
 KV = 4
 D = 128
-CHUNKS = 2
+SPLIT = (2, 2)
+WORK = (((0, 2),), ((0, 2),))
+VMEM = pl.BlockSpec(memory_space=pltpu.VMEM)
+HBM = pl.BlockSpec(memory_space=pl.ANY)
 BUNDLE = 4
 LANES = 256
 STEPS = 4
+ROUND = True
 NEG = -1e30
+TIE1 = 2
+TIE2 = True
+FETCH = True
+FULL = 57
+FWD = True
 NN = (((1,), (0,)), ((), ()))
 NT = (((1,), (1,)), ((), ()))
 TN = (((0,), (0,)), ((), ()))
@@ -24,16 +33,54 @@
     return lax.dot_general(a, b, dims, preferred_element_type=jnp.float32)
 
 
-def pack_kernel(k_ref, v_ref, s_ref, *outs):
+def pack_kernel(begin, per, k_ref, v_ref, s_ref, out, seg, sems):
     rows = k_ref.shape[1]
-    per = KV // len(outs)
-    seg = jnp.broadcast_to(s_ref[...].astype(jnp.float32), (16, rows)).astype(jnp.bfloat16)
-    for c, out in enumerate(outs):
-        for g in range(per):
-            cols = slice((c * per + g) * D, (c * per + g + 1) * D)
-            out[2 * g * rows : (2 * g + 1) * rows, :] = k_ref[0, :, cols]
-            out[(2 * g + 1) * rows : (2 * g + 2) * rows, :] = v_ref[0, :, cols]
-        out[2 * per * rows :, :] = seg
+    copies = [pltpu.make_async_copy(s_ref, seg, sems.at[0])]
+    for g in range(per):
+        for part, ref in enumerate((k_ref, v_ref)):
+            src = ref.at[0, :, pl.ds((begin + g) * D, D)]
+            to = out.at[pl.ds((2 * g + part) * rows, rows)]
+            copies.append(pltpu.make_async_copy(src, to, sems.at[1 + 2 * g + part]))
+    for copy in copies:
+        copy.start()
+    for copy in copies:
+        copy.wait()
+    row = jnp.broadcast_to(seg[...].astype(jnp.float32), (16, rows))
+    out[2 * per * rows :, :] = row.astype(jnp.bfloat16)
+
+
+def pack(begin, per, key_matrix, value_matrix, segment):
+    rows = key_matrix.shape[1]
+    return pl.pallas_call(
+        functools.partial(pack_kernel, begin, per),
+        in_specs=[HBM] * 3,
+        out_specs=VMEM,
+        out_shape=jax.ShapeDtypeStruct((per * 2 * rows + 16, D), jnp.bfloat16),
+        scratch_shapes=[
+            pltpu.VMEM(segment.shape, jnp.int32),
+            pltpu.SemaphoreType.DMA((2 * per + 1,)),
+        ],
+        compiler_params=pltpu.CompilerParams(vmem_limit_bytes=FULL << 20),
+    )(key_matrix, value_matrix, segment)
+
+
+def fetch_kernel(q_ref, c_ref, after_ref, q_out, c_out, sems):
+    copies = [pltpu.make_async_copy(q_ref, q_out, sems.at[0]), pltpu.make_async_copy(c_ref, c_out, sems.at[1])]
+    for copy in copies:
+        copy.start()
+    for copy in copies:
+        copy.wait()
+
+
+def fetch(queries, cotangent, after):
+    return pl.pallas_call(
+        fetch_kernel,
+        in_specs=[HBM, HBM, HBM],
+        out_specs=[VMEM, VMEM],
+        out_shape=[jax.ShapeDtypeStruct(queries.shape, queries.dtype)] * 2,
+        scratch_shapes=[pltpu.SemaphoreType.DMA((2,))],
+        compiler_params=pltpu.CompilerParams(vmem_limit_bytes=16 << 20),
+    )(queries, cotangent, after)
 
 
 def loop(count, body, start, pairs):
@@ -42,14 +89,16 @@
     return lax.fori_loop(0, count, body, start)
 
 
-def attend_kernel(pairs, per, chunk, lanes, has_prev, here_ref, *refs):
+def attend_kernel(pairs, begin, per, span_of_heads, lanes, prevs, here_ref, *refs):
     own = refs[:pairs]
     peer = refs[pairs : 2 * pairs]
     q_ref, c_ref, sq_ref = refs[2 * pairs : 2 * pairs + 3]
-    refs = refs[2 * pairs + 3 + (2 if has_prev else 0) :]
+    refs = refs[2 * pairs + 3 + prevs :]
+    low, high = span_of_heads
     out_ref, gq_ref = refs[:2]
-    parts = refs[2:8]
-    kv, mask, s_scr, p_scr, e_scr, probs_scr, slopes_scr, out_scr, gq_scr, cnt, order, sems = refs[8:]
+    parts = refs[2:7]
+    kv, mask, s_scr, p_scr, e_scr, probs_scr, slopes_scr, out_scr, gq_scr = refs[7:-3]
+    cnt, order, sems = refs[-3:]
     rows = q_ref.shape[1]
     heads = q_ref.shape[2] // KV // D
     each = heads * D
@@ -61,6 +110,9 @@
     power = scale * math.log2(math.e)
     here = here_ref[0]
 
+    def columns(g):
+        return pl.ds((begin + low + g) * each, each)
+
     seg_q = sq_ref[...].astype(jnp.float32)
     q_pos = here * rows + lax.broadcasted_iota(jnp.int32, (rows, rows), 1)
     local = lax.broadcasted_iota(jnp.int32, (rows, rows), 0)
@@ -83,9 +135,9 @@
         for lane, src in enumerate((own[k], peer[k])):
             to = pl.ds(pl.multiple_of(at + lane * rows, rows), rows)
             mask[to, :] = adds[lane]
-            for h in range(per):
+            for h in range(low, high):
                 for part in range(2):
-                    kv[h, part, to, :] = src[(2 * h + part) * rows : (2 * h + part + 1) * rows, :]
+                    kv[h - low, part, to, :] = src[(2 * h + part) * rows : (2 * h + part + 1) * rows, :]
 
     if static:
         for k in range(pairs):
@@ -104,24 +156,24 @@
         def blank(t, carry):
             at = pl.ds(pl.multiple_of(t * two, two), two)
             mask[at, :] = jnp.full((two, rows), NEG, jnp.float32)
-            kv[:, :, at, :] = jnp.zeros((per, 2, two, D), jnp.bfloat16)
+            kv[:, :, at, :] = jnp.zeros((high - low, 2, two, D), jnp.bfloat16)
             order[t] = -1
             return carry
 
         lax.fori_loop(cnt[0], pl.cdiv(cnt[0], BUNDLE) * BUNDLE, blank, 0)
         for ref in parts:
-            ref[...] = jnp.zeros_like(ref)
+            wipe = slice(low * two, high * two)
+            ref[:, wipe, :] = jnp.zeros((ref.shape[0], (high - low) * two, D), ref.dtype)
     bundles = None if static else pl.cdiv(cnt[0], BUNDLE)
     copies = []
 
     def send(src, ref, g, which):
-        to = ref.at[0, :, pl.ds((chunk * per + g) * each, each)]
-        copy = pltpu.make_async_copy(src.at[g], to, sems.at[2 * g + which])
+        copy = pltpu.make_async_copy(src.at[g], ref.at[0, :, columns(g)], sems.at[2 * g + which])
         copy.start()
         copies.append(copy)
 
     def stack(ref, g):
-        first = (chunk * per + g) * heads
+        first = (begin + low + g) * heads
         return jnp.concatenate([ref[0, :, (first + h) * D : (first + h + 1) * D] for h in range(heads)], axis=0)
 
     def tile(t, j):
@@ -134,7 +186,7 @@
     def one_head(g):
         q_all = stack(q_ref, g)
         c_all = stack(c_ref, g)
-        at = g * two
+        at = (low + g) * two
         for w in range(wide // lanes):
             cols = slice(w * lanes, (w + 1) * lanes)
             q_w, c_w = q_all[cols], c_all[cols]
@@ -198,7 +250,9 @@
                 grad_k = all_k[j * two : (j + 1) * two]
 
                 def keep(first, slot):
-                    for lane, ref in enumerate(parts[first : first + 2]):
+                    for lane in range(2):
+                        ref = parts[min(first + lane, 4)]
+                        slot = lane if first == 4 else slot
                         part = slice(lane * rows, (lane + 1) * rows)
                         ref[slot, pl.ds(at, rows), :] = grad_k[part].astype(ref.dtype)
                         ref[slot, pl.ds(at + rows, rows), :] = grad_v[part].astype(ref.dtype)
@@ -213,22 +267,20 @@
 
         loop(bundles, key_side, 0, pairs)
 
-    for g in range(per):
+    for g in range(high - low):
         one_head(g)
     for copy in copies:
         copy.wait()
 
 
-def attend(chunk, here, own, peer, queries, cotangent, segment, prev):
+def attend(begin, per, heads, here, own, peer, queries, cotangent, segment, prev, made):
     pairs = len(own)
-    per = KV // CHUNKS
+    count = heads[1] - heads[0]
     _, rows, width = queries.shape
     each = width // KV
     wide = each // D * rows
     lanes = wide if pairs <= BUNDLE else LANES
     keys = pl.cdiv(pairs, BUNDLE) * BUNDLE * 2 * rows
-    vmem = pl.BlockSpec(memory_space=pltpu.VMEM)
-    hbm = pl.BlockSpec(memory_space=pl.ANY)
     parts = [
         jax.ShapeDtypeStruct((count, per * 2 * rows, D), dtype)
         for count, dtype in (
@@ -236,40 +288,43 @@
             (1, jnp.float32),
             (pairs - 2, jnp.float32),
             (pairs - 2, jnp.bfloat16),
-            (1, jnp.bfloat16),
-            (1, jnp.bfloat16),
+            (2, jnp.bfloat16),
         )
     ]
     args = [here, *own, *peer, queries, cotangent, segment]
-    in_specs = [pl.BlockSpec(memory_space=pltpu.SMEM)] + [vmem] * (len(args) - 1)
+    in_specs = [pl.BlockSpec(memory_space=pltpu.SMEM)] + [VMEM] * (2 * pairs) + [VMEM] * 3
     aliases = {}
     if prev is not None:
-        aliases = {len(args): 0, len(args) + 1: 1}
+        aliases.update({len(args): 0, len(args) + 1: 1})
         args += list(prev)
-        in_specs += [hbm] * 2
-    macs = per * wide * 2 * rows * D * 6 * pairs
+        in_specs += [HBM] * 2
+    if made is not None:
+        aliases.update({len(args) + i: 2 + i for i in range(len(made))})
+        args += list(made)
+        in_specs += [VMEM] * len(made)
+    macs = count * wide * 2 * rows * D * 6 * pairs
     return pl.pallas_call(
-        functools.partial(attend_kernel, pairs, per, chunk, lanes, prev is not None),
+        functools.partial(attend_kernel, pairs, begin, per, heads, lanes, len(args) - 2 * pairs - 4),
         in_specs=in_specs,
-        out_specs=[hbm, hbm] + [vmem] * len(parts),
+        out_specs=[HBM, HBM] + [VMEM] * len(parts),
         out_shape=[
             jax.ShapeDtypeStruct(queries.shape, jnp.bfloat16),
             jax.ShapeDtypeStruct(queries.shape, jnp.float32),
             *parts,
         ],
         scratch_shapes=[
-            pltpu.VMEM((per, 2, keys, D), jnp.bfloat16),
+            pltpu.VMEM((count, 2, keys, D), jnp.bfloat16),
             pltpu.VMEM((keys, rows), jnp.float32),
             pltpu.VMEM((keys, lanes), jnp.float32),
             pltpu.VMEM((keys, lanes), jnp.float32),
             pltpu.VMEM((keys, lanes), jnp.bfloat16),
             pltpu.VMEM((keys, wide), jnp.bfloat16),
             pltpu.VMEM((keys, wide), jnp.bfloat16),
-            pltpu.VMEM((per, rows, each), jnp.bfloat16),
-            pltpu.VMEM((per, rows, each), jnp.float32),
+            pltpu.VMEM((count, rows, each), jnp.bfloat16),
+            pltpu.VMEM((count, rows, each), jnp.float32),
             pltpu.SMEM((1,), jnp.int32),
             pltpu.SMEM((pl.cdiv(pairs, BUNDLE) * BUNDLE,), jnp.int32),
-            pltpu.SemaphoreType.DMA((2 * per,)),
+            pltpu.SemaphoreType.DMA((2 * count,)),
         ],
         input_output_aliases=aliases,
         compiler_params=pltpu.CompilerParams(vmem_limit_bytes=(32 if pairs <= BUNDLE else 48) << 20),
@@ -278,7 +333,7 @@
 
 
 def add_kernel(mine_ref, got_ref, theirs_ref, last_ref, first_ref, *sends):
-    first_ref[...] = (theirs_ref[0] + last_ref[0].astype(jnp.float32)).astype(jnp.bfloat16)
+    first_ref[...] = (theirs_ref[0] + last_ref[1].astype(jnp.float32)).astype(jnp.bfloat16)
     for k, send in enumerate(sends):
         send[...] = (mine_ref[k] + got_ref[k].astype(jnp.float32)).astype(jnp.bfloat16)
 
@@ -287,6 +342,8 @@
     count, tall, _ = mine.shape
     return pl.pallas_call(
         add_kernel,
+        in_specs=[VMEM] * 4,
+        out_specs=[VMEM] * (count + 1),
         out_shape=[jax.ShapeDtypeStruct((tall, D), jnp.bfloat16)] * (count + 1),
         cost_estimate=pl.CostEstimate(flops=mine.size, bytes_accessed=8 * mine.size, transcendentals=0),
         compiler_params=pltpu.CompilerParams(vmem_limit_bytes=48 << 20),
@@ -297,11 +354,12 @@
     ins, (gk_ref, gv_ref) = refs[:-2], refs[-2:]
     rows = gk_ref.shape[1]
     each = pairs + 1
-    per = ins[0].shape[1] // (2 * rows)
+    head = 0
     for c in range(len(ins) // each):
         mine, last, *others = ins[c * each : (c + 1) * each]
-        for g in range(per):
-            cols = slice((c * per + g) * D, (c * per + g + 1) * D)
+        for g in range(mine.shape[1] // (2 * rows)):
+            cols = slice(head * D, (head + 1) * D)
+            head += 1
             for part, out in enumerate((gk_ref, gv_ref)):
                 span = slice((2 * g + part) * rows, (2 * g + part + 1) * rows)
                 total = mine[0, span, :] + last[0, span, :].astype(jnp.float32)
@@ -313,41 +371,81 @@
 def per_device(size, queries, key_matrix, value_matrix, cotangent, segment):
     rows = queries.shape[1]
     pairs = size // 2
-    per = KV // CHUNKS
     here = lax.axis_index("ctx").astype(jnp.int32).reshape(1)
 
     def up(x, k):
-        return lax.ppermute(x, "ctx", [(i, i + 2 * k) for i in range(size - 2 * k)])
+        return lax.ppermute(x, "ctx", [(i, (i + 2 * k) % size) for i in range(size if ROUND else size - 2 * k)])
 
     def down(x, k):
-        return lax.ppermute(x, "ctx", [(i + 2 * k, i) for i in range(size - 2 * k)])
+        return lax.ppermute(x, "ctx", [((i + 2 * k) % size, i) for i in range(size if ROUND else size - 2 * k)])
 
     def swap(x):
         return lax.ppermute(x, "ctx", [(i, i ^ 1) for i in range(size)])
 
-    packed = pl.pallas_call(
-        pack_kernel,
-        out_shape=[jax.ShapeDtypeStruct((per * 2 * rows + 16, D), jnp.bfloat16)] * CHUNKS,
-    )(key_matrix, value_matrix, segment)
-
+    def far(block):
+        if not FWD:
+            return [swap(block)] + [up(block, k) for k in range(1, pairs)]
+        own = [block]
+        for _ in range(pairs - 2):
+            own.append(up(own[-1], 1))
+        return [swap(block), *own[1:], up(block, pairs - 1)]
+
+    def near(block, first):
+        other, *mids, top = first
+        return [block, *mids, top], [other, *(swap(x) for x in mids), up(other, pairs - 1)]
+
+    finals = []
+    blocks = []
+    begin = 0
+    for per in SPLIT:
+        blocks.append(pack(begin, per, key_matrix, value_matrix, segment))
+        begin += per
+    begin = 0
     prev = None
-    finals = []
-    for c in range(CHUNKS):
-        block = packed[c]
-        own = [block] + [up(block, k) for k in range(1, pairs)]
-        other = swap(block)
-        peer = [other] + [swap(x) for x in own[1:-1]] + [up(other, pairs - 1)]
-        attended, grad_query, mine_0, theirs_0, mine_mid, theirs_mid, mine_last, theirs_last = attend(
-            c, here, own, peer, queries, cotangent, segment, prev
-        )
-        prev = (attended, grad_query)
-        first, *mids = add_lanes(
-            mine_mid, swap(theirs_mid), theirs_0, down(theirs_last, pairs - 1)
-        )
-        finals += [mine_0, down(mine_last, pairs - 1), swap(first)]
-        finals += [down(x, k) for k, x in enumerate(mids, 1)]
+    first = far(blocks[0])
+    if FETCH:
+        queries, cotangent = fetch(queries, cotangent, blocks[0])
+    def later(values, event):
+        return lax.optimization_barrier((*values, event))[:-1]
+
+    waiting = None
+
+    def finish(waiting):
+        mine_0, theirs_0, mine_mid, got, last = waiting
+        lower, *mids = add_lanes(mine_mid, got, theirs_0, last)
+        downs = [down(x, k) for k, x in enumerate(mids, 1)]
+        finals.extend([mine_0, last, swap(lower), *downs])
+
+    if FETCH:
+        first[1], queries, cotangent = lax.optimization_barrier((first[1], queries, cotangent))
+    for c, per in enumerate(SPLIT):
+        more = c + 1 < len(SPLIT)
+        own, peer = near(blocks[c], first)
+        if more:
+            (block,) = later(blocks[c + 1 : c + 2], own[TIE1])
+            blocks[c + 1] = block
+            first = far(block)
+        made = None
+        for step, heads in enumerate(WORK[c]):
+            attended, grad_query, *made = attend(
+                begin, per, heads, here, own, peer, queries, cotangent, segment, prev, made
+            )
+            prev = (attended, grad_query)
+            if step == 0 and waiting is not None:
+                waiting[3], waiting[4] = later(waiting[3:], made[0])
+                finish(waiting)
+                waiting = None
+            if step == 0 and more and TIE2:
+                first = list(later(first, made[0]))
+        begin += per
+        mine_0, theirs_0, mine_mid, theirs_mid, last = made
+        waiting = [mine_0, theirs_0, mine_mid, swap(theirs_mid), down(last, pairs - 1)]
+    finish(waiting)
     grads = pl.pallas_call(
         functools.partial(finish_kernel, pairs),
+        in_specs=[VMEM] * len(finals),
+        out_specs=[VMEM] * 2,
+        compiler_params=pltpu.CompilerParams(vmem_limit_bytes=16 << 20),
         out_shape=[jax.ShapeDtypeStruct(key_matrix.shape, jnp.float32)] * 2,
     )(*finals)
     return (attended, grad_query, grads[0], grads[1])

time: 98.4 us -> 81.1 us (0.82)
  starting transfers between devices: 49.2 us -> 35.2 us
  local copies, waits for them, and re-layouts: 6.05 us -> 4.01 us
    ppermute x16 -> x14, starting transfers between devices: 37.3 us -> 24.5 us  [the longest x8 14.6 us: up(): lax.ppermute(x, 'ctx', [(i, (i + 2 * k) % size) for i in range(size if RO...]
    ppermute x16 -> x14, waiting for transfers between devices: 18.7 us -> 16.5 us  [the longest x6 8.29 us: down(): lax.ppermute(x, 'ctx', [((i + 2 * k) % size, i) for i in range(size if RO...]
    unnamed x34 -> x12, local copies, waits for them, and re-layouts: 6.05 us -> 4.01 us
    ppermute x10, waiting for transfers between devices: 0.03 us -> 1.41 us  [swap(): return lax.ppermute(x, 'ctx', [(i, i ^ 1) for i in range(size)])]
    ppermute x10, starting transfers between devices: 11.9 us -> 10.7 us  [swap(): return lax.ppermute(x, 'ctx', [(i, i ^ 1) for i in range(size)])]
    pallas_call x6 -> x8, Pallas kernels: 22.9 us -> 22.8 us  [the longest x2 18.5 us: attend(): pl.pallas_call(functools.partial(attend_kernel, pairs, begin, per, heads,...]
  transfers between devices with their start and end apart: 26 -> 24, of which waited for: 5 -> 7; matrix products, arithmetic and copies ran while one was open for 0% -> 0% of each run, Pallas kernels for 19% -> 25%
where the time goes in v3:
time: 81.1 us; the launch traced here: 80.8 us
  starting transfers between devices  35.2 us (43%)
  Pallas kernels  22.8 us (28%)
  waiting for transfers between devices  17.9 us (22%)
  local copies, waits for them, and re-layouts  4.01 us (5%)
    pallas_call x2, Pallas kernels, attend(): pl.pallas_call(functools.partial(attend_kernel, pairs, begin, per, heads,...  18.5 us
    ppermute x8, starting transfers between devices, up(): lax.ppermute(x, 'ctx', [(i, (i + 2 * k) % size) for i in range(size if RO...  14.6 us
    ppermute x10, starting transfers between devices, swap(): return lax.ppermute(x, 'ctx', [(i, i ^ 1) for i in range(size)])  10.7 us
    ppermute x6, starting transfers between devices, down(): lax.ppermute(x, 'ctx', [((i + 2 * k) % size, i) for i in range(size if RO...  9.9 us
    ppermute x6, waiting for transfers between devices, down(): lax.ppermute(x, 'ctx', [((i + 2 * k) % size, i) for i in range(size if RO...  8.29 us
    ppermute x8, waiting for transfers between devices, up(): lax.ppermute(x, 'ctx', [(i, (i + 2 * k) % size) for i in range(size if RO...  8.21 us
    unnamed x12, local copies, waits for them, and re-layouts  4.01 us
    pallas_call x2, Pallas kernels, pack(): pl.pallas_call(functools.partial(pack_kernel, begin, per), in_specs=[HBM]...  3.06 us
  transfers between devices with their start and end apart: 24, of which 7 were waited for; matrix products, arithmetic and copies ran while one was open for 0% of the time, Pallas kernels for 25%

profile of v3, /device:TPU:0, one launch (start us, length us, event | category | flops | bytes accessed | tf_op | source)
XLA Modules:
  0.0 80.8 jit_solution(3775504196580395486)
XLA Ops:
  0.6 0.0 copy-start.5
  0.6 1.5 %shard_map.85.after_ref.refs_0_ = bf16[528,128]{1,0:T(8,128)(2,1)} custom-call(bf16[1,128,512]{2,1,0:T(8,128)(2,1)} %k_ref.3, bf16[1,128,512]{2,1,0:T(8,128)(2,1)} %v_ref.3, s32[1,128]{1,0:T(1,128)} %refs_10_.3), custom_call_target="tpu_custom_call" | custom-call | tf_op jit(solution)/shard_map/pallas_call | solution.py:54
  2.2 0.0 copy-start.3
  2.2 3.1 %collective-permute-start = (bf16[528,128]{1,0:T(8,128)(2,1)}, bf16[528,128]{1,0:T(8,128)(2,1)S(1)}, u32[]{:S(2)}, u32[]{:S(2)}) collective-permute-start(bf16[528,128]{1,0:T(8,128)(2,1)} %shard_map.85.after_ref.refs_0_), channel_id=1, source_target_pairs={{0,2},{1,3},{2,4},{3,5},{4,6},{5,7},{6,0},{7,1},{8,10},{9,11},{10,... | collective-permute-start | bytes 405512 | tf_op jit(solution)/shard_map/ppermute | solution.py:377
  5.3 1.5 %collective-permute-start.7 = (bf16[528,128]{1,0:T(8,128)(2,1)}, bf16[528,128]{1,0:T(8,128)(2,1)S(1)}, u32[]{:S(2)}, u32[]{:S(2)}) collective-permute-start(bf16[528,128]{1,0:T(8,128)(2,1)} %shard_map.85.after_ref.refs_0_), channel_id=1, source_target_pairs={{0,1},{1,0},{2,3},{3,2},{4,5},{5,4},{6,7},{7,6},{8,9},{9,8},{10,11... | collective-permute-start | bytes 405512 | tf_op jit(solution)/shard_map/ppermute | solution.py:383
  6.8 4.3 %collective-permute-done.refs_1_ = bf16[528,128]{1,0:T(8,128)(2,1)S(1)} collective-permute-done((bf16[528,128]{1,0:T(8,128)(2,1)}, bf16[528,128]{1,0:T(8,128)(2,1)S(1)}, u32[]{:S(2)}, u32[]{:S(2)}) %collective-permute-start) | collective-permute-done | bytes 135200 | tf_op jit(solution)/shard_map/ppermute | solution.py:377
  11.1 0.0 collective-permute-start.1
  11.1 3.8 %collective-permute-start.6 = (bf16[528,128]{1,0:T(8,128)(2,1)}, bf16[528,128]{1,0:T(8,128)(2,1)S(1)}, u32[]{:S(2)}, u32[]{:S(2)}) collective-permute-start(bf16[528,128]{1,0:T(8,128)(2,1)} %shard_map.85.after_ref.refs_0_), channel_id=1, source_target_pairs={{0,6},{1,7},{2,0},{3,1},{4,2},{5,3},{6,4},{7,5},{8,14},{9,15},{10,... | collective-permute-start | bytes 405512 | tf_op jit(solution)/shard_map/ppermute | solution.py:377
  14.9 1.5 %shard_map.84.refs_0_ = bf16[528,128]{1,0:T(8,128)(2,1)} custom-call(bf16[1,128,512]{2,1,0:T(8,128)(2,1)} %k_ref.3, bf16[1,128,512]{2,1,0:T(8,128)(2,1)} %v_ref.3, s32[1,128]{1,0:T(1,128)} %refs_10_.3), custom_call_target="tpu_custom_call" | custom-call | tf_op jit(solution)/shard_map/pallas_call | solution.py:54
  16.5 0.0 copy-start
  16.5 1.2 %copy-done = bf16[1,128,4096]{2,1,0:T(8,128)(2,1)S(1)} copy-done((bf16[1,128,4096]{2,1,0:T(8,128)(2,1)S(1)}, bf16[1,128,4096]{2,1,0:T(8,128)(2,1)}, u32[]{:S(2)}) %copy-start) | copy-done | bytes 1048600
  17.7 1.2 %copy-done.1 = bf16[1,128,4096]{2,1,0:T(8,128)(2,1)S(1)} copy-done((bf16[1,128,4096]{2,1,0:T(8,128)(2,1)S(1)}, bf16[1,128,4096]{2,1,0:T(8,128)(2,1)}, u32[]{:S(2)}) %copy-start.1) | copy-done | bytes 1048600
  18.9 0.9 %copy-done.2 = bf16[528,128]{1,0:T(8,128)(2,1)S(1)} copy-done((bf16[528,128]{1,0:T(8,128)(2,1)S(1)}, bf16[528,128]{1,0:T(8,128)(2,1)}, u32[]{:S(2)}) %copy-start.2) | copy-done | bytes 135192
  19.8 0.2 shard_map.86
  20.0 0.0 collective-permute-done.7.refs_4_
  20.0 0.1 collective-permute-start.10
  20.1 0.6 copy-done.4
  20.7 1.4 %collective-permute-start.3 = (bf16[528,128]{1,0:T(8,128)(2,1)S(1)}, bf16[528,128]{1,0:T(8,128)(2,1)S(1)}, u32[]{:S(2)}, u32[]{:S(2)}) collective-permute-start(bf16[528,128]{1,0:T(8,128)(2,1)S(1)} %copy-done.4), channel_id=1, source_target_pairs={{0,2},{1,3},{2,4},{3,5},{4,6},{5,7},{6,0},{7,1},{8,10},{9,11},{10,... | collective-permute-start | bytes 405512 | tf_op jit(solution)/shard_map/ppermute | solution.py:377
  22.1 1.5 %collective-permute-start.8 = (bf16[528,128]{1,0:T(8,128)(2,1)S(1)}, bf16[528,128]{1,0:T(8,128)(2,1)S(1)}, u32[]{:S(2)}, u32[]{:S(2)}) collective-permute-start(bf16[528,128]{1,0:T(8,128)(2,1)S(1)} %collective-permute-done.refs_1_), channel_id=1, source_target_pairs={{0,1},{1,0},{2,3},{3,2},{4,5},{5,4},{6,7},{7,6},{8,9},{9,8},{10,11... | collective-permute-start | bytes 405512 | tf_op jit(solution)/shard_map/ppermute | solution.py:383
  23.6 0.5 collective-permute-start.9
  24.1 2.5 %collective-permute-start.5 = (bf16[528,128]{1,0:T(8,128)(2,1)S(1)}, bf16[528,128]{1,0:T(8,128)(2,1)S(1)}, u32[]{:S(2)}, u32[]{:S(2)}) collective-permute-start(bf16[528,128]{1,0:T(8,128)(2,1)S(1)} %copy-done.4), channel_id=1, source_target_pairs={{0,6},{1,7},{2,0},{3,1},{4,2},{5,3},{6,4},{7,5},{8,14},{9,15},{10,... | collective-permute-start | bytes 405512 | tf_op jit(solution)/shard_map/ppermute | solution.py:377
  26.6 2.5 %collective-permute-done.10.refs_7_ = bf16[528,128]{1,0:T(8,128)(2,1)S(1)} collective-permute-done((bf16[528,128]{1,0:T(8,128)(2,1)S(1)}, bf16[528,128]{1,0:T(8,128)(2,1)S(1)}, u32[]{:S(2)}, u32[]{:S(2)}) %collective-permute-start.10) | collective-permute-done | bytes 135200 | tf_op jit(solution)/shard_map/ppermute | solution.py:377
  29.1 1.8 %collective-permute-start.2 = (bf16[528,128]{1,0:T(8,128)(2,1)S(1)}, bf16[528,128]{1,0:T(8,128)(2,1)S(1)}, u32[]{:S(2)}, u32[]{:S(2)}) collective-permute-start(bf16[528,128]{1,0:T(8,128)(2,1)S(1)} %copy-done.4), channel_id=1, source_target_pairs={{0,1},{1,0},{2,3},{3,2},{4,5},{5,4},{6,7},{7,6},{8,9},{9,8},{10,11... | collective-permute-start | bytes 405512 | tf_op jit(solution)/shard_map/ppermute | solution.py:383
  30.9 0.0 collective-permute-done.8.refs_5_
  30.9 0.0 collective-permute-done.9.refs_6_
  30.9 9.3 %shard_map.87 = (bf16[1,128,4096]{2,1,0:T(8,128)(2,1)}, f32[1,128,4096]{2,1,0:T(8,128)}, f32[1,512,128]{2,1,0:T(8,128)S(1)}, f32[1,512,128]{2,1,0:T(8,128)S(1)},...) custom-call(s32[1]{0:T(128)} %bitcast.here_ref, ...), custom_call_target="tpu_custom_call" | custom-call | flops 6442450944 | bytes 8388608 | tf_op jit(solution)/shard_map/pallas_call | solution.py:306
  40.2 0.7 collective-permute-start.11
  40.9 1.4 %collective-permute-start.12 = (bf16[528,128]{1,0:T(8,128)(2,1)S(1)}, bf16[528,128]{1,0:T(8,128)(2,1)S(1)}, u32[]{:S(2)}, u32[]{:S(2)}) collective-permute-start(bf16[528,128]{1,0:T(8,128)(2,1)S(1)} %collective-permute-done.4.refs_2_), channel_id=1, source_target_pairs={{0,1},{1,0},{2,3},{3,2},{4,5},{5,4},{6,7},{7,6},{8,9},{9,8},{10,11... | collective-permute-start | bytes 405512 | tf_op jit(solution)/shard_map/ppermute | solution.py:383
  42.3 3.8 %collective-permute-start.13 = (bf16[528,128]{1,0:T(8,128)(2,1)S(1)}, bf16[528,128]{1,0:T(8,128)(2,1)S(1)}, u32[]{:S(2)}, u32[]{:S(2)}) collective-permute-start(bf16[528,128]{1,0:T(8,128)(2,1)S(1)} %collective-permute-done.2.refs_4_), channel_id=1, source_target_pairs={{0,6},{1,7},{2,0},{3,1},{4,2},{5,3},{6,4},{7,5},{8,14},{9,15},{10,... | collective-permute-start | bytes 405512 | tf_op jit(solution)/shard_map/ppermute | solution.py:377
  46.1 0.2 collective-permute-start.14
  46.4 0.0 collective-permute-start.15
  46.4 1.4 %collective-permute-done.12.refs_6_ = bf16[528,128]{1,0:T(8,128)(2,1)S(1)} collective-permute-done((bf16[528,128]{1,0:T(8,128)(2,1)S(1)}, bf16[528,128]{1,0:T(8,128)(2,1)S(1)}, u32[]{:S(2)}, u32[]{:S(2)}) %collective-permute-start.12) | collective-permute-done | bytes 135200 | tf_op jit(solution)/shard_map/ppermute | solution.py:383
  47.8 1.4 %collective-permute-done.13.refs_7_ = bf16[528,128]{1,0:T(8,128)(2,1)S(1)} collective-permute-done((bf16[528,128]{1,0:T(8,128)(2,1)S(1)}, bf16[528,128]{1,0:T(8,128)(2,1)S(1)}, u32[]{:S(2)}, u32[]{:S(2)}) %collective-permute-start.13) | collective-permute-done | bytes 135200 | tf_op jit(solution)/shard_map/ppermute | solution.py:377
  49.2 9.2 %shard_map.88 = (bf16[1,128,4096]{2,1,0:T(8,128)(2,1)}, f32[1,128,4096]{2,1,0:T(8,128)}, f32[1,512,128]{2,1,0:T(8,128)S(1)}, f32[1,512,128]{2,1,0:T(8,128)S(1)},...) custom-call(s32[1]{0:T(128)} %bitcast.here_ref, ...), custom_call_target="tpu_custom_call", output_to_operand_aliasing={{0}: (12, {}), {1}: (13, {})} | custom-call | flops 6442450944 | bytes 8388608 | tf_op jit(solution)/shard_map/pallas_call | solution.py:306
  58.4 0.5 collective-permute-start.19
  58.9 0.8 %collective-permute-start.20 = (bf16[2,512,128]{2,1,0:T(8,128)(2,1)S(1)}, bf16[2,512,128]{2,1,0:T(8,128)(2,1)S(1)}, u32[]{:S(2)}, u32[]{:S(2)}) collective-permute-start(bf16[2,512,128]{2,1,0:T(8,128)(2,1)S(1)} %get-tuple-element.65), channel_id=1, source_target_pairs={{0,1},{1,0},{2,3},{3,2},{4,5},{5,4},{6,7},{7,6},{8,9},{9,8},{10,11... | collective-permute-start | bytes 786440 | tf_op jit(solution)/shard_map/ppermute | solution.py:383
  59.8 0.1 shard_map.89
  59.8 1.3 %collective-permute-start.16 = (bf16[512,128]{1,0:T(8,128)(2,1)S(1)}, bf16[512,128]{1,0:T(8,128)(2,1)S(1)}, u32[]{:S(2)}, u32[]{:S(2)}) collective-permute-start(bf16[512,128]{1,0:T(8,128)(2,1)S(1)} %get-tuple-element.60), channel_id=1, source_target_pairs={{0,1},{1,0},{2,3},{3,2},{4,5},{5,4},{6,7},{7,6},{8,9},{9,8},{10,11... | collective-permute-start | bytes 393224 | tf_op jit(solution)/shard_map/ppermute | solution.py:383
  61.1 3.6 %collective-permute-start.17 = (bf16[512,128]{1,0:T(8,128)(2,1)S(1)}, bf16[512,128]{1,0:T(8,128)(2,1)S(1)}, u32[]{:S(2)}, u32[]{:S(2)}) collective-permute-start(bf16[512,128]{1,0:T(8,128)(2,1)S(1)} %get-tuple-element.61), channel_id=1, source_target_pairs={{2,0},{3,1},{4,2},{5,3},{6,4},{7,5},{0,6},{1,7},{10,8},{11,9},{12,... | collective-permute-start | bytes 393224 | tf_op jit(solution)/shard_map/ppermute | solution.py:380
  64.7 0.5 collective-permute-start.18
  65.1 4.0 %collective-permute-done.19.last_ref.refs_6_ = bf16[2,512,128]{2,1,0:T(8,128)(2,1)S(1)} collective-permute-done((bf16[2,512,128]{2,1,0:T(8,128)(2,1)S(1)}, bf16[2,512,128]{2,1,0:T(8,128)(2,1)S(1)}, u32[]{:S(2)}, u32[]{:S(2)}) %collective-permute-start.19) | collective-permute-done | bytes 262176 | tf_op jit(solution)/shard_map/ppermute | solution.py:380
  69.1 0.1 shard_map.90
  69.2 1.0 %collective-permute-start.21 = (bf16[512,128]{1,0:T(8,128)(2,1)S(1)}, bf16[512,128]{1,0:T(8,128)(2,1)S(1)}, u32[]{:S(2)}, u32[]{:S(2)}) collective-permute-start(bf16[512,128]{1,0:T(8,128)(2,1)S(1)} %get-tuple-element.67), channel_id=1, source_target_pairs={{0,1},{1,0},{2,3},{3,2},{4,5},{5,4},{6,7},{7,6},{8,9},{9,8},{10,11... | collective-permute-start | bytes 393224 | tf_op jit(solution)/shard_map/ppermute | solution.py:383
  70.2 2.7 %collective-permute-start.22 = (bf16[512,128]{1,0:T(8,128)(2,1)S(1)}, bf16[512,128]{1,0:T(8,128)(2,1)S(1)}, u32[]{:S(2)}, u32[]{:S(2)}) collective-permute-start(bf16[512,128]{1,0:T(8,128)(2,1)S(1)} %get-tuple-element.68), channel_id=1, source_target_pairs={{2,0},{3,1},{4,2},{5,3},{6,4},{7,5},{0,6},{1,7},{10,8},{11,9},{12,... | collective-permute-start | bytes 393224 | tf_op jit(solution)/shard_map/ppermute | solution.py:380
  72.9 2.6 %collective-permute-start.23 = (bf16[512,128]{1,0:T(8,128)(2,1)S(1)}, bf16[512,128]{1,0:T(8,128)(2,1)S(1)}, u32[]{:S(2)}, u32[]{:S(2)}) collective-permute-start(bf16[512,128]{1,0:T(8,128)(2,1)S(1)} %get-tuple-element.69), channel_id=1, source_target_pairs={{4,0},{5,1},{6,2},{7,3},{0,4},{1,5},{2,6},{3,7},{12,8},{13,9},{14,... | collective-permute-start | bytes 393224 | tf_op jit(solution)/shard_map/ppermute | solution.py:380
  75.5 1.0 %collective-permute-done.22.refs_8_ = bf16[512,128]{1,0:T(8,128)(2,1)S(1)} collective-permute-done((bf16[512,128]{1,0:T(8,128)(2,1)S(1)}, bf16[512,128]{1,0:T(8,128)(2,1)S(1)}, u32[]{:S(2)}, u32[]{:S(2)}) %collective-permute-start.22) | collective-permute-done | bytes 131104 | tf_op jit(solution)/shard_map/ppermute | solution.py:380
  76.5 3.3 %collective-permute-done.23.refs_9_ = bf16[512,128]{1,0:T(8,128)(2,1)S(1)} collective-permute-done((bf16[512,128]{1,0:T(8,128)(2,1)S(1)}, bf16[512,128]{1,0:T(8,128)(2,1)S(1)}, u32[]{:S(2)}, u32[]{:S(2)}) %collective-permute-start.23) | collective-permute-done | bytes 131104 | tf_op jit(solution)/shard_map/ppermute | solution.py:380
  79.8 0.9 %shard_map.91 = (f32[1,128,512]{2,1,0:T(8,128)}, f32[1,128,512]{2,1,0:T(8,128)}) custom-call(f32[1,512,128]{2,1,0:T(8,128)S(1)} %get-tuple-element.44.refs_0_, bf16[2,512,128]{2,1,0:T(8,128)(2,1)S(1)} %collective-permute-done.15.last_ref.refs_1_, bf16[512,128]{1,0:T(8,128)(2,1)S(1)} %collective-permute-done.16.refs_2_, ...), custom_call_target="tpu_custom_call" | custom-call | tf_op jit(solution)/shard_map/pallas_call | solution.py:444
  (20 shorter events, 0.0 us)
Async XLA Ops:
  0.6 30.3 %copy-start.5 = (s32[1,128]{1,0:T(1,128)S(1)}, s32[1,128]{1,0:T(1,128)}, u32[]{:S(2)}) copy-start(s32[1,128]{1,0:T(1,128)} %refs_10_.3) | copy-start | bytes 1540
  2.2 28.7 %copy-start.3 = (bf16[528,128]{1,0:T(8,128)(2,1)S(1)}, bf16[528,128]{1,0:T(8,128)(2,1)}, u32[]{:S(2)}) copy-start(bf16[528,128]{1,0:T(8,128)(2,1)} %shard_map.85.after_ref.refs_0_) | copy-start | bytes 405508
  2.2 8.9 %collective-permute-start = (bf16[528,128]{1,0:T(8,128)(2,1)}, bf16[528,128]{1,0:T(8,128)(2,1)S(1)}, u32[]{:S(2)}, u32[]{:S(2)}) collective-permute-start(bf16[528,128]{1,0:T(8,128)(2,1)} %shard_map.85.after_ref.refs_0_), channel_id=1, source_target_pairs={{0,2},{1,3},{2,4},{3,5},{4,6},{5,7},{6,0},{7,1},{8,10},{9,11},{10,... | collective-permute-start | bytes 405512 | tf_op jit(solution)/shard_map/ppermute | solution.py:377
  5.3 14.7 %collective-permute-start.7 = (bf16[528,128]{1,0:T(8,128)(2,1)}, bf16[528,128]{1,0:T(8,128)(2,1)S(1)}, u32[]{:S(2)}, u32[]{:S(2)}) collective-permute-start(bf16[528,128]{1,0:T(8,128)(2,1)} %shard_map.85.after_ref.refs_0_), channel_id=1, source_target_pairs={{0,1},{1,0},{2,3},{3,2},{4,5},{5,4},{6,7},{7,6},{8,9},{9,8},{10,11... | collective-permute-start | bytes 405512 | tf_op jit(solution)/shard_map/ppermute | solution.py:383
  11.1 9.0 %collective-permute-start.1 = (bf16[528,128]{1,0:T(8,128)(2,1)S(1)}, bf16[528,128]{1,0:T(8,128)(2,1)S(1)}, u32[]{:S(2)}, u32[]{:S(2)}) collective-permute-start(bf16[528,128]{1,0:T(8,128)(2,1)S(1)} %collective-permute-done.refs_1_), channel_id=1, source_target_pairs={{0,2},{1,3},{2,4},{3,5},{4,6},{5,7},{6,0},{7,1},{8,10},{9,11},{10,... | collective-permute-start | bytes 405512 | tf_op jit(solution)/shard_map/ppermute | solution.py:377
  11.1 13.0 %collective-permute-start.6 = (bf16[528,128]{1,0:T(8,128)(2,1)}, bf16[528,128]{1,0:T(8,128)(2,1)S(1)}, u32[]{:S(2)}, u32[]{:S(2)}) collective-permute-start(bf16[528,128]{1,0:T(8,128)(2,1)} %shard_map.85.after_ref.refs_0_), channel_id=1, source_target_pairs={{0,6},{1,7},{2,0},{3,1},{4,2},{5,3},{6,4},{7,5},{8,14},{9,15},{10,... | collective-permute-start | bytes 405512 | tf_op jit(solution)/shard_map/ppermute | solution.py:377
  16.5 1.2 %copy-start = (bf16[1,128,4096]{2,1,0:T(8,128)(2,1)S(1)}, bf16[1,128,4096]{2,1,0:T(8,128)(2,1)}, u32[]{:S(2)}) copy-start(bf16[1,128,4096]{2,1,0:T(8,128)(2,1)} %q_ref.1) | copy-start | bytes 3145732
  17.7 1.2 %copy-start.1 = (bf16[1,128,4096]{2,1,0:T(8,128)(2,1)S(1)}, bf16[1,128,4096]{2,1,0:T(8,128)(2,1)}, u32[]{:S(2)}) copy-start(bf16[1,128,4096]{2,1,0:T(8,128)(2,1)} %c_ref.1) | copy-start | bytes 3145732
  18.9 0.9 %copy-start.2 = (bf16[528,128]{1,0:T(8,128)(2,1)S(1)}, bf16[528,128]{1,0:T(8,128)(2,1)}, u32[]{:S(2)}) copy-start(bf16[528,128]{1,0:T(8,128)(2,1)} %shard_map.85.after_ref.refs_0_) | copy-start | bytes 405508
  19.8 0.9 %copy-start.4 = (bf16[528,128]{1,0:T(8,128)(2,1)S(1)}, bf16[528,128]{1,0:T(8,128)(2,1)}, u32[]{:S(2)}) copy-start(bf16[528,128]{1,0:T(8,128)(2,1)} %shard_map.84.refs_0_) | copy-start | bytes 405508
  20.0 9.1 %collective-permute-start.10 = (bf16[528,128]{1,0:T(8,128)(2,1)S(1)}, bf16[528,128]{1,0:T(8,128)(2,1)S(1)}, u32[]{:S(2)}, u32[]{:S(2)}) collective-permute-start(bf16[528,128]{1,0:T(8,128)(2,1)S(1)} %collective-permute-done.7.refs_4_), channel_id=1, source_target_pairs={{0,6},{1,7},{2,0},{3,1},{4,2},{5,3},{6,4},{7,5},{8,14},{9,15},{10,... | collective-permute-start | bytes 405512 | tf_op jit(solution)/shard_map/ppermute | solution.py:377
  20.7 10.1 %collective-permute-start.3 = (bf16[528,128]{1,0:T(8,128)(2,1)S(1)}, bf16[528,128]{1,0:T(8,128)(2,1)S(1)}, u32[]{:S(2)}, u32[]{:S(2)}) collective-permute-start(bf16[528,128]{1,0:T(8,128)(2,1)S(1)} %copy-done.4), channel_id=1, source_target_pairs={{0,2},{1,3},{2,4},{3,5},{4,6},{5,7},{6,0},{7,1},{8,10},{9,11},{10,... | collective-permute-start | bytes 405512 | tf_op jit(solution)/shard_map/ppermute | solution.py:377
  22.1 8.8 %collective-permute-start.8 = (bf16[528,128]{1,0:T(8,128)(2,1)S(1)}, bf16[528,128]{1,0:T(8,128)(2,1)S(1)}, u32[]{:S(2)}, u32[]{:S(2)}) collective-permute-start(bf16[528,128]{1,0:T(8,128)(2,1)S(1)} %collective-permute-done.refs_1_), channel_id=1, source_target_pairs={{0,1},{1,0},{2,3},{3,2},{4,5},{5,4},{6,7},{7,6},{8,9},{9,8},{10,11... | collective-permute-start | bytes 405512 | tf_op jit(solution)/shard_map/ppermute | solution.py:383
  23.6 7.3 %collective-permute-start.9 = (bf16[528,128]{1,0:T(8,128)(2,1)S(1)}, bf16[528,128]{1,0:T(8,128)(2,1)S(1)}, u32[]{:S(2)}, u32[]{:S(2)}) collective-permute-start(bf16[528,128]{1,0:T(8,128)(2,1)S(1)} %collective-permute-done.1.refs_2_), channel_id=1, source_target_pairs={{0,1},{1,0},{2,3},{3,2},{4,5},{5,4},{6,7},{7,6},{8,9},{9,8},{10,11... | collective-permute-start | bytes 405512 | tf_op jit(solution)/shard_map/ppermute | solution.py:383
  24.1 16.1 %collective-permute-start.5 = (bf16[528,128]{1,0:T(8,128)(2,1)S(1)}, bf16[528,128]{1,0:T(8,128)(2,1)S(1)}, u32[]{:S(2)}, u32[]{:S(2)}) collective-permute-start(bf16[528,128]{1,0:T(8,128)(2,1)S(1)} %copy-done.4), channel_id=1, source_target_pairs={{0,6},{1,7},{2,0},{3,1},{4,2},{5,3},{6,4},{7,5},{8,14},{9,15},{10,... | collective-permute-start | bytes 405512 | tf_op jit(solution)/shard_map/ppermute | solution.py:377
  29.1 11.1 %collective-permute-start.2 = (bf16[528,128]{1,0:T(8,128)(2,1)S(1)}, bf16[528,128]{1,0:T(8,128)(2,1)S(1)}, u32[]{:S(2)}, u32[]{:S(2)}) collective-permute-start(bf16[528,128]{1,0:T(8,128)(2,1)S(1)} %copy-done.4), channel_id=1, source_target_pairs={{0,1},{1,0},{2,3},{3,2},{4,5},{5,4},{6,7},{7,6},{8,9},{9,8},{10,11... | collective-permute-start | bytes 405512 | tf_op jit(solution)/shard_map/ppermute | solution.py:383
  30.9 9.4 %collective-permute-start.4 = (bf16[528,128]{1,0:T(8,128)(2,1)S(1)}, bf16[528,128]{1,0:T(8,128)(2,1)S(1)}, u32[]{:S(2)}, u32[]{:S(2)}) collective-permute-start(bf16[528,128]{1,0:T(8,128)(2,1)S(1)} %collective-permute-done.3.refs_1_), channel_id=1, source_target_pairs={{0,2},{1,3},{2,4},{3,5},{4,6},{5,7},{6,0},{7,1},{8,10},{9,11},{10,... | collective-permute-start | bytes 405512 | tf_op jit(solution)/shard_map/ppermute | solution.py:377
  40.2 6.2 %collective-permute-start.11 = (bf16[528,128]{1,0:T(8,128)(2,1)S(1)}, bf16[528,128]{1,0:T(8,128)(2,1)S(1)}, u32[]{:S(2)}, u32[]{:S(2)}) collective-permute-start(bf16[528,128]{1,0:T(8,128)(2,1)S(1)} %collective-permute-done.3.refs_1_), channel_id=1, source_target_pairs={{0,1},{1,0},{2,3},{3,2},{4,5},{5,4},{6,7},{7,6},{8,9},{9,8},{10,11... | collective-permute-start | bytes 405512 | tf_op jit(solution)/shard_map/ppermute | solution.py:383
  40.9 6.9 %collective-permute-start.12 = (bf16[528,128]{1,0:T(8,128)(2,1)S(1)}, bf16[528,128]{1,0:T(8,128)(2,1)S(1)}, u32[]{:S(2)}, u32[]{:S(2)}) collective-permute-start(bf16[528,128]{1,0:T(8,128)(2,1)S(1)} %collective-permute-done.4.refs_2_), channel_id=1, source_target_pairs={{0,1},{1,0},{2,3},{3,2},{4,5},{5,4},{6,7},{7,6},{8,9},{9,8},{10,11... | collective-permute-start | bytes 405512 | tf_op jit(solution)/shard_map/ppermute | solution.py:383
  42.3 6.8 %collective-permute-start.13 = (bf16[528,128]{1,0:T(8,128)(2,1)S(1)}, bf16[528,128]{1,0:T(8,128)(2,1)S(1)}, u32[]{:S(2)}, u32[]{:S(2)}) collective-permute-start(bf16[528,128]{1,0:T(8,128)(2,1)S(1)} %collective-permute-done.2.refs_4_), channel_id=1, source_target_pairs={{0,6},{1,7},{2,0},{3,1},{4,2},{5,3},{6,4},{7,5},{8,14},{9,15},{10,... | collective-permute-start | bytes 405512 | tf_op jit(solution)/shard_map/ppermute | solution.py:377
  46.1 13.6 %collective-permute-start.14 = (bf16[2,512,128]{2,1,0:T(8,128)(2,1)S(1)}, bf16[2,512,128]{2,1,0:T(8,128)(2,1)S(1)}, u32[]{:S(2)}, u32[]{:S(2)}) collective-permute-start(bf16[2,512,128]{2,1,0:T(8,128)(2,1)S(1)} %get-tuple-element.53), channel_id=1, source_target_pairs={{0,1},{1,0},{2,3},{3,2},{4,5},{5,4},{6,7},{7,6},{8,9},{9,8},{10,11... | collective-permute-start | bytes 786440 | tf_op jit(solution)/shard_map/ppermute | solution.py:383
  46.4 13.4 %collective-permute-start.15 = (bf16[2,512,128]{2,1,0:T(8,128)(2,1)S(1)}, bf16[2,512,128]{2,1,0:T(8,128)(2,1)S(1)}, u32[]{:S(2)}, u32[]{:S(2)}) collective-permute-start(bf16[2,512,128]{2,1,0:T(8,128)(2,1)S(1)} %get-tuple-element.54), channel_id=1, source_target_pairs={{6,0},{7,1},{0,2},{1,3},{2,4},{3,5},{4,6},{5,7},{14,8},{15,9},{8,1... | collective-permute-start | bytes 786440 | tf_op jit(solution)/shard_map/ppermute | solution.py:380
  58.4 10.7 %collective-permute-start.19 = (bf16[2,512,128]{2,1,0:T(8,128)(2,1)S(1)}, bf16[2,512,128]{2,1,0:T(8,128)(2,1)S(1)}, u32[]{:S(2)}, u32[]{:S(2)}) collective-permute-start(bf16[2,512,128]{2,1,0:T(8,128)(2,1)S(1)} %get-tuple-element.63), channel_id=1, source_target_pairs={{6,0},{7,1},{0,2},{1,3},{2,4},{3,5},{4,6},{5,7},{14,8},{15,9},{8,1... | collective-permute-start | bytes 786440 | tf_op jit(solution)/shard_map/ppermute | solution.py:380
  58.9 10.2 %collective-permute-start.20 = (bf16[2,512,128]{2,1,0:T(8,128)(2,1)S(1)}, bf16[2,512,128]{2,1,0:T(8,128)(2,1)S(1)}, u32[]{:S(2)}, u32[]{:S(2)}) collective-permute-start(bf16[2,512,128]{2,1,0:T(8,128)(2,1)S(1)} %get-tuple-element.65), channel_id=1, source_target_pairs={{0,1},{1,0},{2,3},{3,2},{4,5},{5,4},{6,7},{7,6},{8,9},{9,8},{10,11... | collective-permute-start | bytes 786440 | tf_op jit(solution)/shard_map/ppermute | solution.py:383
  59.8 13.1 %collective-permute-start.16 = (bf16[512,128]{1,0:T(8,128)(2,1)S(1)}, bf16[512,128]{1,0:T(8,128)(2,1)S(1)}, u32[]{:S(2)}, u32[]{:S(2)}) collective-permute-start(bf16[512,128]{1,0:T(8,128)(2,1)S(1)} %get-tuple-element.60), channel_id=1, source_target_pairs={{0,1},{1,0},{2,3},{3,2},{4,5},{5,4},{6,7},{7,6},{8,9},{9,8},{10,11... | collective-permute-start | bytes 393224 | tf_op jit(solution)/shard_map/ppermute | solution.py:383
  61.1 14.4 %collective-permute-start.17 = (bf16[512,128]{1,0:T(8,128)(2,1)S(1)}, bf16[512,128]{1,0:T(8,128)(2,1)S(1)}, u32[]{:S(2)}, u32[]{:S(2)}) collective-permute-start(bf16[512,128]{1,0:T(8,128)(2,1)S(1)} %get-tuple-element.61), channel_id=1, source_target_pairs={{2,0},{3,1},{4,2},{5,3},{6,4},{7,5},{0,6},{1,7},{10,8},{11,9},{12,... | collective-permute-start | bytes 393224 | tf_op jit(solution)/shard_map/ppermute | solution.py:380
  64.7 10.8 %collective-permute-start.18 = (bf16[512,128]{1,0:T(8,128)(2,1)S(1)}, bf16[512,128]{1,0:T(8,128)(2,1)S(1)}, u32[]{:S(2)}, u32[]{:S(2)}) collective-permute-start(bf16[512,128]{1,0:T(8,128)(2,1)S(1)} %get-tuple-element.62), channel_id=1, source_target_pairs={{4,0},{5,1},{6,2},{7,3},{0,4},{1,5},{2,6},{3,7},{12,8},{13,9},{14,... | collective-permute-start | bytes 393224 | tf_op jit(solution)/shard_map/ppermute | solution.py:380
  69.2 6.3 %collective-permute-start.21 = (bf16[512,128]{1,0:T(8,128)(2,1)S(1)}, bf16[512,128]{1,0:T(8,128)(2,1)S(1)}, u32[]{:S(2)}, u32[]{:S(2)}) collective-permute-start(bf16[512,128]{1,0:T(8,128)(2,1)S(1)} %get-tuple-element.67), channel_id=1, source_target_pairs={{0,1},{1,0},{2,3},{3,2},{4,5},{5,4},{6,7},{7,6},{8,9},{9,8},{10,11... | collective-permute-start | bytes 393224 | tf_op jit(solution)/shard_map/ppermute | solution.py:383
  70.2 6.4 %collective-permute-start.22 = (bf16[512,128]{1,0:T(8,128)(2,1)S(1)}, bf16[512,128]{1,0:T(8,128)(2,1)S(1)}, u32[]{:S(2)}, u32[]{:S(2)}) collective-permute-start(bf16[512,128]{1,0:T(8,128)(2,1)S(1)} %get-tuple-element.68), channel_id=1, source_target_pairs={{2,0},{3,1},{4,2},{5,3},{6,4},{7,5},{0,6},{1,7},{10,8},{11,9},{12,... | collective-permute-start | bytes 393224 | tf_op jit(solution)/shard_map/ppermute | solution.py:380
  72.9 7.0 %collective-permute-start.23 = (bf16[512,128]{1,0:T(8,128)(2,1)S(1)}, bf16[512,128]{1,0:T(8,128)(2,1)S(1)}, u32[]{:S(2)}, u32[]{:S(2)}) collective-permute-start(bf16[512,128]{1,0:T(8,128)(2,1)S(1)} %get-tuple-element.69), channel_id=1, source_target_pairs={{4,0},{5,1},{6,2},{7,3},{0,4},{1,5},{2,6},{3,7},{12,8},{13,9},{14,... | collective-permute-start | bytes 393224 | tf_op jit(solution)/shard_map/ppermute | solution.py:380

commit v4 on v3

--- a/solution.py
+++ b/solution.py
@@ -16,14 +16,14 @@
 HBM = pl.BlockSpec(memory_space=pl.ANY)
 BUNDLE = 4
 LANES = 256
-STEPS = 4
+STEPS = 1
+MIX = True
 ROUND = True
 NEG = -1e30
-TIE1 = 2
+TIE1 = 5
 TIE2 = True
-FETCH = True
+DIRECT = True
 FULL = 57
-FWD = True
 NN = (((1,), (0,)), ((), ()))
 NT = (((1,), (1,)), ((), ()))
 TN = (((0,), (0,)), ((), ()))
@@ -106,6 +106,7 @@
     wide = heads * rows
     two = 2 * rows
     tall = BUNDLE * two
+    keys = mask.shape[0]
     scale = 1.0 / math.sqrt(D)
     power = scale * math.log2(math.e)
     here = here_ref[0]
@@ -267,8 +268,97 @@
 
         loop(bundles, key_side, 0, pairs)
 
-    for g in range(high - low):
-        one_head(g)
+    def interleaved(count):
+        state = [{} for _ in range(count)]
+        steps = range(STEPS)
+
+        def offset(g):
+            return g * keys
+
+        def rows_of(g, j):
+            step = keys // STEPS
+            return slice(offset(g) + j * step, offset(g) + (j + 1) * step)
+
+        def score(g, j):
+            st = state[g]
+            if j == 0:
+                st["q"], st["c"] = stack(q_ref, g), stack(c_ref, g)
+                st["top"] = jnp.full((1, wide), NEG, jnp.float32)
+            at, to = tile(0, j), rows_of(g, j)
+            s = dot(kv[g, 0, at, :], st["q"], NT)
+            s = s + jnp.concatenate([mask[at, :]] * heads, axis=1)
+            s_scr[to, :] = s
+            p_scr[to, :] = dot(kv[g, 1, at, :], st["c"], NT)
+            st["top"] = jnp.maximum(st["top"], jnp.max(s, axis=0, keepdims=True))
+
+        def weigh(g, j):
+            st, to = state[g], rows_of(g, j)
+            e = jnp.exp2((s_scr[to, :] - st["top"]) * power)
+            s_scr[to, :] = e
+            e_scr[to, :] = e.astype(jnp.bfloat16)
+            total = jnp.sum(e, axis=0, keepdims=True)
+            delta = jnp.sum(e * p_scr[to, :], axis=0, keepdims=True)
+            st["total"] = total if j == 0 else st["total"] + total
+            st["delta"] = delta if j == 0 else st["delta"] + delta
+
+        def outputs(g):
+            st = state[g]
+            st["inverse"] = 1.0 / st["total"]
+            st["delta"] = st["delta"] * st["inverse"]
+            acc = dot(kv[g, 1], e_scr[offset(g) : offset(g) + keys, :], TN) * st["inverse"]
+            for h in range(heads):
+                out = jnp.transpose(acc[:, h * rows : (h + 1) * rows])
+                out_scr[g, :, h * D : (h + 1) * D] = out.astype(jnp.bfloat16)
+            send(out_scr, out_ref, g, 0)
+
+        def slope(g, j):
+            st, to = state[g], rows_of(g, j)
+            probs = s_scr[to, :] * st["inverse"]
+            probs_scr[to, :] = probs.astype(jnp.bfloat16)
+            slopes_scr[to, :] = (probs * (p_scr[to, :] - st["delta"])).astype(jnp.bfloat16)
+
+        def query_side(g):
+            grad = dot(kv[g, 0], slopes_scr[offset(g) : offset(g) + keys, :], TN) * scale
+            for h in range(heads):
+                gq_scr[g, :, h * D : (h + 1) * D] = jnp.transpose(grad[:, h * rows : (h + 1) * rows])
+            send(gq_scr, gq_ref, g, 1)
+
+        def key_side(g):
+            st = state[g]
+            span = slice(offset(g), offset(g) + keys)
+            all_v = dot(probs_scr[span, :], st["c"], NN)
+            all_k = dot(slopes_scr[span, :], st["q"], NN) * scale
+            first = (low + g) * two
+            for k in range(pairs):
+                for lane in range(2):
+                    base = 0 if k == 0 else 4 if k == pairs - 1 else 2
+                    ref = parts[min(base + lane, 4)]
+                    slot = 0 if k == 0 else lane if k == pairs - 1 else k - 1
+                    part = slice(k * two + lane * rows, k * two + (lane + 1) * rows)
+                    ref[slot, first : first + rows, :] = all_k[part].astype(ref.dtype)
+                    ref[slot, first + rows : first + two, :] = all_v[part].astype(ref.dtype)
+
+        for j in steps:
+            score(0, j)
+        for g in range(count):
+            for j in steps:
+                weigh(g, j)
+                if g + 1 < count and MIX:
+                    score(g + 1, j)
+            outputs(g)
+            for j in steps:
+                slope(g, j)
+            query_side(g)
+            key_side(g)
+            if g + 1 < count and not MIX:
+                for j in steps:
+                    score(g + 1, j)
+
+    if static:
+        interleaved(high - low)
+    else:
+        for g in range(high - low):
+            one_head(g)
     for copy in copies:
         copy.wait()
 
@@ -281,6 +371,7 @@
     wide = each // D * rows
     lanes = wide if pairs <= BUNDLE else LANES
     keys = pl.cdiv(pairs, BUNDLE) * BUNDLE * 2 * rows
+    many = count if pairs <= BUNDLE else 1
     parts = [
         jax.ShapeDtypeStruct((count, per * 2 * rows, D), dtype)
         for count, dtype in (
@@ -315,11 +406,11 @@
         scratch_shapes=[
             pltpu.VMEM((count, 2, keys, D), jnp.bfloat16),
             pltpu.VMEM((keys, rows), jnp.float32),
-            pltpu.VMEM((keys, lanes), jnp.float32),
-            pltpu.VMEM((keys, lanes), jnp.float32),
-            pltpu.VMEM((keys, lanes), jnp.bfloat16),
-            pltpu.VMEM((keys, wide), jnp.bfloat16),
-            pltpu.VMEM((keys, wide), jnp.bfloat16),
+            pltpu.VMEM((many * keys, lanes), jnp.float32),
+            pltpu.VMEM((many * keys, lanes), jnp.float32),
+            pltpu.VMEM((many * keys, lanes), jnp.bfloat16),
+            pltpu.VMEM((many * keys, wide), jnp.bfloat16),
+            pltpu.VMEM((many * keys, wide), jnp.bfloat16),
             pltpu.VMEM((count, rows, each), jnp.bfloat16),
             pltpu.VMEM((count, rows, each), jnp.float32),
             pltpu.SMEM((1,), jnp.int32),
@@ -327,7 +418,7 @@
             pltpu.SemaphoreType.DMA((2 * count,)),
         ],
         input_output_aliases=aliases,
-        compiler_params=pltpu.CompilerParams(vmem_limit_bytes=(32 if pairs <= BUNDLE else 48) << 20),
+        compiler_params=pltpu.CompilerParams(vmem_limit_bytes=48 << 20),
         cost_estimate=pl.CostEstimate(flops=4 * macs, bytes_accessed=8 << 20, transcendentals=0),
     )(*args)
 
@@ -382,13 +473,16 @@
     def swap(x):
         return lax.ppermute(x, "ctx", [(i, i ^ 1) for i in range(size)])
 
-    def far(block):
-        if not FWD:
-            return [swap(block)] + [up(block, k) for k in range(1, pairs)]
-        own = [block]
-        for _ in range(pairs - 2):
+    def far(block, direct, meanwhile=()):
+        own = [up(block, 1)]
+        for k in range(2, pairs - 1):
+            if direct:
+                own.append(up(block, k))
+                continue
+            if k == 2 and meanwhile:
+                own[0], *meanwhile = lax.optimization_barrier((own[0], *meanwhile))
             own.append(up(own[-1], 1))
-        return [swap(block), *own[1:], up(block, pairs - 1)]
+        return [swap(block), *own, up(block, pairs - 1)], meanwhile
 
     def near(block, first):
         other, *mids, top = first
@@ -402,9 +496,9 @@
         begin += per
     begin = 0
     prev = None
-    first = far(blocks[0])
-    if FETCH:
-        queries, cotangent = fetch(queries, cotangent, blocks[0])
+    queries, cotangent = fetch(queries, cotangent, blocks[0])
+    first, (queries, cotangent) = far(blocks[0], False, (queries, cotangent))
+
     def later(values, event):
         return lax.optimization_barrier((*values, event))[:-1]
 
@@ -416,15 +510,13 @@
         downs = [down(x, k) for k, x in enumerate(mids, 1)]
         finals.extend([mine_0, last, swap(lower), *downs])
 
-    if FETCH:
-        first[1], queries, cotangent = lax.optimization_barrier((first[1], queries, cotangent))
     for c, per in enumerate(SPLIT):
         more = c + 1 < len(SPLIT)
         own, peer = near(blocks[c], first)
         if more:
-            (block,) = later(blocks[c + 1 : c + 2], own[TIE1])
+            (block,) = later(blocks[c + 1 : c + 2], (own + peer)[TIE1])
             blocks[c + 1] = block
-            first = far(block)
+            first, _ = far(block, DIRECT)
         made = None
         for step, heads in enumerate(WORK[c]):
             attended, grad_query, *made = attend(

time: 81.1 us -> 77.5 us (0.956)
  starting transfers between devices: 35.2 us -> 32.7 us
  local copies, waits for them, and re-layouts: 4.01 us -> 2.46 us
  Pallas kernels: 22.8 us -> 24.1 us
  waiting for transfers between devices: 17.9 us -> 17 us
    ppermute x8, waiting for transfers between devices: 8.21 us -> 4.69 us  [up(): lax.ppermute(x, 'ctx', [(i, (i + 2 * k) % size) for i in range(size if RO...]
    ppermute x8, starting transfers between devices: 14.6 us -> 11.6 us  [up(): lax.ppermute(x, 'ctx', [(i, (i + 2 * k) % size) for i in range(size if RO...]
    ppermute x10, waiting for transfers between devices: 1.41 us -> 3.48 us  [swap(): return lax.ppermute(x, 'ctx', [(i, i ^ 1) for i in range(size)])]
    unnamed x12 -> x8, local copies, waits for them, and re-layouts: 4.01 us -> 2.46 us
    pallas_call x2, Pallas kernels: 18.5 us -> 19.8 us  [attend(): pl.pallas_call(functools.partial(attend_kernel, pairs, begin, per, heads,...]
    ppermute x10, starting transfers between devices: 10.7 us -> 12 us  [swap(): return lax.ppermute(x, 'ctx', [(i, i ^ 1) for i in range(size)])]
    ppermute x6, starting transfers between devices: 9.9 us -> 9.07 us  [down(): lax.ppermute(x, 'ctx', [((i + 2 * k) % size, i) for i in range(size if RO...]
  transfers between devices with their start and end apart: 24 -> 24, of which waited for: 7 -> 8; matrix products, arithmetic and copies ran while one was open for 0% -> 0% of each run, Pallas kernels for 25% -> 28%
where the time goes in v4:
time: 77.5 us; the launch traced here: 77.1 us
  starting transfers between devices  32.7 us (42%)
  Pallas kernels  24.1 us (31%)
  waiting for transfers between devices  17 us (22%)
  local copies, waits for them, and re-layouts  2.46 us (3%)
  between operations  0.78 us (1%)
    pallas_call x2, Pallas kernels, attend(): pl.pallas_call(functools.partial(attend_kernel, pairs, begin, per, heads,...  19.8 us
    ppermute x10, starting transfers between devices, swap(): return lax.ppermute(x, 'ctx', [(i, i ^ 1) for i in range(size)])  12 us
    ppermute x8, starting transfers between devices, up(): lax.ppermute(x, 'ctx', [(i, (i + 2 * k) % size) for i in range(size if RO...  11.6 us
    ppermute x6, starting transfers between devices, down(): lax.ppermute(x, 'ctx', [((i + 2 * k) % size, i) for i in range(size if RO...  9.07 us
    ppermute x6, waiting for transfers between devices, down(): lax.ppermute(x, 'ctx', [((i + 2 * k) % size, i) for i in range(size if RO...  8.86 us
    ppermute x8, waiting for transfers between devices, up(): lax.ppermute(x, 'ctx', [(i, (i + 2 * k) % size) for i in range(size if RO...  4.69 us
    ppermute x10, waiting for transfers between devices, swap(): return lax.ppermute(x, 'ctx', [(i, i ^ 1) for i in range(size)])  3.48 us
    pallas_call x2, Pallas kernels, pack(): pl.pallas_call(functools.partial(pack_kernel, begin, per), in_specs=[HBM]...  3.06 us
  transfers between devices with their start and end apart: 24, of which 8 were waited for; matrix products, arithmetic and copies ran while one was open for 0% of the time, Pallas kernels for 28%

profile of v4, /device:TPU:0, one launch (start us, length us, event | category | flops | bytes accessed | tf_op | source)
XLA Modules:
  0.0 77.1 jit_solution(2664081195621555915)
XLA Ops:
  0.6 0.0 copy-start.3
  0.6 1.5 %shard_map.85.after_ref.refs_0_ = bf16[528,128]{1,0:T(8,128)(2,1)} custom-call(bf16[1,128,512]{2,1,0:T(8,128)(2,1)} %k_ref.3, bf16[1,128,512]{2,1,0:T(8,128)(2,1)} %v_ref.3, s32[1,128]{1,0:T(1,128)} %refs_10_.3), custom_call_target="tpu_custom_call" | custom-call | tf_op jit(solution)/shard_map/pallas_call | solution.py:54
  2.2 3.1 %collective-permute-start = (bf16[528,128]{1,0:T(8,128)(2,1)}, bf16[528,128]{1,0:T(8,128)(2,1)S(1)}, u32[]{:S(2)}, u32[]{:S(2)}) collective-permute-start(bf16[528,128]{1,0:T(8,128)(2,1)} %shard_map.85.after_ref.refs_0_), channel_id=1, source_target_pairs={{0,2},{1,3},{2,4},{3,5},{4,6},{5,7},{6,0},{7,1},{8,10},{9,11},{10,... | collective-permute-start | bytes 405512 | tf_op jit(solution)/shard_map/ppermute | solution.py:468
  5.3 1.5 %collective-permute-start.8 = (bf16[528,128]{1,0:T(8,128)(2,1)}, bf16[528,128]{1,0:T(8,128)(2,1)S(1)}, u32[]{:S(2)}, u32[]{:S(2)}) collective-permute-start(bf16[528,128]{1,0:T(8,128)(2,1)} %shard_map.85.after_ref.refs_0_), channel_id=1, source_target_pairs={{0,1},{1,0},{2,3},{3,2},{4,5},{5,4},{6,7},{7,6},{8,9},{9,8},{10,11... | collective-permute-start | bytes 405512 | tf_op jit(solution)/shard_map/ppermute | solution.py:474
  6.8 1.2 %copy-done = bf16[1,128,4096]{2,1,0:T(8,128)(2,1)S(1)} copy-done((bf16[1,128,4096]{2,1,0:T(8,128)(2,1)S(1)}, bf16[1,128,4096]{2,1,0:T(8,128)(2,1)}, u32[]{:S(2)}) %copy-start) | copy-done | bytes 1048600
  8.0 1.2 %copy-done.1 = bf16[1,128,4096]{2,1,0:T(8,128)(2,1)S(1)} copy-done((bf16[1,128,4096]{2,1,0:T(8,128)(2,1)S(1)}, bf16[1,128,4096]{2,1,0:T(8,128)(2,1)}, u32[]{:S(2)}) %copy-start.1) | copy-done | bytes 1048600
  9.2 0.2 shard_map.86
  9.4 1.7 %collective-permute-done.refs_1_ = bf16[528,128]{1,0:T(8,128)(2,1)S(1)} collective-permute-done((bf16[528,128]{1,0:T(8,128)(2,1)}, bf16[528,128]{1,0:T(8,128)(2,1)S(1)}, u32[]{:S(2)}, u32[]{:S(2)}) %collective-permute-start) | collective-permute-done | bytes 135200 | tf_op jit(solution)/shard_map/ppermute | solution.py:468
  11.1 1.5 %collective-permute-start.1 = (bf16[528,128]{1,0:T(8,128)(2,1)S(1)}, bf16[528,128]{1,0:T(8,128)(2,1)S(1)}, u32[]{:S(2)}, u32[]{:S(2)}) collective-permute-start(bf16[528,128]{1,0:T(8,128)(2,1)S(1)} %collective-permute-done.refs_1_), channel_id=1, source_target_pairs={{0,1},{1,0},{2,3},{3,2},{4,5},{5,4},{6,7},{7,6},{8,9},{9,8},{10,11... | collective-permute-start | bytes 405512 | tf_op jit(solution)/shard_map/ppermute | solution.py:474
  12.6 3.8 %collective-permute-start.7 = (bf16[528,128]{1,0:T(8,128)(2,1)}, bf16[528,128]{1,0:T(8,128)(2,1)S(1)}, u32[]{:S(2)}, u32[]{:S(2)}) collective-permute-start(bf16[528,128]{1,0:T(8,128)(2,1)} %shard_map.85.after_ref.refs_0_), channel_id=1, source_target_pairs={{0,6},{1,7},{2,0},{3,1},{4,2},{5,3},{6,4},{7,5},{8,14},{9,15},{10,... | collective-permute-start | bytes 405512 | tf_op jit(solution)/shard_map/ppermute | solution.py:468
  16.4 0.0 collective-permute-done.8.refs_4_
  16.4 0.0 collective-permute-start.10
  16.5 2.9 %collective-permute-done.6.refs_2_ = bf16[528,128]{1,0:T(8,128)(2,1)S(1)} collective-permute-done((bf16[528,128]{1,0:T(8,128)(2,1)S(1)}, bf16[528,128]{1,0:T(8,128)(2,1)S(1)}, u32[]{:S(2)}, u32[]{:S(2)}) %collective-permute-start.6) | collective-permute-done | bytes 135200 | tf_op jit(solution)/shard_map/ppermute | solution.py:468
  19.4 1.5 %collective-permute-start.9 = (bf16[528,128]{1,0:T(8,128)(2,1)S(1)}, bf16[528,128]{1,0:T(8,128)(2,1)S(1)}, u32[]{:S(2)}, u32[]{:S(2)}) collective-permute-start(bf16[528,128]{1,0:T(8,128)(2,1)S(1)} %collective-permute-done.6.refs_2_), channel_id=1, source_target_pairs={{0,1},{1,0},{2,3},{3,2},{4,5},{5,4},{6,7},{7,6},{8,9},{9,8},{10,11... | collective-permute-start | bytes 405512 | tf_op jit(solution)/shard_map/ppermute | solution.py:474
  20.9 1.5 %shard_map.84.refs_0_ = bf16[528,128]{1,0:T(8,128)(2,1)} custom-call(bf16[1,128,512]{2,1,0:T(8,128)(2,1)} %k_ref.3, bf16[1,128,512]{2,1,0:T(8,128)(2,1)} %v_ref.3, s32[1,128]{1,0:T(1,128)} %refs_10_.3), custom_call_target="tpu_custom_call" | custom-call | tf_op jit(solution)/shard_map/pallas_call | solution.py:54
  22.5 0.1 collective-permute-start.5
  22.5 0.1 collective-permute-start.4
  22.6 0.0 collective-permute-done.7.refs_3_
  22.6 1.9 %collective-permute-start.3 = (bf16[528,128]{1,0:T(8,128)(2,1)}, bf16[528,128]{1,0:T(8,128)(2,1)S(1)}, u32[]{:S(2)}, u32[]{:S(2)}) collective-permute-start(bf16[528,128]{1,0:T(8,128)(2,1)} %shard_map.84.refs_0_), channel_id=1, source_target_pairs={{0,2},{1,3},{2,4},{3,5},{4,6},{5,7},{6,0},{7,1},{8,10},{9,11},{10,... | collective-permute-start | bytes 405512 | tf_op jit(solution)/shard_map/ppermute | solution.py:468
  24.6 0.0 collective-permute-done.10.refs_7_
  24.6 0.5 collective-permute-start.2
  25.1 10.4 %shard_map.87 = (bf16[1,128,4096]{2,1,0:T(8,128)(2,1)}, f32[1,128,4096]{2,1,0:T(8,128)}, f32[1,512,128]{2,1,0:T(8,128)S(1)}, f32[1,512,128]{2,1,0:T(8,128)S(1)},...) custom-call(s32[1]{0:T(128)} %bitcast.here_ref, ...), custom_call_target="tpu_custom_call" | custom-call | flops 6442450944 | bytes 8388608 | tf_op jit(solution)/shard_map/pallas_call | solution.py:397
  35.5 0.0 collective-permute-done.5.refs_3_
  35.5 0.0 collective-permute-done.3.refs_1_
  35.5 1.7 %collective-permute-start.11 = (bf16[528,128]{1,0:T(8,128)(2,1)S(1)}, bf16[528,128]{1,0:T(8,128)(2,1)S(1)}, u32[]{:S(2)}, u32[]{:S(2)}) collective-permute-start(bf16[528,128]{1,0:T(8,128)(2,1)S(1)} %collective-permute-done.3.refs_1_), channel_id=1, source_target_pairs={{0,1},{1,0},{2,3},{3,2},{4,5},{5,4},{6,7},{7,6},{8,9},{9,8},{10,11... | collective-permute-start | bytes 405512 | tf_op jit(solution)/shard_map/ppermute | solution.py:474
  37.2 0.4 collective-permute-start.12
  37.6 2.6 %collective-permute-start.13 = (bf16[528,128]{1,0:T(8,128)(2,1)S(1)}, bf16[528,128]{1,0:T(8,128)(2,1)S(1)}, u32[]{:S(2)}, u32[]{:S(2)}) collective-permute-start(bf16[528,128]{1,0:T(8,128)(2,1)S(1)} %collective-permute-done.2.refs_4_), channel_id=1, source_target_pairs={{0,6},{1,7},{2,0},{3,1},{4,2},{5,3},{6,4},{7,5},{8,14},{9,15},{10,... | collective-permute-start | bytes 405512 | tf_op jit(solution)/shard_map/ppermute | solution.py:468
  40.3 1.3 %collective-permute-start.14 = (bf16[2,512,128]{2,1,0:T(8,128)(2,1)S(1)}, bf16[2,512,128]{2,1,0:T(8,128)(2,1)S(1)}, u32[]{:S(2)}, u32[]{:S(2)}) collective-permute-start(bf16[2,512,128]{2,1,0:T(8,128)(2,1)S(1)} %get-tuple-element.53), channel_id=1, source_target_pairs={{0,1},{1,0},{2,3},{3,2},{4,5},{5,4},{6,7},{7,6},{8,9},{9,8},{10,11... | collective-permute-start | bytes 786440 | tf_op jit(solution)/shard_map/ppermute | solution.py:474
  41.6 0.0 collective-permute-start.15
  41.6 0.6 collective-permute-done.11.refs_5_
  42.1 2.9 %collective-permute-done.12.refs_6_ = bf16[528,128]{1,0:T(8,128)(2,1)S(1)} collective-permute-done((bf16[528,128]{1,0:T(8,128)(2,1)S(1)}, bf16[528,128]{1,0:T(8,128)(2,1)S(1)}, u32[]{:S(2)}, u32[]{:S(2)}) %collective-permute-start.12) | collective-permute-done | bytes 135200 | tf_op jit(solution)/shard_map/ppermute | solution.py:474
  45.0 0.0 collective-permute-done.13.refs_7_
  45.1 9.4 %shard_map.88 = (bf16[1,128,4096]{2,1,0:T(8,128)(2,1)}, f32[1,128,4096]{2,1,0:T(8,128)}, f32[1,512,128]{2,1,0:T(8,128)S(1)}, f32[1,512,128]{2,1,0:T(8,128)S(1)},...) custom-call(s32[1]{0:T(128)} %bitcast.here_ref, ...), custom_call_target="tpu_custom_call", output_to_operand_aliasing={{0}: (12, {}), {1}: (13, {})} | custom-call | flops 6442450944 | bytes 8388608 | tf_op jit(solution)/shard_map/pallas_call | solution.py:397
  54.5 0.6 collective-permute-start.19
  55.1 0.9 %collective-permute-start.20 = (bf16[2,512,128]{2,1,0:T(8,128)(2,1)S(1)}, bf16[2,512,128]{2,1,0:T(8,128)(2,1)S(1)}, u32[]{:S(2)}, u32[]{:S(2)}) collective-permute-start(bf16[2,512,128]{2,1,0:T(8,128)(2,1)S(1)} %get-tuple-element.65), channel_id=1, source_target_pairs={{0,1},{1,0},{2,3},{3,2},{4,5},{5,4},{6,7},{7,6},{8,9},{9,8},{10,11... | collective-permute-start | bytes 786440 | tf_op jit(solution)/shard_map/ppermute | solution.py:474
  56.1 0.1 shard_map.89
  56.1 1.2 %collective-permute-start.16 = (bf16[512,128]{1,0:T(8,128)(2,1)S(1)}, bf16[512,128]{1,0:T(8,128)(2,1)S(1)}, u32[]{:S(2)}, u32[]{:S(2)}) collective-permute-start(bf16[512,128]{1,0:T(8,128)(2,1)S(1)} %get-tuple-element.60), channel_id=1, source_target_pairs={{0,1},{1,0},{2,3},{3,2},{4,5},{5,4},{6,7},{7,6},{8,9},{9,8},{10,11... | collective-permute-start | bytes 393224 | tf_op jit(solution)/shard_map/ppermute | solution.py:474
  57.3 3.3 %collective-permute-start.17 = (bf16[512,128]{1,0:T(8,128)(2,1)S(1)}, bf16[512,128]{1,0:T(8,128)(2,1)S(1)}, u32[]{:S(2)}, u32[]{:S(2)}) collective-permute-start(bf16[512,128]{1,0:T(8,128)(2,1)S(1)} %get-tuple-element.61), channel_id=1, source_target_pairs={{2,0},{3,1},{4,2},{5,3},{6,4},{7,5},{0,6},{1,7},{10,8},{11,9},{12,... | collective-permute-start | bytes 393224 | tf_op jit(solution)/shard_map/ppermute | solution.py:471
  60.6 0.2 collective-permute-start.18
  60.8 4.5 %collective-permute-done.19.last_ref.refs_6_ = bf16[2,512,128]{2,1,0:T(8,128)(2,1)S(1)} collective-permute-done((bf16[2,512,128]{2,1,0:T(8,128)(2,1)S(1)}, bf16[2,512,128]{2,1,0:T(8,128)(2,1)S(1)}, u32[]{:S(2)}, u32[]{:S(2)}) %collective-permute-start.19) | collective-permute-done | bytes 262176 | tf_op jit(solution)/shard_map/ppermute | solution.py:471
  65.3 0.1 shard_map.90
  65.4 1.5 %collective-permute-start.21 = (bf16[512,128]{1,0:T(8,128)(2,1)S(1)}, bf16[512,128]{1,0:T(8,128)(2,1)S(1)}, u32[]{:S(2)}, u32[]{:S(2)}) collective-permute-start(bf16[512,128]{1,0:T(8,128)(2,1)S(1)} %get-tuple-element.67), channel_id=1, source_target_pairs={{0,1},{1,0},{2,3},{3,2},{4,5},{5,4},{6,7},{7,6},{8,9},{9,8},{10,11... | collective-permute-start | bytes 393224 | tf_op jit(solution)/shard_map/ppermute | solution.py:474
  66.9 0.3 collective-permute-start.22
  67.2 4.7 %collective-permute-start.23 = (bf16[512,128]{1,0:T(8,128)(2,1)S(1)}, bf16[512,128]{1,0:T(8,128)(2,1)S(1)}, u32[]{:S(2)}, u32[]{:S(2)}) collective-permute-start(bf16[512,128]{1,0:T(8,128)(2,1)S(1)} %get-tuple-element.69), channel_id=1, source_target_pairs={{4,0},{5,1},{6,2},{7,3},{0,4},{1,5},{2,6},{3,7},{12,8},{13,9},{14,... | collective-permute-start | bytes 393224 | tf_op jit(solution)/shard_map/ppermute | solution.py:471
  71.9 0.4 collective-permute-done.18.refs_4_
  72.2 1.3 %collective-permute-done.22.refs_8_ = bf16[512,128]{1,0:T(8,128)(2,1)S(1)} collective-permute-done((bf16[512,128]{1,0:T(8,128)(2,1)S(1)}, bf16[512,128]{1,0:T(8,128)(2,1)S(1)}, u32[]{:S(2)}, u32[]{:S(2)}) %collective-permute-start.22) | collective-permute-done | bytes 131104 | tf_op jit(solution)/shard_map/ppermute | solution.py:471
  73.6 2.6 %collective-permute-done.23.refs_9_ = bf16[512,128]{1,0:T(8,128)(2,1)S(1)} collective-permute-done((bf16[512,128]{1,0:T(8,128)(2,1)S(1)}, bf16[512,128]{1,0:T(8,128)(2,1)S(1)}, u32[]{:S(2)}, u32[]{:S(2)}) %collective-permute-start.23) | collective-permute-done | bytes 131104 | tf_op jit(solution)/shard_map/ppermute | solution.py:471
  76.2 0.9 %shard_map.91 = (f32[1,128,512]{2,1,0:T(8,128)}, f32[1,128,512]{2,1,0:T(8,128)}) custom-call(f32[1,512,128]{2,1,0:T(8,128)S(1)} %get-tuple-element.44.refs_0_, bf16[2,512,128]{2,1,0:T(8,128)(2,1)S(1)} %collective-permute-done.15.last_ref.refs_1_, bf16[512,128]{1,0:T(8,128)(2,1)S(1)} %collective-permute-done.16.refs_2_, ...), custom_call_target="tpu_custom_call" | custom-call | tf_op jit(solution)/shard_map/pallas_call | solution.py:536
  (16 shorter events, 0.0 us)
Async XLA Ops:
  0.6 24.4 %copy-start.3 = (s32[1,128]{1,0:T(1,128)S(1)}, s32[1,128]{1,0:T(1,128)}, u32[]{:S(2)}) copy-start(s32[1,128]{1,0:T(1,128)} %refs_10_.3) | copy-start | bytes 1540
  2.2 8.9 %collective-permute-start = (bf16[528,128]{1,0:T(8,128)(2,1)}, bf16[528,128]{1,0:T(8,128)(2,1)S(1)}, u32[]{:S(2)}, u32[]{:S(2)}) collective-permute-start(bf16[528,128]{1,0:T(8,128)(2,1)} %shard_map.85.after_ref.refs_0_), channel_id=1, source_target_pairs={{0,2},{1,3},{2,4},{3,5},{4,6},{5,7},{6,0},{7,1},{8,10},{9,11},{10,... | collective-permute-start | bytes 405512 | tf_op jit(solution)/shard_map/ppermute | solution.py:468
  5.3 11.2 %collective-permute-start.8 = (bf16[528,128]{1,0:T(8,128)(2,1)}, bf16[528,128]{1,0:T(8,128)(2,1)S(1)}, u32[]{:S(2)}, u32[]{:S(2)}) collective-permute-start(bf16[528,128]{1,0:T(8,128)(2,1)} %shard_map.85.after_ref.refs_0_), channel_id=1, source_target_pairs={{0,1},{1,0},{2,3},{3,2},{4,5},{5,4},{6,7},{7,6},{8,9},{9,8},{10,11... | collective-permute-start | bytes 405512 | tf_op jit(solution)/shard_map/ppermute | solution.py:474
  6.8 1.2 %copy-start = (bf16[1,128,4096]{2,1,0:T(8,128)(2,1)S(1)}, bf16[1,128,4096]{2,1,0:T(8,128)(2,1)}, u32[]{:S(2)}) copy-start(bf16[1,128,4096]{2,1,0:T(8,128)(2,1)} %q_ref.1) | copy-start | bytes 3145732
  8.0 1.2 %copy-start.1 = (bf16[1,128,4096]{2,1,0:T(8,128)(2,1)S(1)}, bf16[1,128,4096]{2,1,0:T(8,128)(2,1)}, u32[]{:S(2)}) copy-start(bf16[1,128,4096]{2,1,0:T(8,128)(2,1)} %c_ref.1) | copy-start | bytes 3145732
  11.1 8.3 %collective-permute-start.6 = (bf16[528,128]{1,0:T(8,128)(2,1)S(1)}, bf16[528,128]{1,0:T(8,128)(2,1)S(1)}, u32[]{:S(2)}, u32[]{:S(2)}) collective-permute-start(bf16[528,128]{1,0:T(8,128)(2,1)S(1)} %collective-permute-done.refs_1_), channel_id=1, source_target_pairs={{0,2},{1,3},{2,4},{3,5},{4,6},{5,7},{6,0},{7,1},{8,10},{9,11},{10,... | collective-permute-start | bytes 405512 | tf_op jit(solution)/shard_map/ppermute | solution.py:468
  11.1 11.4 %collective-permute-start.1 = (bf16[528,128]{1,0:T(8,128)(2,1)S(1)}, bf16[528,128]{1,0:T(8,128)(2,1)S(1)}, u32[]{:S(2)}, u32[]{:S(2)}) collective-permute-start(bf16[528,128]{1,0:T(8,128)(2,1)S(1)} %collective-permute-done.refs_1_), channel_id=1, source_target_pairs={{0,1},{1,0},{2,3},{3,2},{4,5},{5,4},{6,7},{7,6},{8,9},{9,8},{10,11... | collective-permute-start | bytes 405512 | tf_op jit(solution)/shard_map/ppermute | solution.py:474
  12.6 10.0 %collective-permute-start.7 = (bf16[528,128]{1,0:T(8,128)(2,1)}, bf16[528,128]{1,0:T(8,128)(2,1)S(1)}, u32[]{:S(2)}, u32[]{:S(2)}) collective-permute-start(bf16[528,128]{1,0:T(8,128)(2,1)} %shard_map.85.after_ref.refs_0_), channel_id=1, source_target_pairs={{0,6},{1,7},{2,0},{3,1},{4,2},{5,3},{6,4},{7,5},{8,14},{9,15},{10,... | collective-permute-start | bytes 405512 | tf_op jit(solution)/shard_map/ppermute | solution.py:468
  16.4 8.1 %collective-permute-start.10 = (bf16[528,128]{1,0:T(8,128)(2,1)S(1)}, bf16[528,128]{1,0:T(8,128)(2,1)S(1)}, u32[]{:S(2)}, u32[]{:S(2)}) collective-permute-start(bf16[528,128]{1,0:T(8,128)(2,1)S(1)} %collective-permute-done.8.refs_4_), channel_id=1, source_target_pairs={{0,6},{1,7},{2,0},{3,1},{4,2},{5,3},{6,4},{7,5},{8,14},{9,15},{10,... | collective-permute-start | bytes 405512 | tf_op jit(solution)/shard_map/ppermute | solution.py:468
  19.4 5.7 %collective-permute-start.9 = (bf16[528,128]{1,0:T(8,128)(2,1)S(1)}, bf16[528,128]{1,0:T(8,128)(2,1)S(1)}, u32[]{:S(2)}, u32[]{:S(2)}) collective-permute-start(bf16[528,128]{1,0:T(8,128)(2,1)S(1)} %collective-permute-done.6.refs_2_), channel_id=1, source_target_pairs={{0,1},{1,0},{2,3},{3,2},{4,5},{5,4},{6,7},{7,6},{8,9},{9,8},{10,11... | collective-permute-start | bytes 405512 | tf_op jit(solution)/shard_map/ppermute | solution.py:474
  22.5 13.0 %collective-permute-start.5 = (bf16[528,128]{1,0:T(8,128)(2,1)}, bf16[528,128]{1,0:T(8,128)(2,1)S(1)}, u32[]{:S(2)}, u32[]{:S(2)}) collective-permute-start(bf16[528,128]{1,0:T(8,128)(2,1)} %shard_map.84.refs_0_), channel_id=1, source_target_pairs={{0,6},{1,7},{2,0},{3,1},{4,2},{5,3},{6,4},{7,5},{8,14},{9,15},{10,... | collective-permute-start | bytes 405512 | tf_op jit(solution)/shard_map/ppermute | solution.py:468
  22.5 13.0 %collective-permute-start.4 = (bf16[528,128]{1,0:T(8,128)(2,1)}, bf16[528,128]{1,0:T(8,128)(2,1)S(1)}, u32[]{:S(2)}, u32[]{:S(2)}) collective-permute-start(bf16[528,128]{1,0:T(8,128)(2,1)} %shard_map.84.refs_0_), channel_id=1, source_target_pairs={{0,4},{1,5},{2,6},{3,7},{4,0},{5,1},{6,2},{7,3},{8,12},{9,13},{10,... | collective-permute-start | bytes 405512 | tf_op jit(solution)/shard_map/ppermute | solution.py:468
  22.6 12.9 %collective-permute-start.3 = (bf16[528,128]{1,0:T(8,128)(2,1)}, bf16[528,128]{1,0:T(8,128)(2,1)S(1)}, u32[]{:S(2)}, u32[]{:S(2)}) collective-permute-start(bf16[528,128]{1,0:T(8,128)(2,1)} %shard_map.84.refs_0_), channel_id=1, source_target_pairs={{0,2},{1,3},{2,4},{3,5},{4,6},{5,7},{6,0},{7,1},{8,10},{9,11},{10,... | collective-permute-start | bytes 405512 | tf_op jit(solution)/shard_map/ppermute | solution.py:468
  24.6 11.0 %collective-permute-start.2 = (bf16[528,128]{1,0:T(8,128)(2,1)}, bf16[528,128]{1,0:T(8,128)(2,1)S(1)}, u32[]{:S(2)}, u32[]{:S(2)}) collective-permute-start(bf16[528,128]{1,0:T(8,128)(2,1)} %shard_map.84.refs_0_), channel_id=1, source_target_pairs={{0,1},{1,0},{2,3},{3,2},{4,5},{5,4},{6,7},{7,6},{8,9},{9,8},{10,11... | collective-permute-start | bytes 405512 | tf_op jit(solution)/shard_map/ppermute | solution.py:474
  25.1 20.0 %copy-start.2 = (bf16[528,128]{1,0:T(8,128)(2,1)S(1)}, bf16[528,128]{1,0:T(8,128)(2,1)}, u32[]{:S(2)}) copy-start(bf16[528,128]{1,0:T(8,128)(2,1)} %shard_map.84.refs_0_) | copy-start | bytes 405508
  35.5 6.6 %collective-permute-start.11 = (bf16[528,128]{1,0:T(8,128)(2,1)S(1)}, bf16[528,128]{1,0:T(8,128)(2,1)S(1)}, u32[]{:S(2)}, u32[]{:S(2)}) collective-permute-start(bf16[528,128]{1,0:T(8,128)(2,1)S(1)} %collective-permute-done.3.refs_1_), channel_id=1, source_target_pairs={{0,1},{1,0},{2,3},{3,2},{4,5},{5,4},{6,7},{7,6},{8,9},{9,8},{10,11... | collective-permute-start | bytes 405512 | tf_op jit(solution)/shard_map/ppermute | solution.py:474
  37.2 7.8 %collective-permute-start.12 = (bf16[528,128]{1,0:T(8,128)(2,1)S(1)}, bf16[528,128]{1,0:T(8,128)(2,1)S(1)}, u32[]{:S(2)}, u32[]{:S(2)}) collective-permute-start(bf16[528,128]{1,0:T(8,128)(2,1)S(1)} %collective-permute-done.4.refs_2_), channel_id=1, source_target_pairs={{0,1},{1,0},{2,3},{3,2},{4,5},{5,4},{6,7},{7,6},{8,9},{9,8},{10,11... | collective-permute-start | bytes 405512 | tf_op jit(solution)/shard_map/ppermute | solution.py:474
  37.6 7.4 %collective-permute-start.13 = (bf16[528,128]{1,0:T(8,128)(2,1)S(1)}, bf16[528,128]{1,0:T(8,128)(2,1)S(1)}, u32[]{:S(2)}, u32[]{:S(2)}) collective-permute-start(bf16[528,128]{1,0:T(8,128)(2,1)S(1)} %collective-permute-done.2.refs_4_), channel_id=1, source_target_pairs={{0,6},{1,7},{2,0},{3,1},{4,2},{5,3},{6,4},{7,5},{8,14},{9,15},{10,... | collective-permute-start | bytes 405512 | tf_op jit(solution)/shard_map/ppermute | solution.py:468
  40.3 15.8 %collective-permute-start.14 = (bf16[2,512,128]{2,1,0:T(8,128)(2,1)S(1)}, bf16[2,512,128]{2,1,0:T(8,128)(2,1)S(1)}, u32[]{:S(2)}, u32[]{:S(2)}) collective-permute-start(bf16[2,512,128]{2,1,0:T(8,128)(2,1)S(1)} %get-tuple-element.53), channel_id=1, source_target_pairs={{0,1},{1,0},{2,3},{3,2},{4,5},{5,4},{6,7},{7,6},{8,9},{9,8},{10,11... | collective-permute-start | bytes 786440 | tf_op jit(solution)/shard_map/ppermute | solution.py:474
  41.6 14.5 %collective-permute-start.15 = (bf16[2,512,128]{2,1,0:T(8,128)(2,1)S(1)}, bf16[2,512,128]{2,1,0:T(8,128)(2,1)S(1)}, u32[]{:S(2)}, u32[]{:S(2)}) collective-permute-start(bf16[2,512,128]{2,1,0:T(8,128)(2,1)S(1)} %get-tuple-element.54), channel_id=1, source_target_pairs={{6,0},{7,1},{0,2},{1,3},{2,4},{3,5},{4,6},{5,7},{14,8},{15,9},{8,1... | collective-permute-start | bytes 786440 | tf_op jit(solution)/shard_map/ppermute | solution.py:471
  54.5 10.8 %collective-permute-start.19 = (bf16[2,512,128]{2,1,0:T(8,128)(2,1)S(1)}, bf16[2,512,128]{2,1,0:T(8,128)(2,1)S(1)}, u32[]{:S(2)}, u32[]{:S(2)}) collective-permute-start(bf16[2,512,128]{2,1,0:T(8,128)(2,1)S(1)} %get-tuple-element.63), channel_id=1, source_target_pairs={{6,0},{7,1},{0,2},{1,3},{2,4},{3,5},{4,6},{5,7},{14,8},{15,9},{8,1... | collective-permute-start | bytes 786440 | tf_op jit(solution)/shard_map/ppermute | solution.py:471
  55.1 10.2 %collective-permute-start.20 = (bf16[2,512,128]{2,1,0:T(8,128)(2,1)S(1)}, bf16[2,512,128]{2,1,0:T(8,128)(2,1)S(1)}, u32[]{:S(2)}, u32[]{:S(2)}) collective-permute-start(bf16[2,512,128]{2,1,0:T(8,128)(2,1)S(1)} %get-tuple-element.65), channel_id=1, source_target_pairs={{0,1},{1,0},{2,3},{3,2},{4,5},{5,4},{6,7},{7,6},{8,9},{9,8},{10,11... | collective-permute-start | bytes 786440 | tf_op jit(solution)/shard_map/ppermute | solution.py:474
  56.1 11.0 %collective-permute-start.16 = (bf16[512,128]{1,0:T(8,128)(2,1)S(1)}, bf16[512,128]{1,0:T(8,128)(2,1)S(1)}, u32[]{:S(2)}, u32[]{:S(2)}) collective-permute-start(bf16[512,128]{1,0:T(8,128)(2,1)S(1)} %get-tuple-element.60), channel_id=1, source_target_pairs={{0,1},{1,0},{2,3},{3,2},{4,5},{5,4},{6,7},{7,6},{8,9},{9,8},{10,11... | collective-permute-start | bytes 393224 | tf_op jit(solution)/shard_map/ppermute | solution.py:474
  57.3 14.6 %collective-permute-start.17 = (bf16[512,128]{1,0:T(8,128)(2,1)S(1)}, bf16[512,128]{1,0:T(8,128)(2,1)S(1)}, u32[]{:S(2)}, u32[]{:S(2)}) collective-permute-start(bf16[512,128]{1,0:T(8,128)(2,1)S(1)} %get-tuple-element.61), channel_id=1, source_target_pairs={{2,0},{3,1},{4,2},{5,3},{6,4},{7,5},{0,6},{1,7},{10,8},{11,9},{12,... | collective-permute-start | bytes 393224 | tf_op jit(solution)/shard_map/ppermute | solution.py:471
  60.6 11.7 %collective-permute-start.18 = (bf16[512,128]{1,0:T(8,128)(2,1)S(1)}, bf16[512,128]{1,0:T(8,128)(2,1)S(1)}, u32[]{:S(2)}, u32[]{:S(2)}) collective-permute-start(bf16[512,128]{1,0:T(8,128)(2,1)S(1)} %get-tuple-element.62), channel_id=1, source_target_pairs={{4,0},{5,1},{6,2},{7,3},{0,4},{1,5},{2,6},{3,7},{12,8},{13,9},{14,... | collective-permute-start | bytes 393224 | tf_op jit(solution)/shard_map/ppermute | solution.py:471
  65.4 6.9 %collective-permute-start.21 = (bf16[512,128]{1,0:T(8,128)(2,1)S(1)}, bf16[512,128]{1,0:T(8,128)(2,1)S(1)}, u32[]{:S(2)}, u32[]{:S(2)}) collective-permute-start(bf16[512,128]{1,0:T(8,128)(2,1)S(1)} %get-tuple-element.67), channel_id=1, source_target_pairs={{0,1},{1,0},{2,3},{3,2},{4,5},{5,4},{6,7},{7,6},{8,9},{9,8},{10,11... | collective-permute-start | bytes 393224 | tf_op jit(solution)/shard_map/ppermute | solution.py:474
  66.9 6.7 %collective-permute-start.22 = (bf16[512,128]{1,0:T(8,128)(2,1)S(1)}, bf16[512,128]{1,0:T(8,128)(2,1)S(1)}, u32[]{:S(2)}, u32[]{:S(2)}) collective-permute-start(bf16[512,128]{1,0:T(8,128)(2,1)S(1)} %get-tuple-element.68), channel_id=1, source_target_pairs={{2,0},{3,1},{4,2},{5,3},{6,4},{7,5},{0,6},{1,7},{10,8},{11,9},{12,... | collective-permute-start | bytes 393224 | tf_op jit(solution)/shard_map/ppermute | solution.py:471
  67.2 9.0 %collective-permute-start.23 = (bf16[512,128]{1,0:T(8,128)(2,1)S(1)}, bf16[512,128]{1,0:T(8,128)(2,1)S(1)}, u32[]{:S(2)}, u32[]{:S(2)}) collective-permute-start(bf16[512,128]{1,0:T(8,128)(2,1)S(1)} %get-tuple-element.69), channel_id=1, source_target_pairs={{4,0},{5,1},{6,2},{7,3},{0,4},{1,5},{2,6},{3,7},{12,8},{13,9},{14,... | collective-permute-start | bytes 393224 | tf_op jit(solution)/shard_map/ppermute | solution.py:471

commit v5 on v4

--- a/solution.py
+++ b/solution.py
@@ -11,17 +11,17 @@
 KV = 4
 D = 128
 SPLIT = (2, 2)
-WORK = (((0, 2),), ((0, 2),))
 VMEM = pl.BlockSpec(memory_space=pltpu.VMEM)
 HBM = pl.BlockSpec(memory_space=pl.ANY)
 BUNDLE = 4
 LANES = 256
 STEPS = 1
-MIX = True
+ORDER = 0
 ROUND = True
 NEG = -1e30
 TIE1 = 5
 TIE2 = True
+TIE3 = False
 DIRECT = True
 FULL = 57
 NN = (((1,), (0,)), ((), ()))
@@ -33,32 +33,37 @@
     return lax.dot_general(a, b, dims, preferred_element_type=jnp.float32)
 
 
-def pack_kernel(begin, per, k_ref, v_ref, s_ref, out, seg, sems):
+def pack_kernel(k_ref, v_ref, s_ref, *refs):
+    *outs, seg, sems = refs
     rows = k_ref.shape[1]
     copies = [pltpu.make_async_copy(s_ref, seg, sems.at[0])]
-    for g in range(per):
-        for part, ref in enumerate((k_ref, v_ref)):
-            src = ref.at[0, :, pl.ds((begin + g) * D, D)]
-            to = out.at[pl.ds((2 * g + part) * rows, rows)]
-            copies.append(pltpu.make_async_copy(src, to, sems.at[1 + 2 * g + part]))
+    head = 0
+    for per, out in zip(SPLIT, outs):
+        for g in range(per):
+            for part, ref in enumerate((k_ref, v_ref)):
+                src = ref.at[0, :, pl.ds(head * D, D)]
+                to = out.at[pl.ds((2 * g + part) * rows, rows)]
+                copies.append(pltpu.make_async_copy(src, to, sems.at[1 + 2 * head + part]))
+            head += 1
     for copy in copies:
         copy.start()
     for copy in copies:
         copy.wait()
-    row = jnp.broadcast_to(seg[...].astype(jnp.float32), (16, rows))
-    out[2 * per * rows :, :] = row.astype(jnp.bfloat16)
-
-
-def pack(begin, per, key_matrix, value_matrix, segment):
+    row = jnp.broadcast_to(seg[...].astype(jnp.float32), (16, rows)).astype(jnp.bfloat16)
+    for per, out in zip(SPLIT, outs):
+        out[2 * per * rows :, :] = row
+
+
+def pack(key_matrix, value_matrix, segment):
     rows = key_matrix.shape[1]
     return pl.pallas_call(
-        functools.partial(pack_kernel, begin, per),
+        pack_kernel,
         in_specs=[HBM] * 3,
-        out_specs=VMEM,
-        out_shape=jax.ShapeDtypeStruct((per * 2 * rows + 16, D), jnp.bfloat16),
+        out_specs=[VMEM] * len(SPLIT),
+        out_shape=[jax.ShapeDtypeStruct((per * 2 * rows + 16, D), jnp.bfloat16) for per in SPLIT],
         scratch_shapes=[
             pltpu.VMEM(segment.shape, jnp.int32),
-            pltpu.SemaphoreType.DMA((2 * per + 1,)),
+            pltpu.SemaphoreType.DMA((2 * KV + 1,)),
         ],
         compiler_params=pltpu.CompilerParams(vmem_limit_bytes=FULL << 20),
     )(key_matrix, value_matrix, segment)
@@ -273,7 +278,7 @@
         steps = range(STEPS)
 
         def offset(g):
-            return g * keys
+            return g % 2 * keys
 
         def rows_of(g, j):
             step = keys // STEPS
@@ -341,18 +346,29 @@
         for j in steps:
             score(0, j)
         for g in range(count):
-            for j in steps:
-                weigh(g, j)
-                if g + 1 < count and MIX:
+            more = g + 1 < count
+            if g == 0 or ORDER == 0:
+                for j in steps:
+                    weigh(g, j)
+                    if more:
+                        score(g + 1, j)
+            elif more:
+                for j in steps:
                     score(g + 1, j)
             outputs(g)
             for j in steps:
                 slope(g, j)
+            if ORDER == 1 and more:
+                for j in steps:
+                    weigh(g + 1, j)
             query_side(g)
+            if ORDER == 2 and more:
+                for j in steps:
+                    weigh(g + 1, j)
             key_side(g)
-            if g + 1 < count and not MIX:
+            if ORDER == 3 and more:
                 for j in steps:
-                    score(g + 1, j)
+                    weigh(g + 1, j)
 
     if static:
         interleaved(high - low)
@@ -371,7 +387,7 @@
     wide = each // D * rows
     lanes = wide if pairs <= BUNDLE else LANES
     keys = pl.cdiv(pairs, BUNDLE) * BUNDLE * 2 * rows
-    many = count if pairs <= BUNDLE else 1
+    many = min(count, 2) if pairs <= BUNDLE else 1
     parts = [
         jax.ShapeDtypeStruct((count, per * 2 * rows, D), dtype)
         for count, dtype in (
@@ -489,11 +505,7 @@
         return [block, *mids, top], [other, *(swap(x) for x in mids), up(other, pairs - 1)]
 
     finals = []
-    blocks = []
-    begin = 0
-    for per in SPLIT:
-        blocks.append(pack(begin, per, key_matrix, value_matrix, segment))
-        begin += per
+    blocks = list(pack(key_matrix, value_matrix, segment))
     begin = 0
     prev = None
     queries, cotangent = fetch(queries, cotangent, blocks[0])
@@ -517,18 +529,17 @@
             (block,) = later(blocks[c + 1 : c + 2], (own + peer)[TIE1])
             blocks[c + 1] = block
             first, _ = far(block, DIRECT)
-        made = None
-        for step, heads in enumerate(WORK[c]):
-            attended, grad_query, *made = attend(
-                begin, per, heads, here, own, peer, queries, cotangent, segment, prev, made
-            )
-            prev = (attended, grad_query)
-            if step == 0 and waiting is not None:
-                waiting[3], waiting[4] = later(waiting[3:], made[0])
-                finish(waiting)
-                waiting = None
-            if step == 0 and more and TIE2:
-                first = list(later(first, made[0]))
+        if waiting is not None:
+            lower = finish(waiting)
+            waiting = None
+            if TIE3:
+                prev = later(prev, lower)
+        attended, grad_query, *made = attend(
+            begin, per, (0, per), here, own, peer, queries, cotangent, segment, prev, None
+        )
+        prev = (attended, grad_query)
+        if more and TIE2:
+            first = list(later(first, made[0]))
         begin += per
         mine_0, theirs_0, mine_mid, theirs_mid, last = made
         waiting = [mine_0, theirs_0, mine_mid, swap(theirs_mid), down(last, pairs - 1)]

time: 77.5 us -> 77.8 us (level)
  starting transfers between devices: 32.7 us -> 34.5 us
  Pallas kernels: 24.1 us -> 22.7 us
    pallas_call x2 -> x1, Pallas kernels: 3.06 us -> 1.68 us  [pack(): pl.pallas_call(pack_kernel, in_specs=[HBM] * 3, out_specs=[VMEM] * len(SP...]
    ppermute x10, waiting for transfers between devices: 3.48 us -> 2.28 us  [swap(): return lax.ppermute(x, 'ctx', [(i, i ^ 1) for i in range(size)])]
    ppermute x8, waiting for transfers between devices: 4.69 us -> 5.82 us  [up(): lax.ppermute(x, 'ctx', [(i, (i + 2 * k) % size) for i in range(size if RO...]
    ppermute x10, starting transfers between devices: 12 us -> 13 us  [swap(): return lax.ppermute(x, 'ctx', [(i, i ^ 1) for i in range(size)])]
    ppermute x8, starting transfers between devices: 11.6 us -> 12.5 us  [up(): lax.ppermute(x, 'ctx', [(i, (i + 2 * k) % size) for i in range(size if RO...]
  transfers between devices with their start and end apart: 24 -> 24, of which waited for: 8 -> 9; matrix products, arithmetic and copies ran while one was open for 0% -> 0% of each run, Pallas kernels for 28% -> 26%
where the time goes in v5:
time: 77.8 us; the launch traced here: 77.5 us
  starting transfers between devices  34.5 us (44%)
  Pallas kernels  22.7 us (29%)
  waiting for transfers between devices  17.1 us (22%)
  local copies, waits for them, and re-layouts  2.46 us (3%)
    pallas_call x2, Pallas kernels, attend(): pl.pallas_call(functools.partial(attend_kernel, pairs, begin, per, heads,...  19.8 us
    ppermute x10, starting transfers between devices, swap(): return lax.ppermute(x, 'ctx', [(i, i ^ 1) for i in range(size)])  13 us
    ppermute x8, starting transfers between devices, up(): lax.ppermute(x, 'ctx', [(i, (i + 2 * k) % size) for i in range(size if RO...  12.5 us
    ppermute x6, waiting for transfers between devices, down(): lax.ppermute(x, 'ctx', [((i + 2 * k) % size, i) for i in range(size if RO...  9 us
    ppermute x6, starting transfers between devices, down(): lax.ppermute(x, 'ctx', [((i + 2 * k) % size, i) for i in range(size if RO...  8.99 us
    ppermute x8, waiting for transfers between devices, up(): lax.ppermute(x, 'ctx', [(i, (i + 2 * k) % size) for i in range(size if RO...  5.82 us
    unnamed x8, local copies, waits for them, and re-layouts  2.46 us
    ppermute x10, waiting for transfers between devices, swap(): return lax.ppermute(x, 'ctx', [(i, i ^ 1) for i in range(size)])  2.28 us
  transfers between devices with their start and end apart: 24, of which 9 were waited for; matrix products, arithmetic and copies ran while one was open for 0% of the time, Pallas kernels for 26%

profile of v5, /device:TPU:0, one launch (start us, length us, event | category | flops | bytes accessed | tf_op | source)
XLA Modules:
  0.0 77.5 jit_solution(16915611204005372787)
XLA Ops:
  0.6 1.7 %shard_map.84 = (bf16[528,128]{1,0:T(8,128)(2,1)}, bf16[528,128]{1,0:T(8,128)(2,1)}) custom-call(bf16[1,128,512]{2,1,0:T(8,128)(2,1)} %k_ref.1, bf16[1,128,512]{2,1,0:T(8,128)(2,1)} %v_ref.1, s32[1,128]{1,0:T(1,128)} %refs_10_.3), custom_call_target="tpu_custom_call" | custom-call | tf_op jit(solution)/shard_map/pallas_call | solution.py:59
  2.3 3.1 %collective-permute-start = (bf16[528,128]{1,0:T(8,128)(2,1)}, bf16[528,128]{1,0:T(8,128)(2,1)S(1)}, u32[]{:S(2)}, u32[]{:S(2)}) collective-permute-start(bf16[528,128]{1,0:T(8,128)(2,1)} %get-tuple-element.39.after_ref.refs_0_), channel_id=1, source_target_pairs={{0,2},{1,3},{2,4},{3,5},{4,6},{5,7},{6,0},{7,1},{8,10},{9,11},{10,... | collective-permute-start | bytes 405512 | tf_op jit(solution)/shard_map/ppermute | solution.py:484
  5.4 1.5 %collective-permute-start.8 = (bf16[528,128]{1,0:T(8,128)(2,1)}, bf16[528,128]{1,0:T(8,128)(2,1)S(1)}, u32[]{:S(2)}, u32[]{:S(2)}) collective-permute-start(bf16[528,128]{1,0:T(8,128)(2,1)} %get-tuple-element.39.after_ref.refs_0_), channel_id=1, source_target_pairs={{0,1},{1,0},{2,3},{3,2},{4,5},{5,4},{6,7},{7,6},{8,9},{9,8},{10,11... | collective-permute-start | bytes 405512 | tf_op jit(solution)/shard_map/ppermute | solution.py:490
  6.9 1.2 %copy-done = bf16[1,128,4096]{2,1,0:T(8,128)(2,1)S(1)} copy-done((bf16[1,128,4096]{2,1,0:T(8,128)(2,1)S(1)}, bf16[1,128,4096]{2,1,0:T(8,128)(2,1)}, u32[]{:S(2)}) %copy-start) | copy-done | bytes 1048600
  8.2 1.2 %copy-done.1 = bf16[1,128,4096]{2,1,0:T(8,128)(2,1)S(1)} copy-done((bf16[1,128,4096]{2,1,0:T(8,128)(2,1)S(1)}, bf16[1,128,4096]{2,1,0:T(8,128)(2,1)}, u32[]{:S(2)}) %copy-start.1) | copy-done | bytes 1048600
  9.4 0.2 shard_map.85
  9.5 1.7 %collective-permute-done.refs_1_ = bf16[528,128]{1,0:T(8,128)(2,1)S(1)} collective-permute-done((bf16[528,128]{1,0:T(8,128)(2,1)}, bf16[528,128]{1,0:T(8,128)(2,1)S(1)}, u32[]{:S(2)}, u32[]{:S(2)}) %collective-permute-start) | collective-permute-done | bytes 135200 | tf_op jit(solution)/shard_map/ppermute | solution.py:484
  11.2 0.0 collective-permute-start.6
  11.2 1.5 %collective-permute-start.1 = (bf16[528,128]{1,0:T(8,128)(2,1)S(1)}, bf16[528,128]{1,0:T(8,128)(2,1)S(1)}, u32[]{:S(2)}, u32[]{:S(2)}) collective-permute-start(bf16[528,128]{1,0:T(8,128)(2,1)S(1)} %collective-permute-done.refs_1_), channel_id=1, source_target_pairs={{0,1},{1,0},{2,3},{3,2},{4,5},{5,4},{6,7},{7,6},{8,9},{9,8},{10,11... | collective-permute-start | bytes 405512 | tf_op jit(solution)/shard_map/ppermute | solution.py:490
  12.7 3.8 %collective-permute-start.7 = (bf16[528,128]{1,0:T(8,128)(2,1)}, bf16[528,128]{1,0:T(8,128)(2,1)S(1)}, u32[]{:S(2)}, u32[]{:S(2)}) collective-permute-start(bf16[528,128]{1,0:T(8,128)(2,1)} %get-tuple-element.39.after_ref.refs_0_), channel_id=1, source_target_pairs={{0,6},{1,7},{2,0},{3,1},{4,2},{5,3},{6,4},{7,5},{8,14},{9,15},{10,... | collective-permute-start | bytes 405512 | tf_op jit(solution)/shard_map/ppermute | solution.py:484
  16.6 0.0 collective-permute-done.8.refs_4_
  16.6 0.0 collective-permute-start.10
  16.6 2.9 %collective-permute-done.6.refs_2_ = bf16[528,128]{1,0:T(8,128)(2,1)S(1)} collective-permute-done((bf16[528,128]{1,0:T(8,128)(2,1)S(1)}, bf16[528,128]{1,0:T(8,128)(2,1)S(1)}, u32[]{:S(2)}, u32[]{:S(2)}) %collective-permute-start.6) | collective-permute-done | bytes 135200 | tf_op jit(solution)/shard_map/ppermute | solution.py:484
  19.6 1.5 %collective-permute-start.9 = (bf16[528,128]{1,0:T(8,128)(2,1)S(1)}, bf16[528,128]{1,0:T(8,128)(2,1)S(1)}, u32[]{:S(2)}, u32[]{:S(2)}) collective-permute-start(bf16[528,128]{1,0:T(8,128)(2,1)S(1)} %collective-permute-done.6.refs_2_), channel_id=1, source_target_pairs={{0,1},{1,0},{2,3},{3,2},{4,5},{5,4},{6,7},{7,6},{8,9},{9,8},{10,11... | collective-permute-start | bytes 405512 | tf_op jit(solution)/shard_map/ppermute | solution.py:490
  21.1 0.0 collective-permute-done.1.refs_5_
  21.1 0.4 collective-permute-start.5
  21.5 0.0 collective-permute-start.4
  21.5 0.0 collective-permute-done.7.refs_3_
  21.5 1.6 %collective-permute-start.3 = (bf16[528,128]{1,0:T(8,128)(2,1)S(1)}, bf16[528,128]{1,0:T(8,128)(2,1)S(1)}, u32[]{:S(2)}, u32[]{:S(2)}) collective-permute-start(bf16[528,128]{1,0:T(8,128)(2,1)S(1)} %copy-done.3), channel_id=1, source_target_pairs={{0,2},{1,3},{2,4},{3,5},{4,6},{5,7},{6,0},{7,1},{8,10},{9,11},{10,... | collective-permute-start | bytes 405512 | tf_op jit(solution)/shard_map/ppermute | solution.py:484
  23.1 0.7 collective-permute-done.10.refs_7_
  23.8 1.2 %collective-permute-start.2 = (bf16[528,128]{1,0:T(8,128)(2,1)S(1)}, bf16[528,128]{1,0:T(8,128)(2,1)S(1)}, u32[]{:S(2)}, u32[]{:S(2)}) collective-permute-start(bf16[528,128]{1,0:T(8,128)(2,1)S(1)} %copy-done.3), channel_id=1, source_target_pairs={{0,1},{1,0},{2,3},{3,2},{4,5},{5,4},{6,7},{7,6},{8,9},{9,8},{10,11... | collective-permute-start | bytes 405512 | tf_op jit(solution)/shard_map/ppermute | solution.py:490
  25.0 10.3 %shard_map.86 = (bf16[1,128,4096]{2,1,0:T(8,128)(2,1)}, f32[1,128,4096]{2,1,0:T(8,128)}, f32[1,512,128]{2,1,0:T(8,128)S(1)}, f32[1,512,128]{2,1,0:T(8,128)S(1)},...) custom-call(s32[1]{0:T(128)} %bitcast.here_ref, ...), custom_call_target="tpu_custom_call" | custom-call | flops 6442450944 | bytes 8388608 | tf_op jit(solution)/shard_map/pallas_call | solution.py:413
  35.4 0.0 collective-permute-done.4.refs_2_
  35.4 0.0 collective-permute-done.3.refs_1_
  35.4 2.1 %collective-permute-start.11 = (bf16[528,128]{1,0:T(8,128)(2,1)S(1)}, bf16[528,128]{1,0:T(8,128)(2,1)S(1)}, u32[]{:S(2)}, u32[]{:S(2)}) collective-permute-start(bf16[528,128]{1,0:T(8,128)(2,1)S(1)} %collective-permute-done.3.refs_1_), channel_id=1, source_target_pairs={{0,1},{1,0},{2,3},{3,2},{4,5},{5,4},{6,7},{7,6},{8,9},{9,8},{10,11... | collective-permute-start | bytes 405512 | tf_op jit(solution)/shard_map/ppermute | solution.py:490
  37.5 0.1 collective-permute-start.12
  37.6 3.5 %collective-permute-start.13 = (bf16[528,128]{1,0:T(8,128)(2,1)S(1)}, bf16[528,128]{1,0:T(8,128)(2,1)S(1)}, u32[]{:S(2)}, u32[]{:S(2)}) collective-permute-start(bf16[528,128]{1,0:T(8,128)(2,1)S(1)} %collective-permute-done.2.refs_4_), channel_id=1, source_target_pairs={{0,6},{1,7},{2,0},{3,1},{4,2},{5,3},{6,4},{7,5},{8,14},{9,15},{10,... | collective-permute-start | bytes 405512 | tf_op jit(solution)/shard_map/ppermute | solution.py:484
  41.1 0.0 collective-permute-start.14
  41.1 1.5 %collective-permute-start.15 = (bf16[2,512,128]{2,1,0:T(8,128)(2,1)S(1)}, bf16[2,512,128]{2,1,0:T(8,128)(2,1)S(1)}, u32[]{:S(2)}, u32[]{:S(2)}) collective-permute-start(bf16[2,512,128]{2,1,0:T(8,128)(2,1)S(1)} %get-tuple-element.57), channel_id=1, source_target_pairs={{0,1},{1,0},{2,3},{3,2},{4,5},{5,4},{6,7},{7,6},{8,9},{9,8},{10,11... | collective-permute-start | bytes 786440 | tf_op jit(solution)/shard_map/ppermute | solution.py:490
  42.7 0.0 collective-permute-done.11.refs_5_
  42.7 2.3 %collective-permute-done.12.refs_6_ = bf16[528,128]{1,0:T(8,128)(2,1)S(1)} collective-permute-done((bf16[528,128]{1,0:T(8,128)(2,1)S(1)}, bf16[528,128]{1,0:T(8,128)(2,1)S(1)}, u32[]{:S(2)}, u32[]{:S(2)}) %collective-permute-start.12) | collective-permute-done | bytes 135200 | tf_op jit(solution)/shard_map/ppermute | solution.py:490
  44.9 0.5 collective-permute-done.13.refs_7_
  45.4 9.4 %shard_map.87 = (bf16[1,128,4096]{2,1,0:T(8,128)(2,1)}, f32[1,128,4096]{2,1,0:T(8,128)}, f32[1,512,128]{2,1,0:T(8,128)S(1)}, f32[1,512,128]{2,1,0:T(8,128)S(1)},...) custom-call(s32[1]{0:T(128)} %bitcast.here_ref, ...), custom_call_target="tpu_custom_call", output_to_operand_aliasing={{0}: (12, {}), {1}: (13, {})} | custom-call | flops 6442450944 | bytes 8388608 | tf_op jit(solution)/shard_map/pallas_call | solution.py:413
  54.8 0.6 collective-permute-start.19
  55.5 0.7 collective-permute-start.20
  56.2 0.1 shard_map.88
  56.3 1.3 %collective-permute-start.16 = (bf16[512,128]{1,0:T(8,128)(2,1)S(1)}, bf16[512,128]{1,0:T(8,128)(2,1)S(1)}, u32[]{:S(2)}, u32[]{:S(2)}) collective-permute-start(bf16[512,128]{1,0:T(8,128)(2,1)S(1)} %get-tuple-element.59), channel_id=1, source_target_pairs={{0,1},{1,0},{2,3},{3,2},{4,5},{5,4},{6,7},{7,6},{8,9},{9,8},{10,11... | collective-permute-start | bytes 393224 | tf_op jit(solution)/shard_map/ppermute | solution.py:490
  57.6 3.2 %collective-permute-start.17 = (bf16[512,128]{1,0:T(8,128)(2,1)S(1)}, bf16[512,128]{1,0:T(8,128)(2,1)S(1)}, u32[]{:S(2)}, u32[]{:S(2)}) collective-permute-start(bf16[512,128]{1,0:T(8,128)(2,1)S(1)} %get-tuple-element.60), channel_id=1, source_target_pairs={{2,0},{3,1},{4,2},{5,3},{6,4},{7,5},{0,6},{1,7},{10,8},{11,9},{12,... | collective-permute-start | bytes 393224 | tf_op jit(solution)/shard_map/ppermute | solution.py:487
  60.9 0.1 collective-permute-start.18
  61.0 4.7 %collective-permute-done.19.last_ref.refs_6_ = bf16[2,512,128]{2,1,0:T(8,128)(2,1)S(1)} collective-permute-done((bf16[2,512,128]{2,1,0:T(8,128)(2,1)S(1)}, bf16[2,512,128]{2,1,0:T(8,128)(2,1)S(1)}, u32[]{:S(2)}, u32[]{:S(2)}) %collective-permute-start.19) | collective-permute-done | bytes 262176 | tf_op jit(solution)/shard_map/ppermute | solution.py:487
  65.7 0.1 shard_map.89
  65.8 1.5 %collective-permute-start.21 = (bf16[512,128]{1,0:T(8,128)(2,1)S(1)}, bf16[512,128]{1,0:T(8,128)(2,1)S(1)}, u32[]{:S(2)}, u32[]{:S(2)}) collective-permute-start(bf16[512,128]{1,0:T(8,128)(2,1)S(1)} %get-tuple-element.67), channel_id=1, source_target_pairs={{0,1},{1,0},{2,3},{3,2},{4,5},{5,4},{6,7},{7,6},{8,9},{9,8},{10,11... | collective-permute-start | bytes 393224 | tf_op jit(solution)/shard_map/ppermute | solution.py:490
  67.2 1.0 %collective-permute-start.22 = (bf16[512,128]{1,0:T(8,128)(2,1)S(1)}, bf16[512,128]{1,0:T(8,128)(2,1)S(1)}, u32[]{:S(2)}, u32[]{:S(2)}) collective-permute-start(bf16[512,128]{1,0:T(8,128)(2,1)S(1)} %get-tuple-element.68), channel_id=1, source_target_pairs={{2,0},{3,1},{4,2},{5,3},{6,4},{7,5},{0,6},{1,7},{10,8},{11,9},{12,... | collective-permute-start | bytes 393224 | tf_op jit(solution)/shard_map/ppermute | solution.py:487
  68.2 4.0 %collective-permute-start.23 = (bf16[512,128]{1,0:T(8,128)(2,1)S(1)}, bf16[512,128]{1,0:T(8,128)(2,1)S(1)}, u32[]{:S(2)}, u32[]{:S(2)}) collective-permute-start(bf16[512,128]{1,0:T(8,128)(2,1)S(1)} %get-tuple-element.69), channel_id=1, source_target_pairs={{4,0},{5,1},{6,2},{7,3},{0,4},{1,5},{2,6},{3,7},{12,8},{13,9},{14,... | collective-permute-start | bytes 393224 | tf_op jit(solution)/shard_map/ppermute | solution.py:487
  72.2 0.4 collective-permute-done.18.refs_4_
  72.7 1.3 %collective-permute-done.22.refs_8_ = bf16[512,128]{1,0:T(8,128)(2,1)S(1)} collective-permute-done((bf16[512,128]{1,0:T(8,128)(2,1)S(1)}, bf16[512,128]{1,0:T(8,128)(2,1)S(1)}, u32[]{:S(2)}, u32[]{:S(2)}) %collective-permute-start.22) | collective-permute-done | bytes 131104 | tf_op jit(solution)/shard_map/ppermute | solution.py:487
  74.0 2.6 %collective-permute-done.23.refs_9_ = bf16[512,128]{1,0:T(8,128)(2,1)S(1)} collective-permute-done((bf16[512,128]{1,0:T(8,128)(2,1)S(1)}, bf16[512,128]{1,0:T(8,128)(2,1)S(1)}, u32[]{:S(2)}, u32[]{:S(2)}) %collective-permute-start.23) | collective-permute-done | bytes 131104 | tf_op jit(solution)/shard_map/ppermute | solution.py:487
  76.6 0.9 %shard_map.90 = (f32[1,128,512]{2,1,0:T(8,128)}, f32[1,128,512]{2,1,0:T(8,128)}) custom-call(f32[1,512,128]{2,1,0:T(8,128)S(1)} %get-tuple-element.46.refs_0_, bf16[2,512,128]{2,1,0:T(8,128)(2,1)S(1)} %collective-permute-done.14.last_ref.refs_1_, bf16[512,128]{1,0:T(8,128)(2,1)S(1)} %collective-permute-done.16.refs_2_, ...), custom_call_target="tpu_custom_call" | custom-call | tf_op jit(solution)/shard_map/pallas_call | solution.py:547
  (15 shorter events, 0.0 us)
Async XLA Ops:
  0.6 24.4 %copy-start.2 = (s32[1,128]{1,0:T(1,128)S(1)}, s32[1,128]{1,0:T(1,128)}, u32[]{:S(2)}) copy-start(s32[1,128]{1,0:T(1,128)} %refs_10_.3) | copy-start | bytes 1540
  2.3 8.9 %collective-permute-start = (bf16[528,128]{1,0:T(8,128)(2,1)}, bf16[528,128]{1,0:T(8,128)(2,1)S(1)}, u32[]{:S(2)}, u32[]{:S(2)}) collective-permute-start(bf16[528,128]{1,0:T(8,128)(2,1)} %get-tuple-element.39.after_ref.refs_0_), channel_id=1, source_target_pairs={{0,2},{1,3},{2,4},{3,5},{4,6},{5,7},{6,0},{7,1},{8,10},{9,11},{10,... | collective-permute-start | bytes 405512 | tf_op jit(solution)/shard_map/ppermute | solution.py:484
  5.4 11.2 %collective-permute-start.8 = (bf16[528,128]{1,0:T(8,128)(2,1)}, bf16[528,128]{1,0:T(8,128)(2,1)S(1)}, u32[]{:S(2)}, u32[]{:S(2)}) collective-permute-start(bf16[528,128]{1,0:T(8,128)(2,1)} %get-tuple-element.39.after_ref.refs_0_), channel_id=1, source_target_pairs={{0,1},{1,0},{2,3},{3,2},{4,5},{5,4},{6,7},{7,6},{8,9},{9,8},{10,11... | collective-permute-start | bytes 405512 | tf_op jit(solution)/shard_map/ppermute | solution.py:490
  6.9 1.2 %copy-start = (bf16[1,128,4096]{2,1,0:T(8,128)(2,1)S(1)}, bf16[1,128,4096]{2,1,0:T(8,128)(2,1)}, u32[]{:S(2)}) copy-start(bf16[1,128,4096]{2,1,0:T(8,128)(2,1)} %q_ref.1) | copy-start | bytes 3145732
  8.1 1.2 %copy-start.1 = (bf16[1,128,4096]{2,1,0:T(8,128)(2,1)S(1)}, bf16[1,128,4096]{2,1,0:T(8,128)(2,1)}, u32[]{:S(2)}) copy-start(bf16[1,128,4096]{2,1,0:T(8,128)(2,1)} %c_ref.1) | copy-start | bytes 3145732
  9.4 11.7 %copy-start.3 = (bf16[528,128]{1,0:T(8,128)(2,1)S(1)}, bf16[528,128]{1,0:T(8,128)(2,1)}, u32[]{:S(2)}) copy-start(bf16[528,128]{1,0:T(8,128)(2,1)} %get-tuple-element.43.refs_0_) | copy-start | bytes 405508
  11.2 8.3 %collective-permute-start.6 = (bf16[528,128]{1,0:T(8,128)(2,1)S(1)}, bf16[528,128]{1,0:T(8,128)(2,1)S(1)}, u32[]{:S(2)}, u32[]{:S(2)}) collective-permute-start(bf16[528,128]{1,0:T(8,128)(2,1)S(1)} %collective-permute-done.refs_1_), channel_id=1, source_target_pairs={{0,2},{1,3},{2,4},{3,5},{4,6},{5,7},{6,0},{7,1},{8,10},{9,11},{10,... | collective-permute-start | bytes 405512 | tf_op jit(solution)/shard_map/ppermute | solution.py:484
  11.2 9.8 %collective-permute-start.1 = (bf16[528,128]{1,0:T(8,128)(2,1)S(1)}, bf16[528,128]{1,0:T(8,128)(2,1)S(1)}, u32[]{:S(2)}, u32[]{:S(2)}) collective-permute-start(bf16[528,128]{1,0:T(8,128)(2,1)S(1)} %collective-permute-done.refs_1_), channel_id=1, source_target_pairs={{0,1},{1,0},{2,3},{3,2},{4,5},{5,4},{6,7},{7,6},{8,9},{9,8},{10,11... | collective-permute-start | bytes 405512 | tf_op jit(solution)/shard_map/ppermute | solution.py:490
  12.7 8.7 %collective-permute-start.7 = (bf16[528,128]{1,0:T(8,128)(2,1)}, bf16[528,128]{1,0:T(8,128)(2,1)S(1)}, u32[]{:S(2)}, u32[]{:S(2)}) collective-permute-start(bf16[528,128]{1,0:T(8,128)(2,1)} %get-tuple-element.39.after_ref.refs_0_), channel_id=1, source_target_pairs={{0,6},{1,7},{2,0},{3,1},{4,2},{5,3},{6,4},{7,5},{8,14},{9,15},{10,... | collective-permute-start | bytes 405512 | tf_op jit(solution)/shard_map/ppermute | solution.py:484
  16.6 7.3 %collective-permute-start.10 = (bf16[528,128]{1,0:T(8,128)(2,1)S(1)}, bf16[528,128]{1,0:T(8,128)(2,1)S(1)}, u32[]{:S(2)}, u32[]{:S(2)}) collective-permute-start(bf16[528,128]{1,0:T(8,128)(2,1)S(1)} %collective-permute-done.8.refs_4_), channel_id=1, source_target_pairs={{0,6},{1,7},{2,0},{3,1},{4,2},{5,3},{6,4},{7,5},{8,14},{9,15},{10,... | collective-permute-start | bytes 405512 | tf_op jit(solution)/shard_map/ppermute | solution.py:484
  19.6 5.5 %collective-permute-start.9 = (bf16[528,128]{1,0:T(8,128)(2,1)S(1)}, bf16[528,128]{1,0:T(8,128)(2,1)S(1)}, u32[]{:S(2)}, u32[]{:S(2)}) collective-permute-start(bf16[528,128]{1,0:T(8,128)(2,1)S(1)} %collective-permute-done.6.refs_2_), channel_id=1, source_target_pairs={{0,1},{1,0},{2,3},{3,2},{4,5},{5,4},{6,7},{7,6},{8,9},{9,8},{10,11... | collective-permute-start | bytes 405512 | tf_op jit(solution)/shard_map/ppermute | solution.py:490
  21.1 14.3 %collective-permute-start.5 = (bf16[528,128]{1,0:T(8,128)(2,1)S(1)}, bf16[528,128]{1,0:T(8,128)(2,1)S(1)}, u32[]{:S(2)}, u32[]{:S(2)}) collective-permute-start(bf16[528,128]{1,0:T(8,128)(2,1)S(1)} %copy-done.3), channel_id=1, source_target_pairs={{0,6},{1,7},{2,0},{3,1},{4,2},{5,3},{6,4},{7,5},{8,14},{9,15},{10,... | collective-permute-start | bytes 405512 | tf_op jit(solution)/shard_map/ppermute | solution.py:484
  21.5 13.9 %collective-permute-start.4 = (bf16[528,128]{1,0:T(8,128)(2,1)S(1)}, bf16[528,128]{1,0:T(8,128)(2,1)S(1)}, u32[]{:S(2)}, u32[]{:S(2)}) collective-permute-start(bf16[528,128]{1,0:T(8,128)(2,1)S(1)} %copy-done.3), channel_id=1, source_target_pairs={{0,4},{1,5},{2,6},{3,7},{4,0},{5,1},{6,2},{7,3},{8,12},{9,13},{10,... | collective-permute-start | bytes 405512 | tf_op jit(solution)/shard_map/ppermute | solution.py:484
  21.5 13.9 %collective-permute-start.3 = (bf16[528,128]{1,0:T(8,128)(2,1)S(1)}, bf16[528,128]{1,0:T(8,128)(2,1)S(1)}, u32[]{:S(2)}, u32[]{:S(2)}) collective-permute-start(bf16[528,128]{1,0:T(8,128)(2,1)S(1)} %copy-done.3), channel_id=1, source_target_pairs={{0,2},{1,3},{2,4},{3,5},{4,6},{5,7},{6,0},{7,1},{8,10},{9,11},{10,... | collective-permute-start | bytes 405512 | tf_op jit(solution)/shard_map/ppermute | solution.py:484
  23.8 11.6 %collective-permute-start.2 = (bf16[528,128]{1,0:T(8,128)(2,1)S(1)}, bf16[528,128]{1,0:T(8,128)(2,1)S(1)}, u32[]{:S(2)}, u32[]{:S(2)}) collective-permute-start(bf16[528,128]{1,0:T(8,128)(2,1)S(1)} %copy-done.3), channel_id=1, source_target_pairs={{0,1},{1,0},{2,3},{3,2},{4,5},{5,4},{6,7},{7,6},{8,9},{9,8},{10,11... | collective-permute-start | bytes 405512 | tf_op jit(solution)/shard_map/ppermute | solution.py:490
  35.4 7.2 %collective-permute-start.11 = (bf16[528,128]{1,0:T(8,128)(2,1)S(1)}, bf16[528,128]{1,0:T(8,128)(2,1)S(1)}, u32[]{:S(2)}, u32[]{:S(2)}) collective-permute-start(bf16[528,128]{1,0:T(8,128)(2,1)S(1)} %collective-permute-done.3.refs_1_), channel_id=1, source_target_pairs={{0,1},{1,0},{2,3},{3,2},{4,5},{5,4},{6,7},{7,6},{8,9},{9,8},{10,11... | collective-permute-start | bytes 405512 | tf_op jit(solution)/shard_map/ppermute | solution.py:490
  37.5 7.4 %collective-permute-start.12 = (bf16[528,128]{1,0:T(8,128)(2,1)S(1)}, bf16[528,128]{1,0:T(8,128)(2,1)S(1)}, u32[]{:S(2)}, u32[]{:S(2)}) collective-permute-start(bf16[528,128]{1,0:T(8,128)(2,1)S(1)} %collective-permute-done.4.refs_2_), channel_id=1, source_target_pairs={{0,1},{1,0},{2,3},{3,2},{4,5},{5,4},{6,7},{7,6},{8,9},{9,8},{10,11... | collective-permute-start | bytes 405512 | tf_op jit(solution)/shard_map/ppermute | solution.py:490
  37.6 7.8 %collective-permute-start.13 = (bf16[528,128]{1,0:T(8,128)(2,1)S(1)}, bf16[528,128]{1,0:T(8,128)(2,1)S(1)}, u32[]{:S(2)}, u32[]{:S(2)}) collective-permute-start(bf16[528,128]{1,0:T(8,128)(2,1)S(1)} %collective-permute-done.2.refs_4_), channel_id=1, source_target_pairs={{0,6},{1,7},{2,0},{3,1},{4,2},{5,3},{6,4},{7,5},{8,14},{9,15},{10,... | collective-permute-start | bytes 405512 | tf_op jit(solution)/shard_map/ppermute | solution.py:484
  41.1 15.1 %collective-permute-start.14 = (bf16[2,512,128]{2,1,0:T(8,128)(2,1)S(1)}, bf16[2,512,128]{2,1,0:T(8,128)(2,1)S(1)}, u32[]{:S(2)}, u32[]{:S(2)}) collective-permute-start(bf16[2,512,128]{2,1,0:T(8,128)(2,1)S(1)} %get-tuple-element.55), channel_id=1, source_target_pairs={{6,0},{7,1},{0,2},{1,3},{2,4},{3,5},{4,6},{5,7},{14,8},{15,9},{8,1... | collective-permute-start | bytes 786440 | tf_op jit(solution)/shard_map/ppermute | solution.py:487
  41.1 15.1 %collective-permute-start.15 = (bf16[2,512,128]{2,1,0:T(8,128)(2,1)S(1)}, bf16[2,512,128]{2,1,0:T(8,128)(2,1)S(1)}, u32[]{:S(2)}, u32[]{:S(2)}) collective-permute-start(bf16[2,512,128]{2,1,0:T(8,128)(2,1)S(1)} %get-tuple-element.57), channel_id=1, source_target_pairs={{0,1},{1,0},{2,3},{3,2},{4,5},{5,4},{6,7},{7,6},{8,9},{9,8},{10,11... | collective-permute-start | bytes 786440 | tf_op jit(solution)/shard_map/ppermute | solution.py:490
  54.8 10.8 %collective-permute-start.19 = (bf16[2,512,128]{2,1,0:T(8,128)(2,1)S(1)}, bf16[2,512,128]{2,1,0:T(8,128)(2,1)S(1)}, u32[]{:S(2)}, u32[]{:S(2)}) collective-permute-start(bf16[2,512,128]{2,1,0:T(8,128)(2,1)S(1)} %get-tuple-element.63), channel_id=1, source_target_pairs={{6,0},{7,1},{0,2},{1,3},{2,4},{3,5},{4,6},{5,7},{14,8},{15,9},{8,1... | collective-permute-start | bytes 786440 | tf_op jit(solution)/shard_map/ppermute | solution.py:487
  55.5 10.2 %collective-permute-start.20 = (bf16[2,512,128]{2,1,0:T(8,128)(2,1)S(1)}, bf16[2,512,128]{2,1,0:T(8,128)(2,1)S(1)}, u32[]{:S(2)}, u32[]{:S(2)}) collective-permute-start(bf16[2,512,128]{2,1,0:T(8,128)(2,1)S(1)} %get-tuple-element.65), channel_id=1, source_target_pairs={{0,1},{1,0},{2,3},{3,2},{4,5},{5,4},{6,7},{7,6},{8,9},{9,8},{10,11... | collective-permute-start | bytes 786440 | tf_op jit(solution)/shard_map/ppermute | solution.py:490
  56.3 12.0 %collective-permute-start.16 = (bf16[512,128]{1,0:T(8,128)(2,1)S(1)}, bf16[512,128]{1,0:T(8,128)(2,1)S(1)}, u32[]{:S(2)}, u32[]{:S(2)}) collective-permute-start(bf16[512,128]{1,0:T(8,128)(2,1)S(1)} %get-tuple-element.59), channel_id=1, source_target_pairs={{0,1},{1,0},{2,3},{3,2},{4,5},{5,4},{6,7},{7,6},{8,9},{9,8},{10,11... | collective-permute-start | bytes 393224 | tf_op jit(solution)/shard_map/ppermute | solution.py:490
  57.6 14.6 %collective-permute-start.17 = (bf16[512,128]{1,0:T(8,128)(2,1)S(1)}, bf16[512,128]{1,0:T(8,128)(2,1)S(1)}, u32[]{:S(2)}, u32[]{:S(2)}) collective-permute-start(bf16[512,128]{1,0:T(8,128)(2,1)S(1)} %get-tuple-element.60), channel_id=1, source_target_pairs={{2,0},{3,1},{4,2},{5,3},{6,4},{7,5},{0,6},{1,7},{10,8},{11,9},{12,... | collective-permute-start | bytes 393224 | tf_op jit(solution)/shard_map/ppermute | solution.py:487
  60.9 11.8 %collective-permute-start.18 = (bf16[512,128]{1,0:T(8,128)(2,1)S(1)}, bf16[512,128]{1,0:T(8,128)(2,1)S(1)}, u32[]{:S(2)}, u32[]{:S(2)}) collective-permute-start(bf16[512,128]{1,0:T(8,128)(2,1)S(1)} %get-tuple-element.61), channel_id=1, source_target_pairs={{4,0},{5,1},{6,2},{7,3},{0,4},{1,5},{2,6},{3,7},{12,8},{13,9},{14,... | collective-permute-start | bytes 393224 | tf_op jit(solution)/shard_map/ppermute | solution.py:487
  65.8 6.9 %collective-permute-start.21 = (bf16[512,128]{1,0:T(8,128)(2,1)S(1)}, bf16[512,128]{1,0:T(8,128)(2,1)S(1)}, u32[]{:S(2)}, u32[]{:S(2)}) collective-permute-start(bf16[512,128]{1,0:T(8,128)(2,1)S(1)} %get-tuple-element.67), channel_id=1, source_target_pairs={{0,1},{1,0},{2,3},{3,2},{4,5},{5,4},{6,7},{7,6},{8,9},{9,8},{10,11... | collective-permute-start | bytes 393224 | tf_op jit(solution)/shard_map/ppermute | solution.py:490
  67.2 6.7 %collective-permute-start.22 = (bf16[512,128]{1,0:T(8,128)(2,1)S(1)}, bf16[512,128]{1,0:T(8,128)(2,1)S(1)}, u32[]{:S(2)}, u32[]{:S(2)}) collective-permute-start(bf16[512,128]{1,0:T(8,128)(2,1)S(1)} %get-tuple-element.68), channel_id=1, source_target_pairs={{2,0},{3,1},{4,2},{5,3},{6,4},{7,5},{0,6},{1,7},{10,8},{11,9},{12,... | collective-permute-start | bytes 393224 | tf_op jit(solution)/shard_map/ppermute | solution.py:487
  68.2 8.3 %collective-permute-start.23 = (bf16[512,128]{1,0:T(8,128)(2,1)S(1)}, bf16[512,128]{1,0:T(8,128)(2,1)S(1)}, u32[]{:S(2)}, u32[]{:S(2)}) collective-permute-start(bf16[512,128]{1,0:T(8,128)(2,1)S(1)} %get-tuple-element.69), channel_id=1, source_target_pairs={{4,0},{5,1},{6,2},{7,3},{0,4},{1,5},{2,6},{3,7},{12,8},{13,9},{14,... | collective-permute-start | bytes 393224 | tf_op jit(solution)/shard_map/ppermute | solution.py:487
